TPU v7x, 32 devices: a whole 2x2x4 slice. The times are simulated.
32 devices in a mesh: parts: 2 (over x), space: 8 (over z, y), member: 2 (over core).
Axes of the slice: x: 2, y: 2, z: 4, core: 2. Of those that a mesh axis runs over, the one named last changes fastest.
Arguments:
- densities: float32 [4096, 4, 4096], P('space', ('parts', 'member')), parts along dimension 1, may hold values from 0.05 to 40, as said below
- scaling: float32 [4096, 4, 4096], P('space', ('parts', 'member')), parts along dimension 1, may hold values from 0.25 to 4
- weights: float32 [4], P('parts'), parts along dimension 0, may hold values from 0.5 to 2
- band: float32 [32, 3, 128, 128], replicated, may hold values from 0 to 0.009375, as said below
Outputs:
- barycenter: float32 [8192, 4096], P(('parts', 'space')), parts along dimension 0
- new_scaling: float32 [4096, 4, 4096], P('space', ('parts', 'member')), parts along dimension 1
There are 2 independent parts, one for each index of `parts`. A program takes and returns all parts, laid end to end along the dimension named above; an argument that names none is the same for every part. Nothing has to cross between parts.
Inputs may be any that keep to these rules, and one draw needn't show every extreme that they name: Positive densities. `band`: positive entries.
All inputs are finite; a program needn't handle non-finite values.
Results may differ from a plain program's by a relative error of at most 0.0001.
Values sent between devices are 32-bit elements; how exact they have to be, the bound alone decides.
No kernel may reach another device: no remote copies, remote signals or barrier semaphores. Data moves between devices by JAX's collectives and lax.ppermute only.
A program may use at most 192 MiB of HBM per device.

v0:
```python
import functools

import jax
import jax.numpy as jnp
from jax import lax
from jax.experimental import pallas as pl
from jax.experimental.pallas import tpu as pltpu
from jax.sharding import PartitionSpec as P

F32 = jnp.float32
BF16 = jnp.bfloat16
GROUPS = 4
ANY = pl.BlockSpec(memory_space=pl.ANY)
INVMEM = pl.BlockSpec(memory_space=pltpu.VMEM)
INSMEM = pl.BlockSpec(memory_space=pltpu.SMEM)


def split(x):
    high = x.astype(BF16)
    return high, (x - high.astype(F32)).astype(BF16)


def dot3(stack, b, dims):
    one = functools.partial(lax.dot_general, dimension_numbers=(dims, ((), ())), preferred_element_type=F32)
    rows = stack.shape[0] // 2
    both = one(stack, b[0])
    return both[:rows] + (one(stack[:rows], b[1]) + both[rows:])


def params(mebibytes):
    return pltpu.CompilerParams(vmem_limit_bytes=mebibytes * 1024 * 1024)


def hbm(*arrays):
    return [pltpu.with_memory_space_constraint(a, pltpu.HBM) for a in arrays]


def vmem(*arrays):
    return [pltpu.with_memory_space_constraint(a, pltpu.VMEM) for a in arrays]


def pick(choice, side):
    if isinstance(choice, tuple):
        return pl.multiple_of(jnp.where(side == 0, choice[0], choice[1]), 128)
    return choice


def cut_kernel(first, columns, side_ref, src, *refs):
    *outs, stage, sems = refs
    rows = stage.shape[0] // GROUPS
    start = pick(first, side_ref[0])
    outward = []
    inward = [
        pltpu.make_async_copy(src.at[pl.ds(start + g * rows, rows)], stage.at[pl.ds(g * rows, rows)], sems.at[0, g])
        for g in range(GROUPS)
    ]
    for copy in inward:
        copy.start()
    for g in range(GROUPS):
        inward[g].wait()
        part = pl.ds(g * rows, rows)
        for k, (out, column) in enumerate(zip(outs, columns)):
            at = pl.ds(column_of(column, side_ref), out.shape[2])
            outward.append(pltpu.make_async_copy(stage.at[part, :, at], out.at[part], sems.at[1 + k, g]))
            outward[-1].start()
    for copy in outward:
        copy.wait()


def cut(name, side, array, first, rows, parts):
    columns = array.shape[2]
    return pl.pallas_call(
        functools.partial(cut_kernel, first, [column for column, _ in parts]),
        in_specs=[INSMEM, ANY],
        out_specs=[ANY] * len(parts),
        out_shape=[pltpu.HBM((rows, 1, n), F32) for _, n in parts],
        scratch_shapes=[
            pltpu.VMEM((rows, 1, columns), F32),
            pltpu.SemaphoreType.DMA((1 + len(parts), GROUPS)),
        ],
        compiler_params=params(8),
        name=name,
    )(side, *hbm(array))


def column_of(column, side_ref):
    if isinstance(column, tuple):
        return pl.multiple_of(jnp.where(side_ref[1] == 1, column[0], column[1]), 128)
    return column


def cross_parts(columns):
    half, quarter = columns // 2, columns // 4
    return [(0, half), (half, quarter), ((half, 0), half), (3 * quarter, quarter)]


def cross_send(parts, behind=()):
    def send(part, numbers, ends):
        pairs = []
        for k in range(3):
            for direction, number in ((0, k), (1, 2 - k)):
                if number in numbers:
                    pairs.append(ends(k)[direction])
        return lax.ppermute(part, "space", pairs)

    to_partner = lambda k: ((2 * k + 1, 2 * k), (2 * k + 2, 2 * k + 3))
    onward = lambda k: ((2 * k, 2 * k + 2), (2 * k + 3, 2 * k + 1))
    direct = lambda k: ((2 * k + 1, 2 * k + 2), (2 * k + 2, 2 * k + 1))
    relayed = [send(part, numbers, to_partner) for part, numbers in zip(parts[:2], ((0, 1), (0, 2)))]
    straight = [send(part, numbers, direct) for part, numbers in zip(parts[2:], ((1, 2), (0, 2)))]
    a, b, c, d, *behind = lax.optimization_barrier((*relayed, *straight, *behind))
    relayed, straight = [a, b], [c, d]
    passed = [send(part, numbers, onward) for part, numbers in zip(relayed, ((0, 1), (0, 2)))]
    return passed + straight, behind


def cross_received(base, columns):
    a, b, c, d = range(base, base + 4)
    q = columns // 4
    return ((2, (c, 0), (a, 0)), (2, (c, q), (a, q)), (1, (c, 0), (b, 0)), (1, (c, q), (d, 0)))


def area(ref, row, rows, columns):
    return ref.at[pl.ds(row, rows), 0, columns] if len(ref.shape) == 3 else ref.at[pl.ds(row, rows), columns]


def weight_kernel(nblocks, band_ref, high_ref, low_ref):
    pair = pl.program_id(0)
    width = band_ref.shape[2]
    zero = jnp.zeros((width, width), F32)
    for o in range(2):
        for i in range(4):
            j = i - o
            value = band_ref[o, j] if 0 <= j <= 2 else zero
            if (o, j) == (0, 0):
                value = jnp.where(pair > 0, value, 0.0)
            if (o, j) == (1, 2):
                value = jnp.where(pair < nblocks // 2 - 1, value, 0.0)
            high, low = split(value)
            rows, columns = slice(o * width, (o + 1) * width), slice(i * width, (i + 1) * width)
            high_ref[0, rows, columns] = high
            low_ref[0, rows, columns] = low


def row_weights(band):
    nblocks, _, width, _ = band.shape
    shape = pltpu.HBM((nblocks // 2, 2 * width, 4 * width), BF16)
    out_spec = pl.BlockSpec((1, 2 * width, 4 * width), lambda t: (t, 0, 0))
    return pl.pallas_call(
        functools.partial(weight_kernel, nblocks),
        grid=(nblocks // 2,),
        in_specs=[pl.BlockSpec((2, 3, width, width), lambda t: (t, 0, 0, 0))],
        out_specs=(out_spec, out_spec),
        out_shape=(shape, shape),
        name="row_weights",
    )(*hbm(band))


def blur_kernel(plan, *refs):
    pieces, narrays, extra, final, split_out, units, groups = plan
    side_ref, refs = refs[0], refs[1:]
    arrays = refs[:narrays]
    band_ref, high_ref, low_ref, extra_ref = refs[narrays : narrays + 4]
    rest = refs[narrays + 4 :]
    if final:
        weights_ref, rest = rest[0], rest[1:]
        all_weights = weights_ref[0]
        for k in range(1, weights_ref.shape[0]):
            all_weights += weights_ref[k]
        row_shape = (1, 2 * band_ref.shape[2])
        share = jnp.full(row_shape, weights_ref[side_ref[3]]) / jnp.full(row_shape, all_weights)
    nouts = len(groups) + 1 if final else 1 + len(split_out)
    outs = rest[:nouts]
    field, a_both, y_both, whigh, wlow, other = rest[nouts : nouts + 6]
    *results, in_sems, late_sems, out_sems = rest[nouts + 6 :]

    side = side_ref[0]
    nout, _, width, _ = band_ref.shape
    columns = field.shape[1]
    step = columns // GROUPS
    pairs = step // (2 * width)
    inside, late = [], {}

    def copy_in(u, k, place):
        _, row, rows, to = pieces[k]
        which, column = place
        start, stop = units[u]
        return pltpu.make_async_copy(
            area(arrays[which], pick(row, side), rows, pl.ds(column, stop - start)),
            field.at[pl.ds(pick(to, side), rows), pl.ds(start, stop - start)],
            in_sems.at[u, k],
        )

    def start_in(u, k):
        source = pieces[k][0]
        if isinstance(source, int):
            copy = copy_in(u, k, (source, units[u][0]))
        elif len(source[u]) == 2:
            copy = copy_in(u, k, source[u])
        else:
            number, this, other_one = source[u]
            pl.when(side_ref[2] == number)(copy_in(u, k, this).start)
            pl.when(side_ref[2] != number)(copy_in(u, k, other_one).start)
            return copy_in(u, k, other_one)
        copy.start()
        return copy

    for g in groups:
        at = pl.ds(g * step, step)
        some = pl.ds(g * pairs, pairs)
        late[g] = [
            pltpu.make_async_copy(high_ref.at[some], whigh.at[some], late_sems.at[g, 0]),
            pltpu.make_async_copy(low_ref.at[some], wlow.at[some], late_sems.at[g, 1]),
            pltpu.make_async_copy(
                area(extra_ref, pick(extra, side), other.shape[0], at), other.at[:, at], late_sems.at[g, 2]
            ),
        ]
    waiting = list(groups)
    for u in range(len(units)):
        inside.append([start_in(u, k) for k in range(len(pieces))])
        if u > 0 and waiting:
            for copy in late[waiting.pop(0)]:
                copy.start()
    for g in waiting:
        for copy in late[g]:
            copy.start()

    blocks = [(i, min(2, nout - i)) for i in range(0, nout, 2)]
    total = nout * width
    a_both[...] = jnp.zeros_like(a_both)
    for first, n in blocks:
        for i in range(n):
            for j in range(3):
                for part, value in enumerate(split(band_ref[first + i, j])):
                    row = (2 * first + part * n + i) * width
                    a_both[row : row + width, (i + j) * width : (i + j + 1) * width] = value
    y_both[:, :width] = jnp.zeros((2 * total, width), BF16)
    y_both[:, columns + width :] = jnp.zeros((2 * total, width), BF16)

    def columns_pass(u):
        for copy in inside[u]:
            copy.wait()
        for i in range(units[u][0] // (2 * width), units[u][1] // (2 * width)):
            at = slice(i * 2 * width, (i + 1) * 2 * width)
            to = slice((2 * i + 1) * width, (2 * i + 3) * width)
            for first, n in blocks:
                a = a_both[2 * first * width : 2 * (first + n) * width, : (n + 2) * width]
                y = dot3(a, split(field[first * width : (first + n + 2) * width, at]), ((1,), (0,)))
                for part, value in enumerate(split(y)):
                    row = part * total + first * width
                    y_both[row : row + n * width, to] = value

    def rows_pass(g):
        for copy in late[g]:
            copy.wait()
        for t in range(g * pairs, (g + 1) * pairs):
            source = slice(t * 2 * width, (t + 2) * 2 * width)
            at = slice(t * 2 * width, (t + 1) * 2 * width)
            value = dot3(y_both[:, source], (whigh[t], wlow[t]), ((1,), (1,)))
            if final:
                results[0][:, at] = value
                results[1][:, at] = share * jnp.log(other[:, at] * value)
            else:
                results[0][:, at] = other[:, at] / value
        at = pl.ds(g * step, step)
        targets = [outs[-1].at[:, pl.ds((g - groups[0]) * step, step)]] + ([outs[groups.index(g)]] if final else [])
        copies = [
            pltpu.make_async_copy(src.at[:, at], dst, out_sems.at[g, k])
            for k, (src, dst) in enumerate(zip(results, targets))
        ]
        for k, (start, stop) in enumerate(split_out):
            if g * step < stop <= (g + 1) * step:
                part = results[0].at[:, pl.ds(start, stop - start)]
                copies.append(pltpu.make_async_copy(part, outs[k], out_sems.at[GROUPS, k]))
        for copy in copies:
            copy.start()
        return copies

    going = []
    waiting = list(groups)
    for u, (_, stop) in enumerate(units):
        columns_pass(u)
        while waiting and u > 0 and (stop == columns or (waiting[0] + 1) * step + width <= stop):
            going += rows_pass(waiting.pop(0))
    for copy in going:
        copy.wait()


def blur(
    name, side, arrays, pieces, bands, weights, other, extra,
    map_weights=None, pin=True, split_out=(), units=None, groups=tuple(range(GROUPS)),
):
    nout, _, width, _ = bands.shape
    npairs = weights[0].shape[0]
    columns = npairs * 2 * width
    rows, depth = nout * width, (nout + 2) * width
    final = map_weights is not None
    nouts = 2 if final else 1
    kind = pltpu.HBM if pin else jax.ShapeDtypeStruct
    step = columns // GROUPS
    units = tuple((g * step, (g + 1) * step) for g in range(GROUPS)) if units is None else units
    shapes = [kind((rows, step), F32)] * (len(groups) if final else 0)
    shapes += [pltpu.HBM((rows, stop - start), F32) for start, stop in split_out]
    shapes.append(pltpu.HBM((rows, len(groups) * step), F32))
    plan = (tuple(pieces), len(arrays), extra, final, split_out, units, groups)
    work = 3 * 2 * rows * columns * (depth + 4 * width)
    moved = 4 * (depth + 3 * rows) * columns + npairs * 2 * 2 * 8 * width * width
    size = 4 * columns * (depth + (1 + nouts) * rows) + 4 * rows * columns + npairs * 2 * 2 * 8 * width * width
    result = pl.pallas_call(
        functools.partial(blur_kernel, plan),
        in_specs=[INSMEM] + [ANY] * len(arrays) + [INVMEM, ANY, ANY, ANY] + [INSMEM] * final,
        out_specs=[ANY] * len(shapes),
        out_shape=shapes,
        scratch_shapes=[
            pltpu.VMEM((depth, columns), F32),
            pltpu.VMEM((2 * rows, min(depth, 4 * width)), BF16),
            pltpu.VMEM((2 * rows, columns + 2 * width), BF16),
            pltpu.VMEM((npairs, 2 * width, 4 * width), BF16),
            pltpu.VMEM((npairs, 2 * width, 4 * width), BF16),
            pltpu.VMEM((rows, columns), F32),
        ]
        + [pltpu.VMEM((rows, columns), F32)] * nouts
        + [
            pltpu.SemaphoreType.DMA((len(units), len(pieces))),
            pltpu.SemaphoreType.DMA((GROUPS, 3)),
            pltpu.SemaphoreType.DMA((GROUPS + 1, 2)),
        ],
        compiler_params=params(size // 2**20 + 6),
        cost_estimate=pl.CostEstimate(flops=work // 64, bytes_accessed=moved // 64, transcendentals=0),
        name=name,
    )(side, *arrays, bands, *hbm(*weights, other), *(hbm(map_weights) if final else []))
    return (result[:-1], result[-1]) if final else result if split_out else result[0]


def raw_kernel(fresh, first, side_ref, *refs):
    own, peer, m_ref = refs[:GROUPS], refs[GROUPS : 2 * GROUPS], refs[2 * GROUPS]
    raw_ref, quotient_ref, mass_ref, quotient, sems = refs[-5:]
    tile = raw_ref.shape[0]
    at = pl.program_id(0)
    slot = lax.rem(at, 2)

    def copy(step, slot):
        row = pl.multiple_of(pick(first, side_ref[0]) + step * tile, tile)
        return pltpu.make_async_copy(quotient.at[slot], area(quotient_ref, row, tile, slice(None)), sems.at[slot])

    @pl.when(at >= 2)
    def _():
        copy(at - 2, slot).wait()

    mass = 0.0
    for g in range(GROUPS):
        raw = jnp.exp(own[g][...] + peer[g][...])
        step = raw.shape[1]
        raw_ref[:, g * step : (g + 1) * step] = raw
        mass += jnp.sum(raw)
        quotient[slot, :, g * step : (g + 1) * step] = raw / m_ref[:, g * step : (g + 1) * step]
    before = 0.0 if fresh else refs[2 * GROUPS + 3][...]
    mass_ref[...] = mass + jnp.where(at == 0, before, mass_ref[...])
    copy(at, slot).start()

    @pl.when(at == pl.num_programs(0) - 1)
    def _():
        copy(at - 1, 1 - slot).wait()
        copy(at, slot).wait()


def raw_rows(name, side, row, t, peers, m, rows_here, so_far):
    fresh = so_far is None
    rows, columns = m.shape
    tile = 32
    starts = [r // tile for r in row]
    part = pl.BlockSpec((tile, columns), lambda i, at: (i, 0))
    group = pl.BlockSpec((tile, columns // GROUPS), lambda i, at: (i, 0))
    return pl.pallas_call(
        functools.partial(raw_kernel, fresh, row),
        grid_spec=pltpu.PrefetchScalarGridSpec(
            num_scalar_prefetch=1,
            grid=(rows // tile,),
            in_specs=[group] * (2 * GROUPS) + [part] + ([] if fresh else [ANY, ANY, INVMEM]),
            out_specs=(
                pl.BlockSpec((tile, columns), lambda i, at: (jnp.where(at[0] == 0, *starts) + i, 0)),
                ANY,
                INVMEM,
            ),
            scratch_shapes=[pltpu.VMEM((2, tile, columns), F32), pltpu.SemaphoreType.DMA((2,))],
        ),
        out_shape=(
            pltpu.VMEM((rows_here, columns), F32),
            pltpu.VMEM((rows_here, 1, columns), F32),
            jax.ShapeDtypeStruct((1, 128), F32),
        ),
        input_output_aliases={} if fresh else {2 * GROUPS + 2: 0, 2 * GROUPS + 3: 1},
        compiler_params=params(16),
        cost_estimate=pl.CostEstimate(flops=m.size // 16, bytes_accessed=m.size // 4, transcendentals=0),
        name=name,
    )(side, *t, *peers, m, *([] if fresh else vmem(*so_far[:2]) + [so_far[2]]))


def raw_only_kernel(side_ref, *refs):
    *logs, _, before_ref, raw_ref, mass_ref = refs
    parts = len(logs) // 2
    mass = 0.0
    for g in range(parts):
        raw = jnp.exp(logs[g][...] + logs[parts + g][...])
        step = raw.shape[1]
        raw_ref[:, g * step : (g + 1) * step] = raw
        mass += jnp.sum(raw)
    mass_ref[...] = mass + jnp.where(pl.program_id(0) == 0, before_ref[...], mass_ref[...])


def piece_spec(tile, columns, row, column):
    starts = [r // tile for r in row]
    return pl.BlockSpec((tile, columns), lambda i, at: (jnp.where(at[0] == 0, *starts) + i, column // columns))


def raw_only(name, side, row, column, t, peers, raw_all, mass):
    rows, step = t[0].shape
    columns = len(t) * step
    tile = 64
    group = pl.BlockSpec((tile, step), lambda i, at: (i, 0))
    return pl.pallas_call(
        raw_only_kernel,
        grid_spec=pltpu.PrefetchScalarGridSpec(
            num_scalar_prefetch=1,
            grid=(rows // tile,),
            in_specs=[group] * (2 * len(t)) + [ANY, INVMEM],
            out_specs=(piece_spec(tile, columns, row, column), INVMEM),
        ),
        out_shape=(pltpu.VMEM(raw_all.shape, F32), jax.ShapeDtypeStruct(mass.shape, F32)),
        input_output_aliases={2 * len(t) + 1: 0},
        compiler_params=params(16),
        cost_estimate=pl.CostEstimate(flops=rows * columns // 16, bytes_accessed=rows * columns // 4, transcendentals=0),
        name=name,
    )(side, *t, *peers, *vmem(raw_all), mass)


def quotient_kernel(first, column, side_ref, raw_ref, m_ref, _, quotient_ref, quotient, sems):
    tile, columns = raw_ref.shape
    at = pl.program_id(0)
    row = pick(first, side_ref[0])
    quotient[at] = raw_ref[...] / m_ref[...]
    copies = [
        pltpu.make_async_copy(
            quotient.at[k], area(quotient_ref, row + k * tile, tile, pl.ds(column, columns)), sems.at[k]
        )
        for k in range(quotient.shape[0])
    ]
    for k, copy in enumerate(copies):
        pl.when(at == k)(copy.start)

    @pl.when(at == len(copies) - 1)
    def _():
        for copy in copies:
            copy.wait()


def quotient_part(name, side, row, column, raw_all, m, quotient_all):
    rows, columns = m.shape
    tile = 64
    return pl.pallas_call(
        functools.partial(quotient_kernel, row, column),
        grid_spec=pltpu.PrefetchScalarGridSpec(
            num_scalar_prefetch=1,
            grid=(rows // tile,),
            in_specs=[
                piece_spec(tile, columns, row, column),
                pl.BlockSpec((tile, columns), lambda i, at: (i, 0)),
                ANY,
            ],
            out_specs=ANY,
            scratch_shapes=[
                pltpu.VMEM((rows // tile, tile, columns), F32),
                pltpu.SemaphoreType.DMA((rows // tile,)),
            ],
        ),
        out_shape=pltpu.VMEM(quotient_all.shape, F32),
        input_output_aliases={3: 0},
        compiler_params=params(16),
        cost_estimate=pl.CostEstimate(flops=rows * columns // 16, bytes_accessed=rows * columns // 4, transcendentals=0),
        name=name,
    )(side, *vmem(raw_all), *hbm(m), *vmem(quotient_all))


def sum_kernel(a_ref, b_ref, out_ref):
    out_ref[...] = a_ref[...] + b_ref[...]


def mass_parts(mass, quotient):
    count = lax.axis_size("space")
    if count & (count - 1):
        return [lax.psum(mass, "space")], quotient
    parts = [mass]
    for bit in range(count.bit_length() - 1):
        if len(parts) == 2:
            if bit == 1:
                parts[1], quotient = lax.optimization_barrier((parts[1], quotient))
            parts = [
                pl.pallas_call(
                    sum_kernel,
                    in_specs=[INVMEM, INVMEM],
                    out_specs=INVMEM,
                    out_shape=jax.ShapeDtypeStruct(mass.shape, F32),
                    compiler_params=params(1),
                    name="mass",
                )(*parts)
            ]
        parts.append(lax.ppermute(parts[0], "space", [(i, i ^ (1 << bit)) for i in range(count)]))
    return parts, quotient


def output_kernel(total, raw_ref, quotient_ref, *refs):
    *masses, barycenter_ref, scaling_ref = refs
    mass = masses[0][...]
    for part in masses[1:]:
        mass += part[...]
    scale = total / mass
    width = scale.shape[1]
    for b in range(raw_ref.shape[1] // width):
        at = slice(b * width, (b + 1) * width)
        barycenter_ref[:, at] = raw_ref[:, at] * scale
    scaling_ref[...] = quotient_ref[...] * scale.reshape(1, 1, width)


def outputs(raw, quotient, masses):
    rows, columns = raw.shape
    tile = 64
    flat = pl.BlockSpec((tile, columns), lambda i: (i, 0))
    deep = pl.BlockSpec((tile,) + quotient.shape[1:], lambda i: (i, 0, 0))
    return pl.pallas_call(
        functools.partial(output_kernel, float(columns * columns)),
        grid=(rows // tile,),
        in_specs=[flat, deep] + [INVMEM] * len(masses),
        out_specs=(flat, deep),
        out_shape=(jax.ShapeDtypeStruct(raw.shape, F32), jax.ShapeDtypeStruct(quotient.shape, F32)),
        compiler_params=params(16),
        name="outputs",
    )(*vmem(raw, quotient), *masses)


def local(densities, scaling, weights, band):
    rows_here, maps_here, cols_all = densities.shape
    _, _, width, _ = band.shape
    nlocal = rows_here // width
    inner = max(nlocal - 2, 0)
    place = lax.axis_index("space")
    count = lax.axis_size("space")
    assert maps_here == 1 and lax.axis_size("member") == 2 and count % 2 == 0

    odd = place & 1
    middle = place >> 1
    numbers = [jnp.where(odd == 1, middle, 3 - middle), jnp.where(odd == 1, 2 - middle, middle - 1)]
    side = jnp.stack([odd, *numbers, lax.axis_index("member")])
    spread = count == 8 and nlocal > 1
    last = rows_here - width
    cross_row, near_row = (0, last), (last, 0)
    both = lambda pairs: pairs + [(b, a) for a, b in pairs]
    cross = functools.partial(
        lax.ppermute, axis_name="space", perm=both([(i, i + 1) for i in range(1, count - 1, 2)])
    )
    near = functools.partial(lax.ppermute, axis_name="space", perm=both([(i, i + 1) for i in range(0, count, 2)]))
    swap = functools.partial(lax.ppermute, axis_name="member", perm=[(0, 1), (1, 0)])

    def choose(choice):
        return jnp.where(odd == 0, *[c // width for c in choice]).astype(jnp.int32)

    whole_rows = [(0, cols_all)]
    near_edge = cut("cut_near", side, scaling, near_row, width, whole_rows)
    if spread:
        edge = cut("cut_cross", side, scaling, cross_row, width, cross_parts(cols_all))
        cross1, near_edge = cross_send(edge, near_edge)
    else:
        cross1 = [cross(cut("cut_cross", side, scaling, cross_row, width, whole_rows)[0])]
    near1 = near(near_edge[0])

    wts = row_weights(band)
    mine = place * nlocal
    band_at = lambda block, blocks: lax.dynamic_slice_in_dim(band, mine + block, blocks, 0)

    if inner > 0:
        inner_bands = band_at(1, inner)
        ratio_inner = blur(
            "ratio_inner", side, hbm(scaling), [(0, 0, rows_here, 0)], inner_bands, wts, densities, width
        )
        *cross1, ratio_inner = lax.optimization_barrier((*cross1, ratio_inner))
    if nlocal == 1:
        pieces = [(0, 0, width, width), (1, 0, width, (0, 2 * width)), (2, 0, width, (2 * width, 0))]
        bands = band_at(0, 1)
        ratio = blur("ratio_only", side, [scaling, *cross1, near1], pieces, bands, wts, densities, 0)
        cross2, near2 = cross(ratio), near(ratio)
    else:
        two = rows_here - 2 * width
        halo = cross_received(1, cols_all) if spread else 1
        pieces = [(0, (0, two), 2 * width, (width, 0)), (halo, 0, width, (0, 2 * width))]
        cross_bands = band_at(choose(cross_row), 1)
        ratio_cross = blur(
            "ratio_cross", side, hbm(scaling, *cross1), pieces, cross_bands, wts, densities, cross_row
        )
        ratio_cross, near1 = lax.optimization_barrier((ratio_cross, near1))
        cross2 = cross(ratio_cross)
        half, more = cols_all // 2, 2 * width
        pieces = [(0, (two, 0), 2 * width, (0, width)), (1, 0, width, (2 * width, 0))]
        near_bands = band_at(choose(near_row), 1)
        *parts, ratio_near = blur(
            "ratio_near", side, hbm(scaling) + [near1], pieces, near_bands, wts, densities, near_row,
            split_out=((0, half + more), (half + more, cols_all)),
        )
        near2 = [near(part) for part in parts]

    def finish(name, arrays, pieces, bands, row, weights, state):
        t, m = blur("logs_" + name, side, arrays, pieces, bands, wts, scaling, row, weights)
        return raw_rows(
            "raw_" + name, side, row, hbm(*t), [swap(part) for part in t], *hbm(m), rows_here, state
        )

    if nlocal == 1:
        pieces = [(0, 0, width, width), (1, 0, width, (0, 2 * width)), (2, 0, width, (2 * width, 0))]
        state = finish("only", [ratio, cross2, near2], pieces, bands, (0, 0), weights, None)
    else:
        state = None
        beside, beside_row = ratio_near, (0, 0)
        if inner > 0:
            arrays = hbm(ratio_inner, ratio_cross, ratio_near)
            pieces = [(0, 0, inner * width, width), (1, 0, width, cross_row), (2, 0, width, near_row)]
            state = finish("inner", arrays, pieces, inner_bands, (width, width), weights, None)
            weights, state = lax.optimization_barrier((weights, state))
            beside, beside_row = ratio_inner, (0, (inner - 1) * width)
        arrays = hbm(ratio_cross, beside) + [cross2]
        pieces = [(0, 0, width, width), (1, beside_row, width, (2 * width, 0)), (2, 0, width, (0, 2 * width))]
        state = finish("cross", arrays, pieces, cross_bands, cross_row, weights, state)
        weights, state = lax.optimization_barrier((weights, state))
        if inner == 0:
            beside = ratio_cross
        raw, quotient, mass = state
        step = cols_all // GROUPS
        first_units = tuple((g * step, (g + 1) * step) for g in range(GROUPS // 2)) + ((half, half + more),)
        later_units = ((half - more, half + more), (half + more, half + step)) + tuple(
            (g * step, (g + 1) * step) for g in range(GROUPS // 2 + 1, GROUPS)
        )
        plans = [
            ("near_first", first_units, 0, [(2, start) for start, _ in first_units]),
            ("near_later", later_units, half, [(2, half - more)] + [(3, a - half - more) for a, _ in later_units[1:]]),
        ]
        for part, (name, units, column, halo) in enumerate(plans):
            arrays = hbm(ratio_near, beside) + near2[: part + 1]
            pieces = [
                (0, 0, width, width),
                (1, beside_row[::-1], width, (0, 2 * width)),
                (tuple(halo), 0, width, (2 * width, 0)),
            ]
            groups = tuple(g for g in range(GROUPS) if column <= g * step < column + half)
            t, m = blur(
                "logs_" + name, side, arrays, pieces, near_bands, wts, scaling, near_row, weights,
                pin=False, units=units, groups=groups,
            )
            raw, mass = raw_only("raw_" + name, side, near_row, column, t, [swap(part) for part in t], raw, mass)
            quotient = quotient_part("quotient_" + name, side, near_row, column, raw, m, quotient)
            if part == 0:
                weights, raw, mass, quotient = lax.optimization_barrier((weights, raw, mass, quotient))
        state = raw, quotient, mass

    raw, quotient, mass = state
    masses, quotient = mass_parts(mass, quotient)
    barycenter, new_scaling = outputs(raw, quotient.reshape(rows_here, cols_all // width, width), masses)
    return barycenter, new_scaling.reshape(rows_here, 1, cols_all)


def solution(mesh):
    return jax.shard_map(
        local,
        mesh=mesh,
        in_specs=(
            P("space", ("parts", "member"), None),
            P("space", ("parts", "member"), None),
            P("parts"),
            P(),
        ),
        out_specs=(P(("parts", "space"), None), P("space", ("parts", "member"), None)),
        check_vma=False,
    )
```

profile of v0, /device:TPU:0, one launch (start us, length us, event | category | flops | bytes accessed | tf_op | source)
XLA Modules:
  0.0 220.2 jit_solution(11886241266100461943)
XLA Ops:
  0.7 3.4 %cut_cross.1 = (f32[128,1,2048]{2,1,0:T(1,128)}, f32[128,1,1024]{2,1,0:T(1,128)}, f32[128,1,2048]{2,1,0:T(1,128)}, f32[128,1,1024]{2,1,0:T(1,128)}) custom-call(s32[4]{0:T(128)S(1)} %pad_add_fusion.side_ref.refs_0_, f32[512,1,4096]{2,1,0:T(1,128)} %refs_8_.5), custom_call_target="tpu_custom_call" | custom-call | tf_op jit(solution)/shard_map/cut_cross/pallas_call | solution.py:72
  8.2 3.0 %cut_near.1 = f32[128,1,4096]{2,1,0:T(1,128)} custom-call(s32[4]{0:T(128)S(1)} %pad_add_fusion.side_ref.refs_0_, f32[512,1,4096]{2,1,0:T(1,128)} %refs_8_.5), custom_call_target="tpu_custom_call" | custom-call | tf_op jit(solution)/shard_map/cut_near/pallas_call | solution.py:72
  11.2 31.9 %collective-permute-done.1 = f32[128,1,1024]{2,1,0:T(1,128)} collective-permute-done((f32[128,1,1024]{2,1,0:T(1,128)}, f32[128,1,1024]{2,1,0:T(1,128)}, u32[]{:S(2)}, u32[]{:S(2)}) %collective-permute-start.1) | collective-permute-done | bytes 524320 | tf_op jit(solution)/shard_map/ppermute | solution.py:104
  43.9 5.4 %collective-permute-start.6 = (f32[128,1,4096]{2,1,0:T(1,128)}, f32[128,1,4096]{2,1,0:T(1,128)S(1)}, u32[]{:S(2)}, u32[]{:S(2)}) collective-permute-start(f32[128,1,4096]{2,1,0:T(1,128)} %cut_near.1), channel_id=1, source_target_pairs={{0,2},{4,6},{8,10},{12,14},{2,0},{6,4},{10,8},{14,12},{1,3},{5,7},... | collective-permute-start | bytes 6291464 | tf_op jit(solution)/shard_map/ppermute | solution.py:573
  49.3 5.5 %collective-permute-start.4 = (f32[128,1,2048]{2,1,0:T(1,128)}, f32[128,1,2048]{2,1,0:T(1,128)}, u32[]{:S(2)}, u32[]{:S(2)}) collective-permute-start(f32[128,1,2048]{2,1,0:T(1,128)} %collective-permute-done), channel_id=1, source_target_pairs={{0,4},{4,8},{10,6},{14,10},{1,5},{5,9},{11,7},{15,11},{16,20},{20,... | collective-permute-start | bytes 3145736 | tf_op jit(solution)/shard_map/ppermute | solution.py:104
  54.8 2.7 %collective-permute-start.5 = (f32[128,1,1024]{2,1,0:T(1,128)}, f32[128,1,1024]{2,1,0:T(1,128)}, u32[]{:S(2)}, u32[]{:S(2)}) collective-permute-start(f32[128,1,1024]{2,1,0:T(1,128)} %collective-permute-done.1), channel_id=1, source_target_pairs={{0,4},{6,2},{8,12},{14,10},{1,5},{7,3},{9,13},{15,11},{16,20},{22,... | collective-permute-start | bytes 1572872 | tf_op jit(solution)/shard_map/ppermute | solution.py:104
  57.5 11.6 %row_weights.1 = (bf16[16,256,512]{2,1,0:T(8,128)(2,1)}, bf16[16,256,512]{2,1,0:T(8,128)(2,1)}) custom-call(f32[32,3,128,128]{3,2,1,0:T(8,128)} %band_ref.1), custom_call_target="tpu_custom_call" | custom-call | tf_op jit(solution)/shard_map/row_weights/pallas_call | solution.py:149
  70.2 11.4 %ratio_inner.1.refs_1_.refs_2_ = f32[256,4096]{1,0:T(8,128)} custom-call(s32[4]{0:T(128)S(1)} %pad_add_fusion.side_ref.refs_0_, f32[512,1,4096]{2,1,0:T(1,128)} %refs_8_.5, f32[2,3,128,128]{3,2,1,0:T(8,128)S(1)} %constant_dynamic-slice_fusion.2.refs_2_.refs_4_, bf16[16,256,512]{2,1,0:T(8,128)(2,1)} %get-tuple-element.73.refs_3_.refs_7_.refs_4_.refs_5_.refs_6_, ...), custom_call_target="tpu_custom_call" | custom-call | flops 100663296 | bytes 458752 | tf_op jit(solution)/shard_map/ratio_inner/pallas_call | solution.py:309
  82.7 4.9 %collective-permute-done.5.refs_3_ = f32[128,1,1024]{2,1,0:T(1,128)} collective-permute-done((f32[128,1,1024]{2,1,0:T(1,128)}, f32[128,1,1024]{2,1,0:T(1,128)}, u32[]{:S(2)}, u32[]{:S(2)}) %collective-permute-start.5) | collective-permute-done | bytes 524320 | tf_op jit(solution)/shard_map/ppermute | solution.py:104
  87.6 8.7 %ratio_cross.1.refs_2_.refs_1_ = f32[128,4096]{1,0:T(8,128)} custom-call(s32[4]{0:T(128)S(1)} %pad_add_fusion.side_ref.refs_0_, f32[512,1,4096]{2,1,0:T(1,128)} %refs_8_.5, f32[128,1,2048]{2,1,0:T(1,128)} %collective-permute-done.4.refs_2_, f32[128,1,1024]{2,1,0:T(1,128)} %collective-permute-done.5.refs_3_, f32[128,1,2048]{2,1,0:T(1,128)} %copy-done, ...), custom_call_target="tpu_custom_call" | custom-call | flops 44040192 | bytes 327680 | tf_op jit(solution)/shard_map/ratio_cross/pallas_call | solution.py:309
  97.3 8.9 %ratio_near.1 = (f32[128,2304]{1,0:T(8,128)}, f32[128,1792]{1,0:T(8,128)}, f32[128,4096]{1,0:T(8,128)}) custom-call(s32[4]{0:T(128)S(1)} %pad_add_fusion.side_ref.refs_0_, f32[512,1,4096]{2,1,0:T(1,128)} %refs_8_.5, f32[128,1,4096]{2,1,0:T(1,128)S(1)} %collective-permute-done.6.refs_2_, f32[1,3,128,128]{3,2,1,0:T(8,128)S(1)} %get-tuple-element.130.refs_3_.refs_4_.refs_5_, ...), custom_call_target="tpu_custom_call" | custom-call | flops 44040192 | bytes 327680 | tf_op jit(solution)/shard_map/ratio_near/pallas_call | solution.py:309
  106.2 12.3 %logs_inner.1 = (f32[256,1024]{1,0:T(8,128)}, f32[256,1024]{1,0:T(8,128)}, f32[256,1024]{1,0:T(8,128)}, f32[256,1024]{1,0:T(8,128)}, f32[256,4096]{1,0:T(8,128)}) custom-call(s32[4]{0:T(128)S(1)} %pad_add_fusion.side_ref.refs_0_, f32[256,4096]{1,0:T(8,128)} %ratio_inner.1.refs_1_.refs_2_, f32[128,4096]{1,0:T(8,128)} %ratio_cross.1.refs_2_.refs_1_, ...), custom_call_target="tpu_custom_call" | custom-call | flops 100663296 | bytes 458752 | tf_op jit(solution)/shard_map/logs_inner/pallas_call | solution.py:309
  121.5 5.0 %collective-permute-start.7 = (f32[128,2304]{1,0:T(8,128)S(1)}, f32[128,2304]{1,0:T(8,128)S(1)}, u32[]{:S(2)}, u32[]{:S(2)}) collective-permute-start(f32[128,2304]{1,0:T(8,128)S(1)} %copy-done.2), channel_id=1, source_target_pairs={{0,2},{4,6},{8,10},{12,14},{2,0},{6,4},{10,8},{14,12},{1,3},{5,7},... | collective-permute-start | bytes 3538952 | tf_op jit(solution)/shard_map/ppermute | solution.py:607
  126.6 8.8 %raw_inner.1 = (f32[512,4096]{1,0:T(8,128)S(1)}, f32[512,1,4096]{2,1,0:T(1,128)S(1)}, f32[1,128]{1,0:T(1,128)S(1)}) custom-call(s32[4]{0:T(128)S(1)} %pad_add_fusion.side_ref.refs_0_, f32[256,1024]{1,0:T(8,128)} %get-tuple-element.86.refs_0_, f32[256,1024]{1,0:T(8,128)} %get-tuple-element.87.refs_1_, f32[256,1024]{1,0:T(8,128)} %get-tuple-element.88.refs_2_, ...), custom_call_target="tpu_custom_call" | custom-call | flops 65536 | bytes 262144 | tf_op jit(solution)/shard_map/raw_inner/pallas_call | solution.py:374
  135.4 8.9 %logs_cross.1 = (f32[128,1024]{1,0:T(8,128)}, f32[128,1024]{1,0:T(8,128)}, f32[128,1024]{1,0:T(8,128)}, f32[128,1024]{1,0:T(8,128)}, f32[128,4096]{1,0:T(8,128)}) custom-call(s32[4]{0:T(128)S(1)} %pad_add_fusion.side_ref.refs_0_, f32[128,4096]{1,0:T(8,128)} %ratio_cross.1.refs_2_.refs_1_, f32[256,4096]{1,0:T(8,128)} %ratio_inner.1.refs_1_.refs_2_, ...), custom_call_target="tpu_custom_call" | custom-call | flops 44040192 | bytes 327680 | tf_op jit(solution)/shard_map/logs_cross/pallas_call | solution.py:309
  146.5 11.6 %collective-permute-start.8 = (f32[128,1792]{1,0:T(8,128)S(1)}, f32[128,1792]{1,0:T(8,128)S(1)}, u32[]{:S(2)}, u32[]{:S(2)}) collective-permute-start(f32[128,1792]{1,0:T(8,128)S(1)} %copy-done.3), channel_id=1, source_target_pairs={{0,2},{4,6},{8,10},{12,14},{2,0},{6,4},{10,8},{14,12},{1,3},{5,7},... | collective-permute-start | bytes 2752520 | tf_op jit(solution)/shard_map/ppermute | solution.py:607
  158.1 4.9 %raw_cross.1 = (f32[512,4096]{1,0:T(8,128)S(1)}, f32[512,1,4096]{2,1,0:T(1,128)S(1)}, f32[1,128]{1,0:T(1,128)S(1)}) custom-call(s32[4]{0:T(128)S(1)} %pad_add_fusion.side_ref.refs_0_, f32[128,1024]{1,0:T(8,128)} %get-tuple-element.95.refs_0_, f32[128,1024]{1,0:T(8,128)} %get-tuple-element.96.refs_1_, ...), custom_call_target="tpu_custom_call", output_to_operand_aliasing={{0}: (10, {}), {1}: (11, {})} | custom-call | flops 32768 | bytes 131072 | tf_op jit(solution)/shard_map/raw_cross/pallas_call | solution.py:374
  163.1 6.8 %collective-permute-done.7.refs_3_ = f32[128,2304]{1,0:T(8,128)S(1)} collective-permute-done((f32[128,2304]{1,0:T(8,128)S(1)}, f32[128,2304]{1,0:T(8,128)S(1)}, u32[]{:S(2)}, u32[]{:S(2)}) %collective-permute-start.7) | collective-permute-done | bytes 1179680 | tf_op jit(solution)/shard_map/ppermute | solution.py:607
  169.9 6.1 %logs_near_first.1 = (f32[128,1024]{1,0:T(8,128)S(1)}, f32[128,1024]{1,0:T(8,128)S(1)}, f32[128,2048]{1,0:T(8,128)}) custom-call(s32[4]{0:T(128)S(1)} %pad_add_fusion.side_ref.refs_0_, f32[128,4096]{1,0:T(8,128)} %get-tuple-element.81.refs_3_.refs_1_, f32[256,4096]{1,0:T(8,128)} %ratio_inner.1.refs_1_.refs_2_, ...), custom_call_target="tpu_custom_call" | custom-call | flops 44040192 | bytes 327680 | tf_op jit(solution)/shard_map/logs_near_first/pallas_call | solution.py:309
  180.0 2.6 %quotient_near_first.1._ = f32[512,1,4096]{2,1,0:T(1,128)S(1)} custom-call(s32[4]{0:T(128)S(1)} %pad_add_fusion.side_ref.refs_0_, f32[512,4096]{1,0:T(8,128)S(1)} %get-tuple-element.118.raw_ref.refs_4_, f32[128,2048]{1,0:T(8,128)} %get-tuple-element.113.m_ref, f32[512,1,4096]{2,1,0:T(1,128)S(1)} %get-tuple-element.114._), custom_call_target="tpu_custom_call", output_to_operand_aliasing={{}: (3, {})} | custom-call | flops 16384 | bytes 65536 | tf_op jit(solution)/shard_map/quotient_near_first/pallas_call | solution.py:460
  182.6 6.9 %collective-permute-done.8.refs_4_ = f32[128,1792]{1,0:T(8,128)S(1)} collective-permute-done((f32[128,1792]{1,0:T(8,128)S(1)}, f32[128,1792]{1,0:T(8,128)S(1)}, u32[]{:S(2)}, u32[]{:S(2)}) %collective-permute-start.8) | collective-permute-done | bytes 917536 | tf_op jit(solution)/shard_map/ppermute | solution.py:607
  189.5 6.3 %logs_near_later.1 = (f32[128,1024]{1,0:T(8,128)S(1)}, f32[128,1024]{1,0:T(8,128)S(1)}, f32[128,2048]{1,0:T(8,128)}) custom-call(s32[4]{0:T(128)S(1)} %pad_add_fusion.side_ref.refs_0_, f32[128,4096]{1,0:T(8,128)} %get-tuple-element.81.refs_3_.refs_1_, f32[256,4096]{1,0:T(8,128)} %ratio_inner.1.refs_1_.refs_2_, ...), custom_call_target="tpu_custom_call" | custom-call | flops 44040192 | bytes 327680 | tf_op jit(solution)/shard_map/logs_near_later/pallas_call | solution.py:309
  208.7 3.5 %collective-permute-start.24 = (f32[1,128]{1,0:T(1,128)S(1)}, f32[1,128]{1,0:T(1,128)S(1)}, u32[]{:S(2)}, u32[]{:S(2)}) collective-permute-start(f32[1,128]{1,0:T(1,128)S(1)} %mass.3.refs_0_), channel_id=1, source_target_pairs={{0,8},{2,10},{4,12},{6,14},{8,0},{10,2},{12,4},{14,6},{1,9},{3,11}... | collective-permute-start | bytes 1544 | tf_op jit(solution)/shard_map/ppermute | solution.py:507
  213.7 6.4 %outputs.1 = (f32[512,4096]{1,0:T(8,128)}, f32[512,32,128]{2,1,0:T(8,128)}) custom-call(f32[512,4096]{1,0:T(8,128)S(1)} %get-tuple-element.120.raw_ref, f32[512,32,128]{2,1,0:T(8,128)S(1)} %bitcast.6, f32[1,128]{1,0:T(1,128)S(1)} %mass.3.refs_0_, f32[1,128]{1,0:T(1,128)S(1)} %collective-permute-done.24.refs_1_), custom_call_target="tpu_custom_call" | custom-call | tf_op jit(solution)/shard_map/outputs/pallas_call | solution.py:529
  (56 shorter events, 31.4 us)
Async XLA Ops:
  4.1 39.0 %collective-permute-start = (f32[128,1,2048]{2,1,0:T(1,128)}, f32[128,1,2048]{2,1,0:T(1,128)}, u32[]{:S(2)}, u32[]{:S(2)}) collective-permute-start(f32[128,1,2048]{2,1,0:T(1,128)} %get-tuple-element.65), channel_id=1, source_target_pairs={{2,0},{6,4},{8,10},{12,14},{3,1},{7,5},{9,11},{13,15},{18,16},{22,... | collective-permute-start | bytes 3145736 | tf_op jit(solution)/shard_map/ppermute | solution.py:104
  5.4 37.7 %collective-permute-start.2 = (f32[128,1,2048]{2,1,0:T(1,128)}, f32[128,1,2048]{2,1,0:T(1,128)S(1)}, u32[]{:S(2)}, u32[]{:S(2)}) collective-permute-start(f32[128,1,2048]{2,1,0:T(1,128)} %get-tuple-element.67), channel_id=1, source_target_pairs={{4,2},{6,8},{8,6},{10,12},{5,3},{7,9},{9,7},{11,13},{20,18},{22,24... | collective-permute-start | bytes 3145736 | tf_op jit(solution)/shard_map/ppermute | solution.py:104
  6.2 36.9 %collective-permute-start.1 = (f32[128,1,1024]{2,1,0:T(1,128)}, f32[128,1,1024]{2,1,0:T(1,128)}, u32[]{:S(2)}, u32[]{:S(2)}) collective-permute-start(f32[128,1,1024]{2,1,0:T(1,128)} %get-tuple-element.66), channel_id=1, source_target_pairs={{2,0},{4,6},{10,8},{12,14},{3,1},{5,7},{11,9},{13,15},{18,16},{20,... | collective-permute-start | bytes 1572872 | tf_op jit(solution)/shard_map/ppermute | solution.py:104
  7.5 35.6 %collective-permute-start.3 = (f32[128,1,1024]{2,1,0:T(1,128)}, f32[128,1,1024]{2,1,0:T(1,128)S(1)}, u32[]{:S(2)}, u32[]{:S(2)}) collective-permute-start(f32[128,1,1024]{2,1,0:T(1,128)} %get-tuple-element.68), channel_id=1, source_target_pairs={{2,4},{4,2},{10,12},{12,10},{3,5},{5,3},{11,13},{13,11},{18,20},{2... | collective-permute-start | bytes 1572872 | tf_op jit(solution)/shard_map/ppermute | solution.py:104
  43.9 52.4 %collective-permute-start.6 = (f32[128,1,4096]{2,1,0:T(1,128)}, f32[128,1,4096]{2,1,0:T(1,128)S(1)}, u32[]{:S(2)}, u32[]{:S(2)}) collective-permute-start(f32[128,1,4096]{2,1,0:T(1,128)} %cut_near.1), channel_id=1, source_target_pairs={{0,2},{4,6},{8,10},{12,14},{2,0},{6,4},{10,8},{14,12},{1,3},{5,7},... | collective-permute-start | bytes 6291464 | tf_op jit(solution)/shard_map/ppermute | solution.py:573
  49.3 38.3 %collective-permute-start.4 = (f32[128,1,2048]{2,1,0:T(1,128)}, f32[128,1,2048]{2,1,0:T(1,128)}, u32[]{:S(2)}, u32[]{:S(2)}) collective-permute-start(f32[128,1,2048]{2,1,0:T(1,128)} %collective-permute-done), channel_id=1, source_target_pairs={{0,4},{4,8},{10,6},{14,10},{1,5},{5,9},{11,7},{15,11},{16,20},{20,... | collective-permute-start | bytes 3145736 | tf_op jit(solution)/shard_map/ppermute | solution.py:104
  54.8 32.8 %collective-permute-start.5 = (f32[128,1,1024]{2,1,0:T(1,128)}, f32[128,1,1024]{2,1,0:T(1,128)}, u32[]{:S(2)}, u32[]{:S(2)}) collective-permute-start(f32[128,1,1024]{2,1,0:T(1,128)} %collective-permute-done.1), channel_id=1, source_target_pairs={{0,4},{6,2},{8,12},{14,10},{1,5},{7,3},{9,13},{15,11},{16,20},{22,... | collective-permute-start | bytes 1572872 | tf_op jit(solution)/shard_map/ppermute | solution.py:104
  96.3 39.1 %collective-permute-start.13 = (f32[128,4096]{1,0:T(8,128)}, f32[128,4096]{1,0:T(8,128)S(1)}, u32[]{:S(2)}, u32[]{:S(2)}) collective-permute-start(f32[128,4096]{1,0:T(8,128)} %ratio_cross.1.refs_2_.refs_1_), channel_id=1, source_target_pairs={{2,4},{6,8},{10,12},{4,2},{8,6},{12,10},{3,5},{7,9},{11,13},{5,3},... | collective-permute-start | bytes 6291464 | tf_op jit(solution)/shard_map/ppermute | solution.py:599
  118.6 2.9 %collective-permute-start.9 = (f32[256,1024]{1,0:T(8,128)}, f32[256,1024]{1,0:T(8,128)S(1)}, u32[]{:S(2)}, u32[]{:S(2)}) collective-permute-start(f32[256,1024]{1,0:T(8,128)} %get-tuple-element.86.refs_0_), channel_id=1, source_target_pairs={{0,1},{1,0},{2,3},{3,2},{4,5},{5,4},{6,7},{7,6},{8,9},{9,8},{10,11... | collective-permute-start | bytes 3145736 | tf_op jit(solution)/shard_map/ppermute | solution.py:612
  118.6 7.9 %collective-permute-start.10 = (f32[256,1024]{1,0:T(8,128)}, f32[256,1024]{1,0:T(8,128)S(1)}, u32[]{:S(2)}, u32[]{:S(2)}) collective-permute-start(f32[256,1024]{1,0:T(8,128)} %get-tuple-element.87.refs_1_), channel_id=1, source_target_pairs={{0,1},{1,0},{2,3},{3,2},{4,5},{5,4},{6,7},{7,6},{8,9},{9,8},{10,11... | collective-permute-start | bytes 3145736 | tf_op jit(solution)/shard_map/ppermute | solution.py:612
  119.1 7.4 %collective-permute-start.11 = (f32[256,1024]{1,0:T(8,128)}, f32[256,1024]{1,0:T(8,128)S(1)}, u32[]{:S(2)}, u32[]{:S(2)}) collective-permute-start(f32[256,1024]{1,0:T(8,128)} %get-tuple-element.88.refs_2_), channel_id=1, source_target_pairs={{0,1},{1,0},{2,3},{3,2},{4,5},{5,4},{6,7},{7,6},{8,9},{9,8},{10,11... | collective-permute-start | bytes 3145736 | tf_op jit(solution)/shard_map/ppermute | solution.py:612
  119.2 7.3 %collective-permute-start.12 = (f32[256,1024]{1,0:T(8,128)}, f32[256,1024]{1,0:T(8,128)S(1)}, u32[]{:S(2)}, u32[]{:S(2)}) collective-permute-start(f32[256,1024]{1,0:T(8,128)} %get-tuple-element.89.refs_3_), channel_id=1, source_target_pairs={{0,1},{1,0},{2,3},{3,2},{4,5},{5,4},{6,7},{7,6},{8,9},{9,8},{10,11... | collective-permute-start | bytes 3145736 | tf_op jit(solution)/shard_map/ppermute | solution.py:612
  121.5 48.4 %collective-permute-start.7 = (f32[128,2304]{1,0:T(8,128)S(1)}, f32[128,2304]{1,0:T(8,128)S(1)}, u32[]{:S(2)}, u32[]{:S(2)}) collective-permute-start(f32[128,2304]{1,0:T(8,128)S(1)} %copy-done.2), channel_id=1, source_target_pairs={{0,2},{4,6},{8,10},{12,14},{2,0},{6,4},{10,8},{14,12},{1,3},{5,7},... | collective-permute-start | bytes 3538952 | tf_op jit(solution)/shard_map/ppermute | solution.py:607
  144.4 2.2 collective-permute-start.14
  144.4 13.7 %collective-permute-start.15 = (f32[128,1024]{1,0:T(8,128)}, f32[128,1024]{1,0:T(8,128)S(1)}, u32[]{:S(2)}, u32[]{:S(2)}) collective-permute-start(f32[128,1024]{1,0:T(8,128)} %get-tuple-element.96.refs_1_), channel_id=1, source_target_pairs={{0,1},{1,0},{2,3},{3,2},{4,5},{5,4},{6,7},{7,6},{8,9},{9,8},{10,11... | collective-permute-start | bytes 1572872 | tf_op jit(solution)/shard_map/ppermute | solution.py:612
  144.9 13.2 %collective-permute-start.16 = (f32[128,1024]{1,0:T(8,128)}, f32[128,1024]{1,0:T(8,128)S(1)}, u32[]{:S(2)}, u32[]{:S(2)}) collective-permute-start(f32[128,1024]{1,0:T(8,128)} %get-tuple-element.97.refs_2_), channel_id=1, source_target_pairs={{0,1},{1,0},{2,3},{3,2},{4,5},{5,4},{6,7},{7,6},{8,9},{9,8},{10,11... | collective-permute-start | bytes 1572872 | tf_op jit(solution)/shard_map/ppermute | solution.py:612
  145.0 13.1 %collective-permute-start.17 = (f32[128,1024]{1,0:T(8,128)}, f32[128,1024]{1,0:T(8,128)S(1)}, u32[]{:S(2)}, u32[]{:S(2)}) collective-permute-start(f32[128,1024]{1,0:T(8,128)} %get-tuple-element.98.refs_3_), channel_id=1, source_target_pairs={{0,1},{1,0},{2,3},{3,2},{4,5},{5,4},{6,7},{7,6},{8,9},{9,8},{10,11... | collective-permute-start | bytes 1572872 | tf_op jit(solution)/shard_map/ppermute | solution.py:612
  146.5 43.0 %collective-permute-start.8 = (f32[128,1792]{1,0:T(8,128)S(1)}, f32[128,1792]{1,0:T(8,128)S(1)}, u32[]{:S(2)}, u32[]{:S(2)}) collective-permute-start(f32[128,1792]{1,0:T(8,128)S(1)} %copy-done.3), channel_id=1, source_target_pairs={{0,2},{4,6},{8,10},{12,14},{2,0},{6,4},{10,8},{14,12},{1,3},{5,7},... | collective-permute-start | bytes 2752520 | tf_op jit(solution)/shard_map/ppermute | solution.py:607
  176.0 2.0 collective-permute-start.18
  176.1 2.6 %collective-permute-start.19 = (f32[128,1024]{1,0:T(8,128)S(1)}, f32[128,1024]{1,0:T(8,128)S(1)}, u32[]{:S(2)}, u32[]{:S(2)}) collective-permute-start(f32[128,1024]{1,0:T(8,128)S(1)} %get-tuple-element.108.refs_1_), channel_id=1, source_target_pairs={{0,1},{1,0},{2,3},{3,2},{4,5},{5,4},{6,7},{7,6},{8,9},{9,8},{10,11... | collective-permute-start | bytes 1572872 | tf_op jit(solution)/shard_map/ppermute | solution.py:655
  195.9 2.6 %collective-permute-start.21 = (f32[128,1024]{1,0:T(8,128)S(1)}, f32[128,1024]{1,0:T(8,128)S(1)}, u32[]{:S(2)}, u32[]{:S(2)}) collective-permute-start(f32[128,1024]{1,0:T(8,128)S(1)} %get-tuple-element.117.refs_1_), channel_id=1, source_target_pairs={{0,1},{1,0},{2,3},{3,2},{4,5},{5,4},{6,7},{7,6},{8,9},{9,8},{10,11... | collective-permute-start | bytes 1572872 | tf_op jit(solution)/shard_map/ppermute | solution.py:655
  199.7 5.2 %collective-permute-start.22 = (f32[1,128]{1,0:T(1,128)S(1)}, f32[1,128]{1,0:T(1,128)S(1)}, u32[]{:S(2)}, u32[]{:S(2)}) collective-permute-start(f32[1,128]{1,0:T(1,128)S(1)} %get-tuple-element.121.a_ref), channel_id=1, source_target_pairs={{0,2},{2,0},{4,6},{6,4},{8,10},{10,8},{12,14},{14,12},{1,3},{3,1},... | collective-permute-start | bytes 1544 | tf_op jit(solution)/shard_map/ppermute | solution.py:507
  204.9 3.8 %collective-permute-start.23 = (f32[1,128]{1,0:T(1,128)S(1)}, f32[1,128]{1,0:T(1,128)S(1)}, u32[]{:S(2)}, u32[]{:S(2)}) collective-permute-start(f32[1,128]{1,0:T(1,128)S(1)} %mass.2.a_ref), channel_id=1, source_target_pairs={{0,4},{2,6},{4,0},{6,2},{8,12},{10,14},{12,8},{14,10},{1,5},{3,7},... | collective-permute-start | bytes 1544 | tf_op jit(solution)/shard_map/ppermute | solution.py:507
  208.7 5.0 %collective-permute-start.24 = (f32[1,128]{1,0:T(1,128)S(1)}, f32[1,128]{1,0:T(1,128)S(1)}, u32[]{:S(2)}, u32[]{:S(2)}) collective-permute-start(f32[1,128]{1,0:T(1,128)S(1)} %mass.3.refs_0_), channel_id=1, source_target_pairs={{0,8},{2,10},{4,12},{6,14},{8,0},{10,2},{12,4},{14,6},{1,9},{3,11}... | collective-permute-start | bytes 1544 | tf_op jit(solution)/shard_map/ppermute | solution.py:507
  (5 other events, 67.0 us)
where the time goes:
time: 221 us; the launch traced here: 220 us
  Pallas kernels  109 us (49%)
  waiting for transfers between devices  60.8 us (28%)
  starting transfers between devices  46.9 us (21%)
  local copies, waits for them, and re-layouts  2.89 us (1%)
    pallas_call x7, Pallas kernels, blur(): pl.pallas_call(functools.partial(blur_kernel, plan), in_specs=[INSMEM] +...  62.7 us
    ppermute x6, waiting for transfers between devices, send(): return lax.ppermute(part, 'space', pairs)  36.8 us
    ppermute x2, starting transfers between devices, local(): near2 = [near(part) for part in parts]  16.6 us
    pallas_call x2, Pallas kernels, raw_rows(): pl.pallas_call(functools.partial(raw_kernel, fresh, row), grid_spec=pltpu...  13.8 us
    ppermute x2, waiting for transfers between devices, local(): near2 = [near(part) for part in parts]  13.8 us
    ppermute x6, starting transfers between devices, send(): return lax.ppermute(part, 'space', pairs)  12.2 us
    pallas_call x1, Pallas kernels, row_weights(): pl.pallas_call(functools.partial(weight_kernel, nblocks), grid=(nblocks /...  11.6 us
    ppermute x3, starting transfers between devices, mass_parts(): lax.ppermute(parts[0], 'space', [(i, i ^ 1 << bit) for i in range(count)])  8.33 us
  transfers between devices with their start and end apart: 25, of which 12 were waited for; matrix products, arithmetic and copies ran while one was open for 1% of the time, Pallas kernels for 41%

commit v1 on v0

--- a/solution.py
+++ b/solution.py
@@ -94,7 +94,7 @@
     return [(0, half), (half, quarter), ((half, 0), half), (3 * quarter, quarter)]
 
 
-def cross_send(parts, behind=()):
+def cross_send(parts):
     def send(part, numbers, ends):
         pairs = []
         for k in range(3):
@@ -108,10 +108,10 @@
     direct = lambda k: ((2 * k + 1, 2 * k + 2), (2 * k + 2, 2 * k + 1))
     relayed = [send(part, numbers, to_partner) for part, numbers in zip(parts[:2], ((0, 1), (0, 2)))]
     straight = [send(part, numbers, direct) for part, numbers in zip(parts[2:], ((1, 2), (0, 2)))]
-    a, b, c, d, *behind = lax.optimization_barrier((*relayed, *straight, *behind))
+    a, b, c, d = lax.optimization_barrier((*relayed, *straight))
     relayed, straight = [a, b], [c, d]
     passed = [send(part, numbers, onward) for part, numbers in zip(relayed, ((0, 1), (0, 2)))]
-    return passed + straight, behind
+    return passed + straight
 
 
 def cross_received(base, columns):
@@ -563,14 +563,16 @@
     def choose(choice):
         return jnp.where(odd == 0, *[c // width for c in choice]).astype(jnp.int32)
 
-    whole_rows = [(0, cols_all)]
-    near_edge = cut("cut_near", side, scaling, near_row, width, whole_rows)
+    near_columns = [(0, cols_all * 3 // 4), (cols_all * 3 // 4, cols_all // 4)]
     if spread:
-        edge = cut("cut_cross", side, scaling, cross_row, width, cross_parts(cols_all))
-        cross1, near_edge = cross_send(edge, near_edge)
+        cross1 = cross_send(cut("cut_cross", side, scaling, cross_row, width, cross_parts(cols_all)))
     else:
-        cross1 = [cross(cut("cut_cross", side, scaling, cross_row, width, whole_rows)[0])]
-    near1 = near(near_edge[0])
+        cross1 = [cross(cut("cut_cross", side, scaling, cross_row, width, [(0, cols_all)])[0])]
+    near1 = [near(part) for part in cut("cut_near", side, scaling, near_row, width, near_columns)]
+
+    def near1_at(base):
+        quarter = cols_all // GROUPS
+        return tuple((base, g * quarter) if g < GROUPS - 1 else (base + 1, 0) for g in range(GROUPS))
 
     wts = row_weights(band)
     mine = place * nlocal
@@ -583,9 +585,9 @@
         )
         *cross1, ratio_inner = lax.optimization_barrier((*cross1, ratio_inner))
     if nlocal == 1:
-        pieces = [(0, 0, width, width), (1, 0, width, (0, 2 * width)), (2, 0, width, (2 * width, 0))]
+        pieces = [(0, 0, width, width), (1, 0, width, (0, 2 * width)), (near1_at(2), 0, width, (2 * width, 0))]
         bands = band_at(0, 1)
-        ratio = blur("ratio_only", side, [scaling, *cross1, near1], pieces, bands, wts, densities, 0)
+        ratio = blur("ratio_only", side, [scaling, *cross1, *near1], pieces, bands, wts, densities, 0)
         cross2, near2 = cross(ratio), near(ratio)
     else:
         two = rows_here - 2 * width
@@ -595,13 +597,13 @@
         ratio_cross = blur(
             "ratio_cross", side, hbm(scaling, *cross1), pieces, cross_bands, wts, densities, cross_row
         )
-        ratio_cross, near1 = lax.optimization_barrier((ratio_cross, near1))
+        ratio_cross, *near1 = lax.optimization_barrier((ratio_cross, *near1))
         cross2 = cross(ratio_cross)
         half, more = cols_all // 2, 2 * width
-        pieces = [(0, (two, 0), 2 * width, (0, width)), (1, 0, width, (2 * width, 0))]
+        pieces = [(0, (two, 0), 2 * width, (0, width)), (near1_at(1), 0, width, (2 * width, 0))]
         near_bands = band_at(choose(near_row), 1)
         *parts, ratio_near = blur(
-            "ratio_near", side, hbm(scaling) + [near1], pieces, near_bands, wts, densities, near_row,
+            "ratio_near", side, hbm(scaling, *near1), pieces, near_bands, wts, densities, near_row,
             split_out=((0, half + more), (half + more, cols_all)),
         )
         near2 = [near(part) for part in parts]

time: 221 us -> 218 us (0.986)
  waiting for transfers between devices: 60.8 us -> 44.8 us
  starting transfers between devices: 46.9 us -> 60.4 us
    ppermute x6, waiting for transfers between devices: 36.8 us -> 20.8 us  [send(): return lax.ppermute(part, 'space', pairs)]
    ppermute x1 -> x2, starting transfers between devices: 5.4 us -> 14.5 us  [local(): near(part)]
    ppermute x6, starting transfers between devices: 12.2 us -> 16.9 us  [send(): return lax.ppermute(part, 'space', pairs)]
  transfers between devices with their start and end apart: 25 -> 26, of which waited for: 12 -> 12; matrix products, arithmetic and copies ran while one was open for 1% -> 1% of each run, Pallas kernels for 41% -> 42%
where the time goes in v1:
time: 218 us; the launch traced here: 217 us
  Pallas kernels  109 us (50%)
  starting transfers between devices  60.4 us (28%)
  waiting for transfers between devices  44.8 us (21%)
  local copies, waits for them, and re-layouts  2.26 us (1%)
    pallas_call x7, Pallas kernels, blur(): pl.pallas_call(functools.partial(blur_kernel, plan), in_specs=[INSMEM] +...  63 us
    ppermute x6, waiting for transfers between devices, send(): return lax.ppermute(part, 'space', pairs)  20.8 us
    ppermute x6, starting transfers between devices, send(): return lax.ppermute(part, 'space', pairs)  16.9 us
    ppermute x2, starting transfers between devices, local(): near2 = [near(part) for part in parts]  16.4 us
    ppermute x2, starting transfers between devices, local(): near(part)  14.5 us
    pallas_call x2, Pallas kernels, raw_rows(): pl.pallas_call(functools.partial(raw_kernel, fresh, row), grid_spec=pltpu...  13.8 us
    ppermute x2, waiting for transfers between devices, local(): near2 = [near(part) for part in parts]  13.7 us
    pallas_call x1, Pallas kernels, row_weights(): pl.pallas_call(functools.partial(weight_kernel, nblocks), grid=(nblocks /...  11.6 us
  transfers between devices with their start and end apart: 26, of which 12 were waited for; matrix products, arithmetic and copies ran while one was open for 1% of the time, Pallas kernels for 42%

profile of v1, /device:TPU:0, one launch (start us, length us, event | category | flops | bytes accessed | tf_op | source)
XLA Modules:
  0.0 217.4 jit_solution(18274225341843505446)
XLA Ops:
  0.7 3.4 %cut_cross.1 = (f32[128,1,2048]{2,1,0:T(1,128)}, f32[128,1,1024]{2,1,0:T(1,128)}, f32[128,1,2048]{2,1,0:T(1,128)}, f32[128,1,1024]{2,1,0:T(1,128)}) custom-call(s32[4]{0:T(128)S(1)} %pad_add_fusion.side_ref.refs_0_, f32[512,1,4096]{2,1,0:T(1,128)} %refs_8_.5), custom_call_target="tpu_custom_call" | custom-call | tf_op jit(solution)/shard_map/cut_cross/pallas_call | solution.py:72
  8.2 3.1 %cut_near.1 = (f32[128,1,3072]{2,1,0:T(1,128)}, f32[128,1,1024]{2,1,0:T(1,128)}) custom-call(s32[4]{0:T(128)S(1)} %pad_add_fusion.side_ref.refs_0_, f32[512,1,4096]{2,1,0:T(1,128)} %refs_8_.5), custom_call_target="tpu_custom_call" | custom-call | tf_op jit(solution)/shard_map/cut_near/pallas_call | solution.py:72
  11.2 14.5 %collective-permute-start.6 = (f32[128,1,3072]{2,1,0:T(1,128)}, f32[128,1,3072]{2,1,0:T(1,128)S(1)}, u32[]{:S(2)}, u32[]{:S(2)}) collective-permute-start(f32[128,1,3072]{2,1,0:T(1,128)} %get-tuple-element.81), channel_id=1, source_target_pairs={{0,2},{4,6},{8,10},{12,14},{2,0},{6,4},{10,8},{14,12},{1,3},{5,7},... | collective-permute-start | bytes 4718600 | tf_op jit(solution)/shard_map/ppermute | solution.py:571
  25.7 18.2 %collective-permute-done.1 = f32[128,1,1024]{2,1,0:T(1,128)} collective-permute-done((f32[128,1,1024]{2,1,0:T(1,128)}, f32[128,1,1024]{2,1,0:T(1,128)}, u32[]{:S(2)}, u32[]{:S(2)}) %collective-permute-start.1) | collective-permute-done | bytes 524320 | tf_op jit(solution)/shard_map/ppermute | solution.py:104
  43.9 7.6 %collective-permute-start.4 = (f32[128,1,2048]{2,1,0:T(1,128)}, f32[128,1,2048]{2,1,0:T(1,128)}, u32[]{:S(2)}, u32[]{:S(2)}) collective-permute-start(f32[128,1,2048]{2,1,0:T(1,128)} %collective-permute-done), channel_id=1, source_target_pairs={{0,4},{4,8},{10,6},{14,10},{1,5},{5,9},{11,7},{15,11},{16,20},{20,... | collective-permute-start | bytes 3145736 | tf_op jit(solution)/shard_map/ppermute | solution.py:104
  51.6 5.3 %collective-permute-start.5 = (f32[128,1,1024]{2,1,0:T(1,128)}, f32[128,1,1024]{2,1,0:T(1,128)}, u32[]{:S(2)}, u32[]{:S(2)}) collective-permute-start(f32[128,1,1024]{2,1,0:T(1,128)} %collective-permute-done.1), channel_id=1, source_target_pairs={{0,4},{6,2},{8,12},{14,10},{1,5},{7,3},{9,13},{15,11},{16,20},{22,... | collective-permute-start | bytes 1572872 | tf_op jit(solution)/shard_map/ppermute | solution.py:104
  56.9 11.6 %row_weights.1 = (bf16[16,256,512]{2,1,0:T(8,128)(2,1)}, bf16[16,256,512]{2,1,0:T(8,128)(2,1)}) custom-call(f32[32,3,128,128]{3,2,1,0:T(8,128)} %band_ref.1), custom_call_target="tpu_custom_call" | custom-call | tf_op jit(solution)/shard_map/row_weights/pallas_call | solution.py:149
  69.5 11.4 %ratio_inner.1.refs_1_.refs_2_ = f32[256,4096]{1,0:T(8,128)} custom-call(s32[4]{0:T(128)S(1)} %pad_add_fusion.side_ref.refs_0_, f32[512,1,4096]{2,1,0:T(1,128)} %refs_8_.5, f32[2,3,128,128]{3,2,1,0:T(8,128)S(1)} %constant_dynamic-slice_fusion.2.refs_2_.refs_4_, bf16[16,256,512]{2,1,0:T(8,128)(2,1)} %get-tuple-element.75.refs_3_.refs_7_.refs_5_.refs_6_, ...), custom_call_target="tpu_custom_call" | custom-call | flops 100663296 | bytes 458752 | tf_op jit(solution)/shard_map/ratio_inner/pallas_call | solution.py:309
  84.6 8.7 %ratio_cross.1.refs_2_.refs_1_ = f32[128,4096]{1,0:T(8,128)} custom-call(s32[4]{0:T(128)S(1)} %pad_add_fusion.side_ref.refs_0_, f32[512,1,4096]{2,1,0:T(1,128)} %refs_8_.5, f32[128,1,2048]{2,1,0:T(1,128)} %collective-permute-done.4.refs_2_, f32[128,1,1024]{2,1,0:T(1,128)} %collective-permute-done.5.refs_3_, f32[128,1,2048]{2,1,0:T(1,128)} %copy-done.1, ...), custom_call_target="tpu_custom_call" | custom-call | flops 44040192 | bytes 327680 | tf_op jit(solution)/shard_map/ratio_cross/pallas_call | solution.py:309
  94.5 9.0 %ratio_near.1 = (f32[128,2304]{1,0:T(8,128)}, f32[128,1792]{1,0:T(8,128)}, f32[128,4096]{1,0:T(8,128)}) custom-call(s32[4]{0:T(128)S(1)} %pad_add_fusion.side_ref.refs_0_, f32[512,1,4096]{2,1,0:T(1,128)} %refs_8_.5, f32[128,1,3072]{2,1,0:T(1,128)} %copy-done, f32[128,1,1024]{2,1,0:T(1,128)} %collective-permute-done.7.refs_3_, ...), custom_call_target="tpu_custom_call" | custom-call | flops 44040192 | bytes 327680 | tf_op jit(solution)/shard_map/ratio_near/pallas_call | solution.py:309
  103.6 12.4 %logs_inner.1 = (f32[256,1024]{1,0:T(8,128)}, f32[256,1024]{1,0:T(8,128)}, f32[256,1024]{1,0:T(8,128)}, f32[256,1024]{1,0:T(8,128)}, f32[256,4096]{1,0:T(8,128)}) custom-call(s32[4]{0:T(128)S(1)} %pad_add_fusion.side_ref.refs_0_, f32[256,4096]{1,0:T(8,128)} %ratio_inner.1.refs_1_.refs_2_, f32[128,4096]{1,0:T(8,128)} %ratio_cross.1.refs_2_.refs_1_, ...), custom_call_target="tpu_custom_call" | custom-call | flops 100663296 | bytes 458752 | tf_op jit(solution)/shard_map/logs_inner/pallas_call | solution.py:309
  118.9 4.9 %collective-permute-start.8 = (f32[128,2304]{1,0:T(8,128)S(1)}, f32[128,2304]{1,0:T(8,128)S(1)}, u32[]{:S(2)}, u32[]{:S(2)}) collective-permute-start(f32[128,2304]{1,0:T(8,128)S(1)} %copy-done.3), channel_id=1, source_target_pairs={{0,2},{4,6},{8,10},{12,14},{2,0},{6,4},{10,8},{14,12},{1,3},{5,7},... | collective-permute-start | bytes 3538952 | tf_op jit(solution)/shard_map/ppermute | solution.py:609
  123.9 8.8 %raw_inner.1 = (f32[512,4096]{1,0:T(8,128)S(1)}, f32[512,1,4096]{2,1,0:T(1,128)S(1)}, f32[1,128]{1,0:T(1,128)S(1)}) custom-call(s32[4]{0:T(128)S(1)} %pad_add_fusion.side_ref.refs_0_, f32[256,1024]{1,0:T(8,128)} %get-tuple-element.90.refs_0_, f32[256,1024]{1,0:T(8,128)} %get-tuple-element.91.refs_1_, f32[256,1024]{1,0:T(8,128)} %get-tuple-element.92.refs_2_, ...), custom_call_target="tpu_custom_call" | custom-call | flops 65536 | bytes 262144 | tf_op jit(solution)/shard_map/raw_inner/pallas_call | solution.py:374
  132.7 8.9 %logs_cross.1 = (f32[128,1024]{1,0:T(8,128)}, f32[128,1024]{1,0:T(8,128)}, f32[128,1024]{1,0:T(8,128)}, f32[128,1024]{1,0:T(8,128)}, f32[128,4096]{1,0:T(8,128)}) custom-call(s32[4]{0:T(128)S(1)} %pad_add_fusion.side_ref.refs_0_, f32[128,4096]{1,0:T(8,128)} %ratio_cross.1.refs_2_.refs_1_, f32[256,4096]{1,0:T(8,128)} %ratio_inner.1.refs_1_.refs_2_, ...), custom_call_target="tpu_custom_call" | custom-call | flops 44040192 | bytes 327680 | tf_op jit(solution)/shard_map/logs_cross/pallas_call | solution.py:309
  143.8 11.5 %collective-permute-start.9 = (f32[128,1792]{1,0:T(8,128)S(1)}, f32[128,1792]{1,0:T(8,128)S(1)}, u32[]{:S(2)}, u32[]{:S(2)}) collective-permute-start(f32[128,1792]{1,0:T(8,128)S(1)} %copy-done.4), channel_id=1, source_target_pairs={{0,2},{4,6},{8,10},{12,14},{2,0},{6,4},{10,8},{14,12},{1,3},{5,7},... | collective-permute-start | bytes 2752520 | tf_op jit(solution)/shard_map/ppermute | solution.py:609
  155.4 4.9 %raw_cross.1 = (f32[512,4096]{1,0:T(8,128)S(1)}, f32[512,1,4096]{2,1,0:T(1,128)S(1)}, f32[1,128]{1,0:T(1,128)S(1)}) custom-call(s32[4]{0:T(128)S(1)} %pad_add_fusion.side_ref.refs_0_, f32[128,1024]{1,0:T(8,128)} %get-tuple-element.99.refs_0_, f32[128,1024]{1,0:T(8,128)} %get-tuple-element.100.refs_1_, ...), custom_call_target="tpu_custom_call", output_to_operand_aliasing={{0}: (10, {}), {1}: (11, {})} | custom-call | flops 32768 | bytes 131072 | tf_op jit(solution)/shard_map/raw_cross/pallas_call | solution.py:374
  160.3 6.8 %collective-permute-done.8.refs_3_ = f32[128,2304]{1,0:T(8,128)S(1)} collective-permute-done((f32[128,2304]{1,0:T(8,128)S(1)}, f32[128,2304]{1,0:T(8,128)S(1)}, u32[]{:S(2)}, u32[]{:S(2)}) %collective-permute-start.8) | collective-permute-done | bytes 1179680 | tf_op jit(solution)/shard_map/ppermute | solution.py:609
  167.2 6.2 %logs_near_first.1 = (f32[128,1024]{1,0:T(8,128)S(1)}, f32[128,1024]{1,0:T(8,128)S(1)}, f32[128,2048]{1,0:T(8,128)}) custom-call(s32[4]{0:T(128)S(1)} %pad_add_fusion.side_ref.refs_0_, f32[128,4096]{1,0:T(8,128)} %get-tuple-element.85.refs_3_.refs_1_, f32[256,4096]{1,0:T(8,128)} %ratio_inner.1.refs_1_.refs_2_, ...), custom_call_target="tpu_custom_call" | custom-call | flops 44040192 | bytes 327680 | tf_op jit(solution)/shard_map/logs_near_first/pallas_call | solution.py:309
  177.3 2.6 %quotient_near_first.1._ = f32[512,1,4096]{2,1,0:T(1,128)S(1)} custom-call(s32[4]{0:T(128)S(1)} %pad_add_fusion.side_ref.refs_0_, f32[512,4096]{1,0:T(8,128)S(1)} %get-tuple-element.122.raw_ref.refs_4_, f32[128,2048]{1,0:T(8,128)} %get-tuple-element.117.m_ref, f32[512,1,4096]{2,1,0:T(1,128)S(1)} %get-tuple-element.118._), custom_call_target="tpu_custom_call", output_to_operand_aliasing={{}: (3, {})} | custom-call | flops 16384 | bytes 65536 | tf_op jit(solution)/shard_map/quotient_near_first/pallas_call | solution.py:460
  179.9 6.9 %collective-permute-done.9.refs_4_ = f32[128,1792]{1,0:T(8,128)S(1)} collective-permute-done((f32[128,1792]{1,0:T(8,128)S(1)}, f32[128,1792]{1,0:T(8,128)S(1)}, u32[]{:S(2)}, u32[]{:S(2)}) %collective-permute-start.9) | collective-permute-done | bytes 917536 | tf_op jit(solution)/shard_map/ppermute | solution.py:609
  186.8 6.3 %logs_near_later.1 = (f32[128,1024]{1,0:T(8,128)S(1)}, f32[128,1024]{1,0:T(8,128)S(1)}, f32[128,2048]{1,0:T(8,128)}) custom-call(s32[4]{0:T(128)S(1)} %pad_add_fusion.side_ref.refs_0_, f32[128,4096]{1,0:T(8,128)} %get-tuple-element.85.refs_3_.refs_1_, f32[256,4096]{1,0:T(8,128)} %ratio_inner.1.refs_1_.refs_2_, ...), custom_call_target="tpu_custom_call" | custom-call | flops 44040192 | bytes 327680 | tf_op jit(solution)/shard_map/logs_near_later/pallas_call | solution.py:309
  199.6 2.6 %quotient_near_later.1 = f32[512,1,4096]{2,1,0:T(1,128)S(1)} custom-call(s32[4]{0:T(128)S(1)} %pad_add_fusion.side_ref.refs_0_, f32[512,4096]{1,0:T(8,128)S(1)} %get-tuple-element.124.raw_ref, f32[128,2048]{1,0:T(8,128)} %get-tuple-element.126.m_ref, f32[512,1,4096]{2,1,0:T(1,128)S(1)} %quotient_near_first.1._), custom_call_target="tpu_custom_call", output_to_operand_aliasing={{}: (3, {})} | custom-call | flops 16384 | bytes 65536 | tf_op jit(solution)/shard_map/quotient_near_later/pallas_call | solution.py:460
  206.0 3.4 %collective-permute-start.25 = (f32[1,128]{1,0:T(1,128)S(1)}, f32[1,128]{1,0:T(1,128)S(1)}, u32[]{:S(2)}, u32[]{:S(2)}) collective-permute-start(f32[1,128]{1,0:T(1,128)S(1)} %mass.3.refs_0_), channel_id=1, source_target_pairs={{0,8},{2,10},{4,12},{6,14},{8,0},{10,2},{12,4},{14,6},{1,9},{3,11}... | collective-permute-start | bytes 1544 | tf_op jit(solution)/shard_map/ppermute | solution.py:507
  211.0 6.4 %outputs.1 = (f32[512,4096]{1,0:T(8,128)}, f32[512,32,128]{2,1,0:T(8,128)}) custom-call(f32[512,4096]{1,0:T(8,128)S(1)} %get-tuple-element.124.raw_ref, f32[512,32,128]{2,1,0:T(8,128)S(1)} %bitcast.6, f32[1,128]{1,0:T(1,128)S(1)} %mass.3.refs_0_, f32[1,128]{1,0:T(1,128)S(1)} %collective-permute-done.25.refs_1_), custom_call_target="tpu_custom_call" | custom-call | tf_op jit(solution)/shard_map/outputs/pallas_call | solution.py:529
  (60 shorter events, 30.8 us)
Async XLA Ops:
  4.1 39.8 %collective-permute-start = (f32[128,1,2048]{2,1,0:T(1,128)}, f32[128,1,2048]{2,1,0:T(1,128)}, u32[]{:S(2)}, u32[]{:S(2)}) collective-permute-start(f32[128,1,2048]{2,1,0:T(1,128)} %get-tuple-element.67), channel_id=1, source_target_pairs={{2,0},{6,4},{8,10},{12,14},{3,1},{7,5},{9,11},{13,15},{18,16},{22,... | collective-permute-start | bytes 3145736 | tf_op jit(solution)/shard_map/ppermute | solution.py:104
  5.4 38.5 %collective-permute-start.2 = (f32[128,1,2048]{2,1,0:T(1,128)}, f32[128,1,2048]{2,1,0:T(1,128)S(1)}, u32[]{:S(2)}, u32[]{:S(2)}) collective-permute-start(f32[128,1,2048]{2,1,0:T(1,128)} %get-tuple-element.69), channel_id=1, source_target_pairs={{4,2},{6,8},{8,6},{10,12},{5,3},{7,9},{9,7},{11,13},{20,18},{22,24... | collective-permute-start | bytes 3145736 | tf_op jit(solution)/shard_map/ppermute | solution.py:104
  6.2 37.7 %collective-permute-start.1 = (f32[128,1,1024]{2,1,0:T(1,128)}, f32[128,1,1024]{2,1,0:T(1,128)}, u32[]{:S(2)}, u32[]{:S(2)}) collective-permute-start(f32[128,1,1024]{2,1,0:T(1,128)} %get-tuple-element.68), channel_id=1, source_target_pairs={{2,0},{4,6},{10,8},{12,14},{3,1},{5,7},{11,9},{13,15},{18,16},{20,... | collective-permute-start | bytes 1572872 | tf_op jit(solution)/shard_map/ppermute | solution.py:104
  7.5 36.4 %collective-permute-start.3 = (f32[128,1,1024]{2,1,0:T(1,128)}, f32[128,1,1024]{2,1,0:T(1,128)S(1)}, u32[]{:S(2)}, u32[]{:S(2)}) collective-permute-start(f32[128,1,1024]{2,1,0:T(1,128)} %get-tuple-element.70), channel_id=1, source_target_pairs={{2,4},{4,2},{10,12},{12,10},{3,5},{5,3},{11,13},{13,11},{18,20},{2... | collective-permute-start | bytes 1572872 | tf_op jit(solution)/shard_map/ppermute | solution.py:104
  11.2 82.1 %collective-permute-start.6 = (f32[128,1,3072]{2,1,0:T(1,128)}, f32[128,1,3072]{2,1,0:T(1,128)S(1)}, u32[]{:S(2)}, u32[]{:S(2)}) collective-permute-start(f32[128,1,3072]{2,1,0:T(1,128)} %get-tuple-element.81), channel_id=1, source_target_pairs={{0,2},{4,6},{8,10},{12,14},{2,0},{6,4},{10,8},{14,12},{1,3},{5,7},... | collective-permute-start | bytes 4718600 | tf_op jit(solution)/shard_map/ppermute | solution.py:571
  43.9 40.7 %collective-permute-start.4 = (f32[128,1,2048]{2,1,0:T(1,128)}, f32[128,1,2048]{2,1,0:T(1,128)}, u32[]{:S(2)}, u32[]{:S(2)}) collective-permute-start(f32[128,1,2048]{2,1,0:T(1,128)} %collective-permute-done), channel_id=1, source_target_pairs={{0,4},{4,8},{10,6},{14,10},{1,5},{5,9},{11,7},{15,11},{16,20},{20,... | collective-permute-start | bytes 3145736 | tf_op jit(solution)/shard_map/ppermute | solution.py:104
  51.6 33.0 %collective-permute-start.5 = (f32[128,1,1024]{2,1,0:T(1,128)}, f32[128,1,1024]{2,1,0:T(1,128)}, u32[]{:S(2)}, u32[]{:S(2)}) collective-permute-start(f32[128,1,1024]{2,1,0:T(1,128)} %collective-permute-done.1), channel_id=1, source_target_pairs={{0,4},{6,2},{8,12},{14,10},{1,5},{7,3},{9,13},{15,11},{16,20},{22,... | collective-permute-start | bytes 1572872 | tf_op jit(solution)/shard_map/ppermute | solution.py:104
  56.9 36.5 %collective-permute-start.7 = (f32[128,1,1024]{2,1,0:T(1,128)}, f32[128,1,1024]{2,1,0:T(1,128)}, u32[]{:S(2)}, u32[]{:S(2)}) collective-permute-start(f32[128,1,1024]{2,1,0:T(1,128)} %get-tuple-element.82), channel_id=1, source_target_pairs={{0,2},{4,6},{8,10},{12,14},{2,0},{6,4},{10,8},{14,12},{1,3},{5,7},... | collective-permute-start | bytes 1572872 | tf_op jit(solution)/shard_map/ppermute | solution.py:571
  93.4 39.3 %collective-permute-start.14 = (f32[128,4096]{1,0:T(8,128)}, f32[128,4096]{1,0:T(8,128)S(1)}, u32[]{:S(2)}, u32[]{:S(2)}) collective-permute-start(f32[128,4096]{1,0:T(8,128)} %ratio_cross.1.refs_2_.refs_1_), channel_id=1, source_target_pairs={{2,4},{6,8},{10,12},{4,2},{8,6},{12,10},{3,5},{7,9},{11,13},{5,3},... | collective-permute-start | bytes 6291464 | tf_op jit(solution)/shard_map/ppermute | solution.py:601
  116.0 2.9 %collective-permute-start.10 = (f32[256,1024]{1,0:T(8,128)}, f32[256,1024]{1,0:T(8,128)S(1)}, u32[]{:S(2)}, u32[]{:S(2)}) collective-permute-start(f32[256,1024]{1,0:T(8,128)} %get-tuple-element.90.refs_0_), channel_id=1, source_target_pairs={{0,1},{1,0},{2,3},{3,2},{4,5},{5,4},{6,7},{7,6},{8,9},{9,8},{10,11... | collective-permute-start | bytes 3145736 | tf_op jit(solution)/shard_map/ppermute | solution.py:614
  116.1 7.8 %collective-permute-start.11 = (f32[256,1024]{1,0:T(8,128)}, f32[256,1024]{1,0:T(8,128)S(1)}, u32[]{:S(2)}, u32[]{:S(2)}) collective-permute-start(f32[256,1024]{1,0:T(8,128)} %get-tuple-element.91.refs_1_), channel_id=1, source_target_pairs={{0,1},{1,0},{2,3},{3,2},{4,5},{5,4},{6,7},{7,6},{8,9},{9,8},{10,11... | collective-permute-start | bytes 3145736 | tf_op jit(solution)/shard_map/ppermute | solution.py:614
  116.6 7.3 %collective-permute-start.12 = (f32[256,1024]{1,0:T(8,128)}, f32[256,1024]{1,0:T(8,128)S(1)}, u32[]{:S(2)}, u32[]{:S(2)}) collective-permute-start(f32[256,1024]{1,0:T(8,128)} %get-tuple-element.92.refs_2_), channel_id=1, source_target_pairs={{0,1},{1,0},{2,3},{3,2},{4,5},{5,4},{6,7},{7,6},{8,9},{9,8},{10,11... | collective-permute-start | bytes 3145736 | tf_op jit(solution)/shard_map/ppermute | solution.py:614
  116.7 7.2 %collective-permute-start.13 = (f32[256,1024]{1,0:T(8,128)}, f32[256,1024]{1,0:T(8,128)S(1)}, u32[]{:S(2)}, u32[]{:S(2)}) collective-permute-start(f32[256,1024]{1,0:T(8,128)} %get-tuple-element.93.refs_3_), channel_id=1, source_target_pairs={{0,1},{1,0},{2,3},{3,2},{4,5},{5,4},{6,7},{7,6},{8,9},{9,8},{10,11... | collective-permute-start | bytes 3145736 | tf_op jit(solution)/shard_map/ppermute | solution.py:614
  118.9 48.2 %collective-permute-start.8 = (f32[128,2304]{1,0:T(8,128)S(1)}, f32[128,2304]{1,0:T(8,128)S(1)}, u32[]{:S(2)}, u32[]{:S(2)}) collective-permute-start(f32[128,2304]{1,0:T(8,128)S(1)} %copy-done.3), channel_id=1, source_target_pairs={{0,2},{4,6},{8,10},{12,14},{2,0},{6,4},{10,8},{14,12},{1,3},{5,7},... | collective-permute-start | bytes 3538952 | tf_op jit(solution)/shard_map/ppermute | solution.py:609
  141.6 2.2 %collective-permute-start.15 = (f32[128,1024]{1,0:T(8,128)}, f32[128,1024]{1,0:T(8,128)S(1)}, u32[]{:S(2)}, u32[]{:S(2)}) collective-permute-start(f32[128,1024]{1,0:T(8,128)} %get-tuple-element.99.refs_0_), channel_id=1, source_target_pairs={{0,1},{1,0},{2,3},{3,2},{4,5},{5,4},{6,7},{7,6},{8,9},{9,8},{10,11... | collective-permute-start | bytes 1572872 | tf_op jit(solution)/shard_map/ppermute | solution.py:614
  141.7 13.7 %collective-permute-start.16 = (f32[128,1024]{1,0:T(8,128)}, f32[128,1024]{1,0:T(8,128)S(1)}, u32[]{:S(2)}, u32[]{:S(2)}) collective-permute-start(f32[128,1024]{1,0:T(8,128)} %get-tuple-element.100.refs_1_), channel_id=1, source_target_pairs={{0,1},{1,0},{2,3},{3,2},{4,5},{5,4},{6,7},{7,6},{8,9},{9,8},{10,11... | collective-permute-start | bytes 1572872 | tf_op jit(solution)/shard_map/ppermute | solution.py:614
  142.2 13.2 %collective-permute-start.17 = (f32[128,1024]{1,0:T(8,128)}, f32[128,1024]{1,0:T(8,128)S(1)}, u32[]{:S(2)}, u32[]{:S(2)}) collective-permute-start(f32[128,1024]{1,0:T(8,128)} %get-tuple-element.101.refs_2_), channel_id=1, source_target_pairs={{0,1},{1,0},{2,3},{3,2},{4,5},{5,4},{6,7},{7,6},{8,9},{9,8},{10,11... | collective-permute-start | bytes 1572872 | tf_op jit(solution)/shard_map/ppermute | solution.py:614
  142.3 13.1 %collective-permute-start.18 = (f32[128,1024]{1,0:T(8,128)}, f32[128,1024]{1,0:T(8,128)S(1)}, u32[]{:S(2)}, u32[]{:S(2)}) collective-permute-start(f32[128,1024]{1,0:T(8,128)} %get-tuple-element.102.refs_3_), channel_id=1, source_target_pairs={{0,1},{1,0},{2,3},{3,2},{4,5},{5,4},{6,7},{7,6},{8,9},{9,8},{10,11... | collective-permute-start | bytes 1572872 | tf_op jit(solution)/shard_map/ppermute | solution.py:614
  143.8 42.9 %collective-permute-start.9 = (f32[128,1792]{1,0:T(8,128)S(1)}, f32[128,1792]{1,0:T(8,128)S(1)}, u32[]{:S(2)}, u32[]{:S(2)}) collective-permute-start(f32[128,1792]{1,0:T(8,128)S(1)} %copy-done.4), channel_id=1, source_target_pairs={{0,2},{4,6},{8,10},{12,14},{2,0},{6,4},{10,8},{14,12},{1,3},{5,7},... | collective-permute-start | bytes 2752520 | tf_op jit(solution)/shard_map/ppermute | solution.py:609
  173.4 2.6 %collective-permute-start.20 = (f32[128,1024]{1,0:T(8,128)S(1)}, f32[128,1024]{1,0:T(8,128)S(1)}, u32[]{:S(2)}, u32[]{:S(2)}) collective-permute-start(f32[128,1024]{1,0:T(8,128)S(1)} %get-tuple-element.112.refs_1_), channel_id=1, source_target_pairs={{0,1},{1,0},{2,3},{3,2},{4,5},{5,4},{6,7},{7,6},{8,9},{9,8},{10,11... | collective-permute-start | bytes 1572872 | tf_op jit(solution)/shard_map/ppermute | solution.py:657
  193.2 2.6 %collective-permute-start.22 = (f32[128,1024]{1,0:T(8,128)S(1)}, f32[128,1024]{1,0:T(8,128)S(1)}, u32[]{:S(2)}, u32[]{:S(2)}) collective-permute-start(f32[128,1024]{1,0:T(8,128)S(1)} %get-tuple-element.121.refs_1_), channel_id=1, source_target_pairs={{0,1},{1,0},{2,3},{3,2},{4,5},{5,4},{6,7},{7,6},{8,9},{9,8},{10,11... | collective-permute-start | bytes 1572872 | tf_op jit(solution)/shard_map/ppermute | solution.py:657
  197.0 5.1 %collective-permute-start.23 = (f32[1,128]{1,0:T(1,128)S(1)}, f32[1,128]{1,0:T(1,128)S(1)}, u32[]{:S(2)}, u32[]{:S(2)}) collective-permute-start(f32[1,128]{1,0:T(1,128)S(1)} %get-tuple-element.125.a_ref), channel_id=1, source_target_pairs={{0,2},{2,0},{4,6},{6,4},{8,10},{10,8},{12,14},{14,12},{1,3},{3,1},... | collective-permute-start | bytes 1544 | tf_op jit(solution)/shard_map/ppermute | solution.py:507
  202.2 3.8 %collective-permute-start.24 = (f32[1,128]{1,0:T(1,128)S(1)}, f32[1,128]{1,0:T(1,128)S(1)}, u32[]{:S(2)}, u32[]{:S(2)}) collective-permute-start(f32[1,128]{1,0:T(1,128)S(1)} %mass.2.a_ref), channel_id=1, source_target_pairs={{0,4},{2,6},{4,0},{6,2},{8,12},{10,14},{12,8},{14,10},{1,5},{3,7},... | collective-permute-start | bytes 1544 | tf_op jit(solution)/shard_map/ppermute | solution.py:507
  206.0 5.0 %collective-permute-start.25 = (f32[1,128]{1,0:T(1,128)S(1)}, f32[1,128]{1,0:T(1,128)S(1)}, u32[]{:S(2)}, u32[]{:S(2)}) collective-permute-start(f32[1,128]{1,0:T(1,128)S(1)} %mass.3.refs_0_), channel_id=1, source_target_pairs={{0,8},{2,10},{4,12},{6,14},{8,0},{10,2},{12,4},{14,6},{1,9},{3,11}... | collective-permute-start | bytes 1544 | tf_op jit(solution)/shard_map/ppermute | solution.py:507
  (7 other events, 105.7 us)

commit v2 on v1

--- a/solution.py
+++ b/solution.py
@@ -157,11 +157,13 @@
 
 
 def blur_kernel(plan, *refs):
-    pieces, narrays, extra, final, split_out, units, groups = plan
+    pieces, narrays, extra, final, split_out, units, groups, begun_at = plan
     side_ref, refs = refs[0], refs[1:]
     arrays = refs[:narrays]
     band_ref, high_ref, low_ref, extra_ref = refs[narrays : narrays + 4]
     rest = refs[narrays + 4 :]
+    if begun_at is not None:
+        begun_ref, rest = rest[0], rest[1:]
     if final:
         weights_ref, rest = rest[0], rest[1:]
         all_weights = weights_ref[0]
@@ -173,6 +175,8 @@
     outs = rest[:nouts]
     field, a_both, y_both, whigh, wlow, other = rest[nouts : nouts + 6]
     *results, in_sems, late_sems, out_sems = rest[nouts + 6 :]
+    if begun_at is not None:
+        *results, begun = results
 
     side = side_ref[0]
     nout, _, width, _ = band_ref.shape
@@ -218,6 +222,16 @@
     waiting = list(groups)
     for u in range(len(units)):
         inside.append([start_in(u, k) for k in range(len(pieces))])
+        if begun_at is not None:
+            start, stop = units[u]
+            inside[u].append(
+                pltpu.make_async_copy(
+                    begun_ref.at[:, pl.ds(start - begun_at, stop - start)],
+                    begun.at[:, pl.ds(start, stop - start)],
+                    in_sems.at[u, len(pieces)],
+                )
+            )
+            inside[u][-1].start()
         if u > 0 and waiting:
             for copy in late[waiting.pop(0)]:
                 copy.start()
@@ -227,8 +241,12 @@
 
     blocks = [(i, min(2, nout - i)) for i in range(0, nout, 2)]
     total = nout * width
-    a_both[...] = jnp.zeros_like(a_both)
-    for first, n in blocks:
+    if begun_at is None:
+        a_both[...] = jnp.zeros_like(a_both)
+    else:
+        for part, value in enumerate(split(jnp.where(side == 0, band_ref[0, 2], band_ref[0, 0]))):
+            a_both[part * width : (part + 1) * width, :] = value
+    for first, n in blocks if begun_at is None else ():
         for i in range(n):
             for j in range(3):
                 for part, value in enumerate(split(band_ref[first + i, j])):
@@ -244,8 +262,11 @@
             at = slice(i * 2 * width, (i + 1) * 2 * width)
             to = slice((2 * i + 1) * width, (2 * i + 3) * width)
             for first, n in blocks:
-                a = a_both[2 * first * width : 2 * (first + n) * width, : (n + 2) * width]
-                y = dot3(a, split(field[first * width : (first + n + 2) * width, at]), ((1,), (0,)))
+                k = width if begun_at is not None else (n + 2) * width
+                a = a_both[2 * first * width : 2 * (first + n) * width, :k]
+                y = dot3(a, split(field[first * width : first * width + k, at]), ((1,), (0,)))
+                if begun_at is not None:
+                    y += begun[:, at]
                 for part, value in enumerate(split(y)):
                     row = part * total + first * width
                     y_both[row : row + n * width, to] = value
@@ -288,12 +309,12 @@
 
 def blur(
     name, side, arrays, pieces, bands, weights, other, extra,
-    map_weights=None, pin=True, split_out=(), units=None, groups=tuple(range(GROUPS)),
+    map_weights=None, pin=True, split_out=(), units=None, groups=tuple(range(GROUPS)), begun=None,
 ):
     nout, _, width, _ = bands.shape
     npairs = weights[0].shape[0]
     columns = npairs * 2 * width
-    rows, depth = nout * width, (nout + 2) * width
+    rows, depth = nout * width, (nout + 2) * width if begun is None else width
     final = map_weights is not None
     nouts = 2 if final else 1
     kind = pltpu.HBM if pin else jax.ShapeDtypeStruct
@@ -302,13 +323,13 @@
     shapes = [kind((rows, step), F32)] * (len(groups) if final else 0)
     shapes += [pltpu.HBM((rows, stop - start), F32) for start, stop in split_out]
     shapes.append(pltpu.HBM((rows, len(groups) * step), F32))
-    plan = (tuple(pieces), len(arrays), extra, final, split_out, units, groups)
+    plan = (tuple(pieces), len(arrays), extra, final, split_out, units, groups, None if begun is None else begun[0])
     work = 3 * 2 * rows * columns * (depth + 4 * width)
     moved = 4 * (depth + 3 * rows) * columns + npairs * 2 * 2 * 8 * width * width
     size = 4 * columns * (depth + (1 + nouts) * rows) + 4 * rows * columns + npairs * 2 * 2 * 8 * width * width
     result = pl.pallas_call(
         functools.partial(blur_kernel, plan),
-        in_specs=[INSMEM] + [ANY] * len(arrays) + [INVMEM, ANY, ANY, ANY] + [INSMEM] * final,
+        in_specs=[INSMEM] + [ANY] * len(arrays) + [INVMEM, ANY, ANY, ANY] + [ANY] * (begun is not None) + [INSMEM] * final,
         out_specs=[ANY] * len(shapes),
         out_shape=shapes,
         scratch_shapes=[
@@ -319,17 +340,63 @@
             pltpu.VMEM((npairs, 2 * width, 4 * width), BF16),
             pltpu.VMEM((rows, columns), F32),
         ]
-        + [pltpu.VMEM((rows, columns), F32)] * nouts
+        + [pltpu.VMEM((rows, columns), F32)] * (nouts + (begun is not None))
         + [
-            pltpu.SemaphoreType.DMA((len(units), len(pieces))),
+            pltpu.SemaphoreType.DMA((len(units), len(pieces) + (begun is not None))),
             pltpu.SemaphoreType.DMA((GROUPS, 3)),
             pltpu.SemaphoreType.DMA((GROUPS + 1, 2)),
         ],
         compiler_params=params(size // 2**20 + 6),
         cost_estimate=pl.CostEstimate(flops=work // 64, bytes_accessed=moved // 64, transcendentals=0),
         name=name,
-    )(side, *arrays, bands, *hbm(*weights, other), *(hbm(map_weights) if final else []))
+    )(side, *arrays, bands, *hbm(*weights, other), *(hbm(begun[1]) if begun else []), *(hbm(map_weights) if final else []))
     return (result[:-1], result[-1]) if final else result if split_out else result[0]
+
+
+def begin_kernel(beside_row, start, side_ref, own_ref, beside_ref, band_ref, out_ref, field, a_both, result, sems):
+    width, columns = result.shape
+    side = side_ref[0]
+    at = pl.ds(start, columns)
+    copies = [
+        pltpu.make_async_copy(area(own_ref, 0, width, at), field.at[pl.ds(pick((width, 0), side), width)], sems.at[0]),
+        pltpu.make_async_copy(
+            area(beside_ref, pick(beside_row, side), width, at),
+            field.at[pl.ds(pick((0, width), side), width)],
+            sems.at[1],
+        ),
+    ]
+    for copy in copies:
+        copy.start()
+    for j in range(2):
+        for part, value in enumerate(split(jnp.where(side == 0, band_ref[0, j], band_ref[0, j + 1]))):
+            a_both[part * width : (part + 1) * width, j * width : (j + 1) * width] = value
+    for copy in copies:
+        copy.wait()
+    for i in range(columns // (2 * width)):
+        tile = slice(i * 2 * width, (i + 1) * 2 * width)
+        result[:, tile] = dot3(a_both[...], split(field[:, tile]), ((1,), (0,)))
+    copy = pltpu.make_async_copy(result, out_ref, sems.at[2])
+    copy.start()
+    copy.wait()
+
+
+def begin(name, side, own, beside, beside_row, bands, start):
+    width, columns = own.shape[0], own.shape[1] - start
+    return pl.pallas_call(
+        functools.partial(begin_kernel, beside_row, start),
+        in_specs=[INSMEM, ANY, ANY, INVMEM],
+        out_specs=ANY,
+        out_shape=pltpu.HBM((width, columns), F32),
+        scratch_shapes=[
+            pltpu.VMEM((2 * width, columns), F32),
+            pltpu.VMEM((2 * width, 2 * width), BF16),
+            pltpu.VMEM((width, columns), F32),
+            pltpu.SemaphoreType.DMA((3,)),
+        ],
+        compiler_params=params(12),
+        cost_estimate=pl.CostEstimate(flops=width * columns, bytes_accessed=width * columns, transcendentals=0),
+        name=name,
+    )(side, *hbm(own, beside), bands)
 
 
 def raw_kernel(fresh, first, side_ref, *refs):
@@ -635,9 +702,8 @@
         raw, quotient, mass = state
         step = cols_all // GROUPS
         first_units = tuple((g * step, (g + 1) * step) for g in range(GROUPS // 2)) + ((half, half + more),)
-        later_units = ((half - more, half + more), (half + more, half + step)) + tuple(
-            (g * step, (g + 1) * step) for g in range(GROUPS // 2 + 1, GROUPS)
-        )
+        later_units = ((half - more, half + more), (half + more, half + step + more), (half + step + more, cols_all))
+        begun = begin("begin_near", side, ratio_near, beside, beside_row[::-1], near_bands, half - more)
         plans = [
             ("near_first", first_units, 0, [(2, start) for start, _ in first_units]),
             ("near_later", later_units, half, [(2, half - more)] + [(3, a - half - more) for a, _ in later_units[1:]]),
@@ -649,10 +715,12 @@
                 (1, beside_row[::-1], width, (0, 2 * width)),
                 (tuple(halo), 0, width, (2 * width, 0)),
             ]
+            if part == 1:
+                pieces = [(tuple(halo), 0, width, 0)]
             groups = tuple(g for g in range(GROUPS) if column <= g * step < column + half)
             t, m = blur(
                 "logs_" + name, side, arrays, pieces, near_bands, wts, scaling, near_row, weights,
-                pin=False, units=units, groups=groups,
+                pin=False, units=units, groups=groups, begun=(half - more, begun) if part == 1 else None,
             )
             raw, mass = raw_only("raw_" + name, side, near_row, column, t, [swap(part) for part in t], raw, mass)
             quotient = quotient_part("quotient_" + name, side, near_row, column, raw, m, quotient)

time: 218 us -> 218 us (level)
  waiting for transfers between devices: 44.8 us -> 40.9 us
  Pallas kernels: 109 us -> 112 us
    pallas_call x0 -> x1, Pallas kernels: none -> 3.91 us  [begin(): pl.pallas_call(functools.partial(begin_kernel, beside_row, start), in_spe...]
  transfers between devices with their start and end apart: 26 -> 26, of which waited for: 12 -> 10; matrix products, arithmetic and copies ran while one was open for 1% -> 1% of each run, Pallas kernels for 42% -> 44%
where the time goes in v2:
time: 218 us; the launch traced here: 217 us
  Pallas kernels  112 us (51%)
  starting transfers between devices  60.4 us (28%)
  waiting for transfers between devices  40.9 us (19%)
  local copies, waits for them, and re-layouts  2.26 us (1%)
    pallas_call x7, Pallas kernels, blur(): pl.pallas_call(functools.partial(blur_kernel, plan), in_specs=[INSMEM] +...  62.3 us
    ppermute x6, waiting for transfers between devices, send(): return lax.ppermute(part, 'space', pairs)  20.8 us
    ppermute x6, starting transfers between devices, send(): return lax.ppermute(part, 'space', pairs)  16.9 us
    ppermute x2, starting transfers between devices, local(): near2 = [near(part) for part in parts]  16.4 us
    ppermute x2, starting transfers between devices, local(): near(part)  14.5 us
    pallas_call x2, Pallas kernels, raw_rows(): pl.pallas_call(functools.partial(raw_kernel, fresh, row), grid_spec=pltpu...  13.8 us
    ppermute x2, waiting for transfers between devices, local(): near2 = [near(part) for part in parts]  11.9 us
    pallas_call x1, Pallas kernels, row_weights(): pl.pallas_call(functools.partial(weight_kernel, nblocks), grid=(nblocks /...  11.6 us
  transfers between devices with their start and end apart: 26, of which 10 were waited for; matrix products, arithmetic and copies ran while one was open for 1% of the time, Pallas kernels for 44%

profile of v2, /device:TPU:0, one launch (start us, length us, event | category | flops | bytes accessed | tf_op | source)
XLA Modules:
  0.0 216.7 jit_solution(17596136700597914068)
XLA Ops:
  0.7 3.4 %cut_cross.1 = (f32[128,1,2048]{2,1,0:T(1,128)}, f32[128,1,1024]{2,1,0:T(1,128)}, f32[128,1,2048]{2,1,0:T(1,128)}, f32[128,1,1024]{2,1,0:T(1,128)}) custom-call(s32[4]{0:T(128)S(1)} %pad_add_fusion.side_ref.refs_0_, f32[512,1,4096]{2,1,0:T(1,128)} %refs_8_.5), custom_call_target="tpu_custom_call" | custom-call | tf_op jit(solution)/shard_map/cut_cross/pallas_call | solution.py:72
  8.2 3.1 %cut_near.1 = (f32[128,1,3072]{2,1,0:T(1,128)}, f32[128,1,1024]{2,1,0:T(1,128)}) custom-call(s32[4]{0:T(128)S(1)} %pad_add_fusion.side_ref.refs_0_, f32[512,1,4096]{2,1,0:T(1,128)} %refs_8_.5), custom_call_target="tpu_custom_call" | custom-call | tf_op jit(solution)/shard_map/cut_near/pallas_call | solution.py:72
  11.2 14.5 %collective-permute-start.6 = (f32[128,1,3072]{2,1,0:T(1,128)}, f32[128,1,3072]{2,1,0:T(1,128)S(1)}, u32[]{:S(2)}, u32[]{:S(2)}) collective-permute-start(f32[128,1,3072]{2,1,0:T(1,128)} %get-tuple-element.81), channel_id=1, source_target_pairs={{0,2},{4,6},{8,10},{12,14},{2,0},{6,4},{10,8},{14,12},{1,3},{5,7},... | collective-permute-start | bytes 4718600 | tf_op jit(solution)/shard_map/ppermute | solution.py:638
  25.7 18.2 %collective-permute-done.1 = f32[128,1,1024]{2,1,0:T(1,128)} collective-permute-done((f32[128,1,1024]{2,1,0:T(1,128)}, f32[128,1,1024]{2,1,0:T(1,128)}, u32[]{:S(2)}, u32[]{:S(2)}) %collective-permute-start.1) | collective-permute-done | bytes 524320 | tf_op jit(solution)/shard_map/ppermute | solution.py:104
  43.9 7.6 %collective-permute-start.4 = (f32[128,1,2048]{2,1,0:T(1,128)}, f32[128,1,2048]{2,1,0:T(1,128)}, u32[]{:S(2)}, u32[]{:S(2)}) collective-permute-start(f32[128,1,2048]{2,1,0:T(1,128)} %collective-permute-done), channel_id=1, source_target_pairs={{0,4},{4,8},{10,6},{14,10},{1,5},{5,9},{11,7},{15,11},{16,20},{20,... | collective-permute-start | bytes 3145736 | tf_op jit(solution)/shard_map/ppermute | solution.py:104
  51.6 5.3 %collective-permute-start.5 = (f32[128,1,1024]{2,1,0:T(1,128)}, f32[128,1,1024]{2,1,0:T(1,128)}, u32[]{:S(2)}, u32[]{:S(2)}) collective-permute-start(f32[128,1,1024]{2,1,0:T(1,128)} %collective-permute-done.1), channel_id=1, source_target_pairs={{0,4},{6,2},{8,12},{14,10},{1,5},{7,3},{9,13},{15,11},{16,20},{22,... | collective-permute-start | bytes 1572872 | tf_op jit(solution)/shard_map/ppermute | solution.py:104
  56.9 11.6 %row_weights.1 = (bf16[16,256,512]{2,1,0:T(8,128)(2,1)}, bf16[16,256,512]{2,1,0:T(8,128)(2,1)}) custom-call(f32[32,3,128,128]{3,2,1,0:T(8,128)} %band_ref.1), custom_call_target="tpu_custom_call" | custom-call | tf_op jit(solution)/shard_map/row_weights/pallas_call | solution.py:149
  69.5 11.4 %ratio_inner.1.beside_ref.refs_1_.refs_2_ = f32[256,4096]{1,0:T(8,128)} custom-call(s32[4]{0:T(128)S(1)} %pad_add_fusion.side_ref.refs_0_, f32[512,1,4096]{2,1,0:T(1,128)} %refs_8_.5, f32[2,3,128,128]{3,2,1,0:T(8,128)S(1)} %constant_dynamic-slice_fusion.2.refs_2_.refs_4_, bf16[16,256,512]{2,1,0:T(8,128)(2,1)} %get-tuple-element.75.refs_3_.refs_7_.refs_5_.refs_6_, ...), custom_call_target="tpu_custom_call" | custom-call | flops 100663296 | bytes 458752 | tf_op jit(solution)/shard_map/ratio_inner/pallas_call | solution.py:330
  84.6 8.7 %ratio_cross.1.refs_2_.refs_1_ = f32[128,4096]{1,0:T(8,128)} custom-call(s32[4]{0:T(128)S(1)} %pad_add_fusion.side_ref.refs_0_, f32[512,1,4096]{2,1,0:T(1,128)} %refs_8_.5, f32[128,1,2048]{2,1,0:T(1,128)} %collective-permute-done.4.refs_2_, f32[128,1,1024]{2,1,0:T(1,128)} %collective-permute-done.5.refs_3_, f32[128,1,2048]{2,1,0:T(1,128)} %copy-done.1, ...), custom_call_target="tpu_custom_call" | custom-call | flops 44040192 | bytes 327680 | tf_op jit(solution)/shard_map/ratio_cross/pallas_call | solution.py:330
  94.5 9.0 %ratio_near.1 = (f32[128,2304]{1,0:T(8,128)}, f32[128,1792]{1,0:T(8,128)}, f32[128,4096]{1,0:T(8,128)}) custom-call(s32[4]{0:T(128)S(1)} %pad_add_fusion.side_ref.refs_0_, f32[512,1,4096]{2,1,0:T(1,128)} %refs_8_.5, f32[128,1,3072]{2,1,0:T(1,128)} %copy-done, f32[128,1,1024]{2,1,0:T(1,128)} %collective-permute-done.7.refs_3_, ...), custom_call_target="tpu_custom_call" | custom-call | flops 44040192 | bytes 327680 | tf_op jit(solution)/shard_map/ratio_near/pallas_call | solution.py:330
  103.6 12.4 %logs_inner.1 = (f32[256,1024]{1,0:T(8,128)}, f32[256,1024]{1,0:T(8,128)}, f32[256,1024]{1,0:T(8,128)}, f32[256,1024]{1,0:T(8,128)}, f32[256,4096]{1,0:T(8,128)}) custom-call(s32[4]{0:T(128)S(1)} %pad_add_fusion.side_ref.refs_0_, f32[256,4096]{1,0:T(8,128)} %ratio_inner.1.beside_ref.refs_1_.refs_2_, f32[128,4096]{1,0:T(8,128)} %ratio_cross.1.refs_2_.refs_1_, ...), custom_call_target="tpu_custom_call" | custom-call | flops 100663296 | bytes 458752 | tf_op jit(solution)/shard_map/logs_inner/pallas_call | solution.py:330
  118.9 4.9 %collective-permute-start.8 = (f32[128,2304]{1,0:T(8,128)S(1)}, f32[128,2304]{1,0:T(8,128)S(1)}, u32[]{:S(2)}, u32[]{:S(2)}) collective-permute-start(f32[128,2304]{1,0:T(8,128)S(1)} %copy-done.3), channel_id=1, source_target_pairs={{0,2},{4,6},{8,10},{12,14},{2,0},{6,4},{10,8},{14,12},{1,3},{5,7},... | collective-permute-start | bytes 3538952 | tf_op jit(solution)/shard_map/ppermute | solution.py:676
  123.9 8.8 %raw_inner.1 = (f32[512,4096]{1,0:T(8,128)S(1)}, f32[512,1,4096]{2,1,0:T(1,128)S(1)}, f32[1,128]{1,0:T(1,128)S(1)}) custom-call(s32[4]{0:T(128)S(1)} %pad_add_fusion.side_ref.refs_0_, f32[256,1024]{1,0:T(8,128)} %get-tuple-element.90.refs_0_, f32[256,1024]{1,0:T(8,128)} %get-tuple-element.91.refs_1_, f32[256,1024]{1,0:T(8,128)} %get-tuple-element.92.refs_2_, ...), custom_call_target="tpu_custom_call" | custom-call | flops 65536 | bytes 262144 | tf_op jit(solution)/shard_map/raw_inner/pallas_call | solution.py:441
  132.7 8.9 %logs_cross.1 = (f32[128,1024]{1,0:T(8,128)}, f32[128,1024]{1,0:T(8,128)}, f32[128,1024]{1,0:T(8,128)}, f32[128,1024]{1,0:T(8,128)}, f32[128,4096]{1,0:T(8,128)}) custom-call(s32[4]{0:T(128)S(1)} %pad_add_fusion.side_ref.refs_0_, f32[128,4096]{1,0:T(8,128)} %ratio_cross.1.refs_2_.refs_1_, f32[256,4096]{1,0:T(8,128)} %ratio_inner.1.beside_ref.refs_1_.refs_2_, ...), custom_call_target="tpu_custom_call" | custom-call | flops 44040192 | bytes 327680 | tf_op jit(solution)/shard_map/logs_cross/pallas_call | solution.py:330
  143.8 11.5 %collective-permute-start.9 = (f32[128,1792]{1,0:T(8,128)S(1)}, f32[128,1792]{1,0:T(8,128)S(1)}, u32[]{:S(2)}, u32[]{:S(2)}) collective-permute-start(f32[128,1792]{1,0:T(8,128)S(1)} %copy-done.4), channel_id=1, source_target_pairs={{0,2},{4,6},{8,10},{12,14},{2,0},{6,4},{10,8},{14,12},{1,3},{5,7},... | collective-permute-start | bytes 2752520 | tf_op jit(solution)/shard_map/ppermute | solution.py:676
  155.4 4.9 %raw_cross.1 = (f32[512,4096]{1,0:T(8,128)S(1)}, f32[512,1,4096]{2,1,0:T(1,128)S(1)}, f32[1,128]{1,0:T(1,128)S(1)}) custom-call(s32[4]{0:T(128)S(1)} %pad_add_fusion.side_ref.refs_0_, f32[128,1024]{1,0:T(8,128)} %get-tuple-element.99.refs_0_, f32[128,1024]{1,0:T(8,128)} %get-tuple-element.100.refs_1_, ...), custom_call_target="tpu_custom_call", output_to_operand_aliasing={{0}: (10, {}), {1}: (11, {})} | custom-call | flops 32768 | bytes 131072 | tf_op jit(solution)/shard_map/raw_cross/pallas_call | solution.py:441
  160.3 6.8 %collective-permute-done.8.refs_3_ = f32[128,2304]{1,0:T(8,128)S(1)} collective-permute-done((f32[128,2304]{1,0:T(8,128)S(1)}, f32[128,2304]{1,0:T(8,128)S(1)}, u32[]{:S(2)}, u32[]{:S(2)}) %collective-permute-start.8) | collective-permute-done | bytes 1179680 | tf_op jit(solution)/shard_map/ppermute | solution.py:676
  167.2 6.2 %logs_near_first.1 = (f32[128,1024]{1,0:T(8,128)S(1)}, f32[128,1024]{1,0:T(8,128)S(1)}, f32[128,2048]{1,0:T(8,128)}) custom-call(s32[4]{0:T(128)S(1)} %pad_add_fusion.side_ref.refs_0_, f32[128,4096]{1,0:T(8,128)} %get-tuple-element.85.own_ref.refs_3_.refs_1_, f32[256,4096]{1,0:T(8,128)} %ratio_inner.1.beside_ref.refs_1_.refs_2_, ...), custom_call_target="tpu_custom_call" | custom-call | flops 44040192 | bytes 327680 | tf_op jit(solution)/shard_map/logs_near_first/pallas_call | solution.py:330
  173.9 3.9 %begin_near.1.refs_9_ = f32[128,2304]{1,0:T(8,128)} custom-call(s32[4]{0:T(128)S(1)} %pad_add_fusion.side_ref.refs_0_, f32[128,4096]{1,0:T(8,128)} %get-tuple-element.85.own_ref.refs_3_.refs_1_, f32[256,4096]{1,0:T(8,128)} %ratio_inner.1.beside_ref.refs_1_.refs_2_, f32[1,3,128,128]{3,2,1,0:T(8,128)S(1)} %get-tuple-element.134.refs_4_.band_ref.refs_5_), custom_call_target="tpu_custom_call" | custom-call | flops 294912 | bytes 294912 | tf_op jit(solution)/shard_map/begin_near/pallas_call | solution.py:385
  179.1 2.6 %quotient_near_first.1._ = f32[512,1,4096]{2,1,0:T(1,128)S(1)} custom-call(s32[4]{0:T(128)S(1)} %pad_add_fusion.side_ref.refs_0_, f32[512,4096]{1,0:T(8,128)S(1)} %get-tuple-element.122.raw_ref.refs_4_, f32[128,2048]{1,0:T(8,128)} %get-tuple-element.117.m_ref, f32[512,1,4096]{2,1,0:T(1,128)S(1)} %get-tuple-element.118._), custom_call_target="tpu_custom_call", output_to_operand_aliasing={{}: (3, {})} | custom-call | flops 16384 | bytes 65536 | tf_op jit(solution)/shard_map/quotient_near_first/pallas_call | solution.py:527
  181.7 5.1 %collective-permute-done.9.refs_4_ = f32[128,1792]{1,0:T(8,128)S(1)} collective-permute-done((f32[128,1792]{1,0:T(8,128)S(1)}, f32[128,1792]{1,0:T(8,128)S(1)}, u32[]{:S(2)}, u32[]{:S(2)}) %collective-permute-start.9) | collective-permute-done | bytes 917536 | tf_op jit(solution)/shard_map/ppermute | solution.py:676
  186.8 5.6 %logs_near_later.1 = (f32[128,1024]{1,0:T(8,128)S(1)}, f32[128,1024]{1,0:T(8,128)S(1)}, f32[128,2048]{1,0:T(8,128)}) custom-call(s32[4]{0:T(128)S(1)} %pad_add_fusion.side_ref.refs_0_, f32[128,4096]{1,0:T(8,128)} %get-tuple-element.85.own_ref.refs_3_.refs_1_, f32[256,4096]{1,0:T(8,128)} %ratio_inner.1.beside_ref.refs_1_.refs_2_, ...), custom_call_target="tpu_custom_call" | custom-call | flops 31457280 | bytes 262144 | tf_op jit(solution)/shard_map/logs_near_later/pallas_call | solution.py:330
  205.3 3.4 %collective-permute-start.25 = (f32[1,128]{1,0:T(1,128)S(1)}, f32[1,128]{1,0:T(1,128)S(1)}, u32[]{:S(2)}, u32[]{:S(2)}) collective-permute-start(f32[1,128]{1,0:T(1,128)S(1)} %mass.3.refs_0_), channel_id=1, source_target_pairs={{0,8},{2,10},{4,12},{6,14},{8,0},{10,2},{12,4},{14,6},{1,9},{3,11}... | collective-permute-start | bytes 1544 | tf_op jit(solution)/shard_map/ppermute | solution.py:574
  210.3 6.4 %outputs.1 = (f32[512,4096]{1,0:T(8,128)}, f32[512,32,128]{2,1,0:T(8,128)}) custom-call(f32[512,4096]{1,0:T(8,128)S(1)} %get-tuple-element.124.raw_ref, f32[512,32,128]{2,1,0:T(8,128)S(1)} %bitcast.6, f32[1,128]{1,0:T(1,128)S(1)} %mass.3.refs_0_, f32[1,128]{1,0:T(1,128)S(1)} %collective-permute-done.25.refs_1_), custom_call_target="tpu_custom_call" | custom-call | tf_op jit(solution)/shard_map/outputs/pallas_call | solution.py:596
  (61 shorter events, 31.2 us)
Async XLA Ops:
  4.1 39.8 %collective-permute-start = (f32[128,1,2048]{2,1,0:T(1,128)}, f32[128,1,2048]{2,1,0:T(1,128)}, u32[]{:S(2)}, u32[]{:S(2)}) collective-permute-start(f32[128,1,2048]{2,1,0:T(1,128)} %get-tuple-element.67), channel_id=1, source_target_pairs={{2,0},{6,4},{8,10},{12,14},{3,1},{7,5},{9,11},{13,15},{18,16},{22,... | collective-permute-start | bytes 3145736 | tf_op jit(solution)/shard_map/ppermute | solution.py:104
  5.4 38.5 %collective-permute-start.2 = (f32[128,1,2048]{2,1,0:T(1,128)}, f32[128,1,2048]{2,1,0:T(1,128)S(1)}, u32[]{:S(2)}, u32[]{:S(2)}) collective-permute-start(f32[128,1,2048]{2,1,0:T(1,128)} %get-tuple-element.69), channel_id=1, source_target_pairs={{4,2},{6,8},{8,6},{10,12},{5,3},{7,9},{9,7},{11,13},{20,18},{22,24... | collective-permute-start | bytes 3145736 | tf_op jit(solution)/shard_map/ppermute | solution.py:104
  6.2 37.7 %collective-permute-start.1 = (f32[128,1,1024]{2,1,0:T(1,128)}, f32[128,1,1024]{2,1,0:T(1,128)}, u32[]{:S(2)}, u32[]{:S(2)}) collective-permute-start(f32[128,1,1024]{2,1,0:T(1,128)} %get-tuple-element.68), channel_id=1, source_target_pairs={{2,0},{4,6},{10,8},{12,14},{3,1},{5,7},{11,9},{13,15},{18,16},{20,... | collective-permute-start | bytes 1572872 | tf_op jit(solution)/shard_map/ppermute | solution.py:104
  7.5 36.4 %collective-permute-start.3 = (f32[128,1,1024]{2,1,0:T(1,128)}, f32[128,1,1024]{2,1,0:T(1,128)S(1)}, u32[]{:S(2)}, u32[]{:S(2)}) collective-permute-start(f32[128,1,1024]{2,1,0:T(1,128)} %get-tuple-element.70), channel_id=1, source_target_pairs={{2,4},{4,2},{10,12},{12,10},{3,5},{5,3},{11,13},{13,11},{18,20},{2... | collective-permute-start | bytes 1572872 | tf_op jit(solution)/shard_map/ppermute | solution.py:104
  11.2 82.1 %collective-permute-start.6 = (f32[128,1,3072]{2,1,0:T(1,128)}, f32[128,1,3072]{2,1,0:T(1,128)S(1)}, u32[]{:S(2)}, u32[]{:S(2)}) collective-permute-start(f32[128,1,3072]{2,1,0:T(1,128)} %get-tuple-element.81), channel_id=1, source_target_pairs={{0,2},{4,6},{8,10},{12,14},{2,0},{6,4},{10,8},{14,12},{1,3},{5,7},... | collective-permute-start | bytes 4718600 | tf_op jit(solution)/shard_map/ppermute | solution.py:638
  43.9 40.7 %collective-permute-start.4 = (f32[128,1,2048]{2,1,0:T(1,128)}, f32[128,1,2048]{2,1,0:T(1,128)}, u32[]{:S(2)}, u32[]{:S(2)}) collective-permute-start(f32[128,1,2048]{2,1,0:T(1,128)} %collective-permute-done), channel_id=1, source_target_pairs={{0,4},{4,8},{10,6},{14,10},{1,5},{5,9},{11,7},{15,11},{16,20},{20,... | collective-permute-start | bytes 3145736 | tf_op jit(solution)/shard_map/ppermute | solution.py:104
  51.6 33.0 %collective-permute-start.5 = (f32[128,1,1024]{2,1,0:T(1,128)}, f32[128,1,1024]{2,1,0:T(1,128)}, u32[]{:S(2)}, u32[]{:S(2)}) collective-permute-start(f32[128,1,1024]{2,1,0:T(1,128)} %collective-permute-done.1), channel_id=1, source_target_pairs={{0,4},{6,2},{8,12},{14,10},{1,5},{7,3},{9,13},{15,11},{16,20},{22,... | collective-permute-start | bytes 1572872 | tf_op jit(solution)/shard_map/ppermute | solution.py:104
  56.9 36.5 %collective-permute-start.7 = (f32[128,1,1024]{2,1,0:T(1,128)}, f32[128,1,1024]{2,1,0:T(1,128)}, u32[]{:S(2)}, u32[]{:S(2)}) collective-permute-start(f32[128,1,1024]{2,1,0:T(1,128)} %get-tuple-element.82), channel_id=1, source_target_pairs={{0,2},{4,6},{8,10},{12,14},{2,0},{6,4},{10,8},{14,12},{1,3},{5,7},... | collective-permute-start | bytes 1572872 | tf_op jit(solution)/shard_map/ppermute | solution.py:638
  93.4 39.3 %collective-permute-start.14 = (f32[128,4096]{1,0:T(8,128)}, f32[128,4096]{1,0:T(8,128)S(1)}, u32[]{:S(2)}, u32[]{:S(2)}) collective-permute-start(f32[128,4096]{1,0:T(8,128)} %ratio_cross.1.refs_2_.refs_1_), channel_id=1, source_target_pairs={{2,4},{6,8},{10,12},{4,2},{8,6},{12,10},{3,5},{7,9},{11,13},{5,3},... | collective-permute-start | bytes 6291464 | tf_op jit(solution)/shard_map/ppermute | solution.py:668
  116.0 2.9 %collective-permute-start.10 = (f32[256,1024]{1,0:T(8,128)}, f32[256,1024]{1,0:T(8,128)S(1)}, u32[]{:S(2)}, u32[]{:S(2)}) collective-permute-start(f32[256,1024]{1,0:T(8,128)} %get-tuple-element.90.refs_0_), channel_id=1, source_target_pairs={{0,1},{1,0},{2,3},{3,2},{4,5},{5,4},{6,7},{7,6},{8,9},{9,8},{10,11... | collective-permute-start | bytes 3145736 | tf_op jit(solution)/shard_map/ppermute | solution.py:681
  116.1 7.8 %collective-permute-start.11 = (f32[256,1024]{1,0:T(8,128)}, f32[256,1024]{1,0:T(8,128)S(1)}, u32[]{:S(2)}, u32[]{:S(2)}) collective-permute-start(f32[256,1024]{1,0:T(8,128)} %get-tuple-element.91.refs_1_), channel_id=1, source_target_pairs={{0,1},{1,0},{2,3},{3,2},{4,5},{5,4},{6,7},{7,6},{8,9},{9,8},{10,11... | collective-permute-start | bytes 3145736 | tf_op jit(solution)/shard_map/ppermute | solution.py:681
  116.6 7.3 %collective-permute-start.12 = (f32[256,1024]{1,0:T(8,128)}, f32[256,1024]{1,0:T(8,128)S(1)}, u32[]{:S(2)}, u32[]{:S(2)}) collective-permute-start(f32[256,1024]{1,0:T(8,128)} %get-tuple-element.92.refs_2_), channel_id=1, source_target_pairs={{0,1},{1,0},{2,3},{3,2},{4,5},{5,4},{6,7},{7,6},{8,9},{9,8},{10,11... | collective-permute-start | bytes 3145736 | tf_op jit(solution)/shard_map/ppermute | solution.py:681
  116.7 7.2 %collective-permute-start.13 = (f32[256,1024]{1,0:T(8,128)}, f32[256,1024]{1,0:T(8,128)S(1)}, u32[]{:S(2)}, u32[]{:S(2)}) collective-permute-start(f32[256,1024]{1,0:T(8,128)} %get-tuple-element.93.refs_3_), channel_id=1, source_target_pairs={{0,1},{1,0},{2,3},{3,2},{4,5},{5,4},{6,7},{7,6},{8,9},{9,8},{10,11... | collective-permute-start | bytes 3145736 | tf_op jit(solution)/shard_map/ppermute | solution.py:681
  118.9 48.2 %collective-permute-start.8 = (f32[128,2304]{1,0:T(8,128)S(1)}, f32[128,2304]{1,0:T(8,128)S(1)}, u32[]{:S(2)}, u32[]{:S(2)}) collective-permute-start(f32[128,2304]{1,0:T(8,128)S(1)} %copy-done.3), channel_id=1, source_target_pairs={{0,2},{4,6},{8,10},{12,14},{2,0},{6,4},{10,8},{14,12},{1,3},{5,7},... | collective-permute-start | bytes 3538952 | tf_op jit(solution)/shard_map/ppermute | solution.py:676
  141.7 13.7 %collective-permute-start.16 = (f32[128,1024]{1,0:T(8,128)}, f32[128,1024]{1,0:T(8,128)S(1)}, u32[]{:S(2)}, u32[]{:S(2)}) collective-permute-start(f32[128,1024]{1,0:T(8,128)} %get-tuple-element.100.refs_1_), channel_id=1, source_target_pairs={{0,1},{1,0},{2,3},{3,2},{4,5},{5,4},{6,7},{7,6},{8,9},{9,8},{10,11... | collective-permute-start | bytes 1572872 | tf_op jit(solution)/shard_map/ppermute | solution.py:681
  142.2 13.2 %collective-permute-start.17 = (f32[128,1024]{1,0:T(8,128)}, f32[128,1024]{1,0:T(8,128)S(1)}, u32[]{:S(2)}, u32[]{:S(2)}) collective-permute-start(f32[128,1024]{1,0:T(8,128)} %get-tuple-element.101.refs_2_), channel_id=1, source_target_pairs={{0,1},{1,0},{2,3},{3,2},{4,5},{5,4},{6,7},{7,6},{8,9},{9,8},{10,11... | collective-permute-start | bytes 1572872 | tf_op jit(solution)/shard_map/ppermute | solution.py:681
  142.3 13.1 %collective-permute-start.18 = (f32[128,1024]{1,0:T(8,128)}, f32[128,1024]{1,0:T(8,128)S(1)}, u32[]{:S(2)}, u32[]{:S(2)}) collective-permute-start(f32[128,1024]{1,0:T(8,128)} %get-tuple-element.102.refs_3_), channel_id=1, source_target_pairs={{0,1},{1,0},{2,3},{3,2},{4,5},{5,4},{6,7},{7,6},{8,9},{9,8},{10,11... | collective-permute-start | bytes 1572872 | tf_op jit(solution)/shard_map/ppermute | solution.py:681
  143.8 42.9 %collective-permute-start.9 = (f32[128,1792]{1,0:T(8,128)S(1)}, f32[128,1792]{1,0:T(8,128)S(1)}, u32[]{:S(2)}, u32[]{:S(2)}) collective-permute-start(f32[128,1792]{1,0:T(8,128)S(1)} %copy-done.4), channel_id=1, source_target_pairs={{0,2},{4,6},{8,10},{12,14},{2,0},{6,4},{10,8},{14,12},{1,3},{5,7},... | collective-permute-start | bytes 2752520 | tf_op jit(solution)/shard_map/ppermute | solution.py:676
  173.3 4.5 %collective-permute-start.19 = (f32[128,1024]{1,0:T(8,128)S(1)}, f32[128,1024]{1,0:T(8,128)S(1)}, u32[]{:S(2)}, u32[]{:S(2)}) collective-permute-start(f32[128,1024]{1,0:T(8,128)S(1)} %get-tuple-element.111.refs_0_), channel_id=1, source_target_pairs={{0,1},{1,0},{2,3},{3,2},{4,5},{5,4},{6,7},{7,6},{8,9},{9,8},{10,11... | collective-permute-start | bytes 1572872 | tf_op jit(solution)/shard_map/ppermute | solution.py:725
  173.4 4.4 %collective-permute-start.20 = (f32[128,1024]{1,0:T(8,128)S(1)}, f32[128,1024]{1,0:T(8,128)S(1)}, u32[]{:S(2)}, u32[]{:S(2)}) collective-permute-start(f32[128,1024]{1,0:T(8,128)S(1)} %get-tuple-element.112.refs_1_), channel_id=1, source_target_pairs={{0,1},{1,0},{2,3},{3,2},{4,5},{5,4},{6,7},{7,6},{8,9},{9,8},{10,11... | collective-permute-start | bytes 1572872 | tf_op jit(solution)/shard_map/ppermute | solution.py:725
  192.5 2.6 %collective-permute-start.22 = (f32[128,1024]{1,0:T(8,128)S(1)}, f32[128,1024]{1,0:T(8,128)S(1)}, u32[]{:S(2)}, u32[]{:S(2)}) collective-permute-start(f32[128,1024]{1,0:T(8,128)S(1)} %get-tuple-element.121.refs_1_), channel_id=1, source_target_pairs={{0,1},{1,0},{2,3},{3,2},{4,5},{5,4},{6,7},{7,6},{8,9},{9,8},{10,11... | collective-permute-start | bytes 1572872 | tf_op jit(solution)/shard_map/ppermute | solution.py:725
  196.3 5.1 %collective-permute-start.23 = (f32[1,128]{1,0:T(1,128)S(1)}, f32[1,128]{1,0:T(1,128)S(1)}, u32[]{:S(2)}, u32[]{:S(2)}) collective-permute-start(f32[1,128]{1,0:T(1,128)S(1)} %get-tuple-element.125.a_ref), channel_id=1, source_target_pairs={{0,2},{2,0},{4,6},{6,4},{8,10},{10,8},{12,14},{14,12},{1,3},{3,1},... | collective-permute-start | bytes 1544 | tf_op jit(solution)/shard_map/ppermute | solution.py:574
  201.5 3.8 %collective-permute-start.24 = (f32[1,128]{1,0:T(1,128)S(1)}, f32[1,128]{1,0:T(1,128)S(1)}, u32[]{:S(2)}, u32[]{:S(2)}) collective-permute-start(f32[1,128]{1,0:T(1,128)S(1)} %mass.2.a_ref), channel_id=1, source_target_pairs={{0,4},{2,6},{4,0},{6,2},{8,12},{10,14},{12,8},{14,10},{1,5},{3,7},... | collective-permute-start | bytes 1544 | tf_op jit(solution)/shard_map/ppermute | solution.py:574
  205.3 5.0 %collective-permute-start.25 = (f32[1,128]{1,0:T(1,128)S(1)}, f32[1,128]{1,0:T(1,128)S(1)}, u32[]{:S(2)}, u32[]{:S(2)}) collective-permute-start(f32[1,128]{1,0:T(1,128)S(1)} %mass.3.refs_0_), channel_id=1, source_target_pairs={{0,8},{2,10},{4,12},{6,14},{8,0},{10,2},{12,4},{14,6},{1,9},{3,11}... | collective-permute-start | bytes 1544 | tf_op jit(solution)/shard_map/ppermute | solution.py:574
  (7 other events, 105.9 us)

commit v3 on v2

--- a/solution.py
+++ b/solution.py
@@ -157,7 +157,7 @@
 
 
 def blur_kernel(plan, *refs):
-    pieces, narrays, extra, final, split_out, units, groups, begun_at = plan
+    pieces, narrays, extra, final, split_out, units, groups, begun_at, joined = plan
     side_ref, refs = refs[0], refs[1:]
     arrays = refs[:narrays]
     band_ref, high_ref, low_ref, extra_ref = refs[narrays : narrays + 4]
@@ -171,7 +171,7 @@
             all_weights += weights_ref[k]
         row_shape = (1, 2 * band_ref.shape[2])
         share = jnp.full(row_shape, weights_ref[side_ref[3]]) / jnp.full(row_shape, all_weights)
-    nouts = len(groups) + 1 if final else 1 + len(split_out)
+    nouts = (1 if joined else len(groups)) + 1 if final else 1 + len(split_out)
     outs = rest[:nouts]
     field, a_both, y_both, whigh, wlow, other = rest[nouts : nouts + 6]
     *results, in_sems, late_sems, out_sems = rest[nouts + 6 :]
@@ -284,7 +284,10 @@
             else:
                 results[0][:, at] = other[:, at] / value
         at = pl.ds(g * step, step)
-        targets = [outs[-1].at[:, pl.ds((g - groups[0]) * step, step)]] + ([outs[groups.index(g)]] if final else [])
+        place = pl.ds((g - groups[0]) * step, step)
+        targets = [outs[-1].at[:, place]]
+        if final:
+            targets.append(outs[0].at[:, place] if joined else outs[groups.index(g)])
         copies = [
             pltpu.make_async_copy(src.at[:, at], dst, out_sems.at[g, k])
             for k, (src, dst) in enumerate(zip(results, targets))
@@ -309,7 +312,7 @@
 
 def blur(
     name, side, arrays, pieces, bands, weights, other, extra,
-    map_weights=None, pin=True, split_out=(), units=None, groups=tuple(range(GROUPS)), begun=None,
+    map_weights=None, pin=True, split_out=(), units=None, groups=tuple(range(GROUPS)), begun=None, joined=False,
 ):
     nout, _, width, _ = bands.shape
     npairs = weights[0].shape[0]
@@ -320,10 +323,11 @@
     kind = pltpu.HBM if pin else jax.ShapeDtypeStruct
     step = columns // GROUPS
     units = tuple((g * step, (g + 1) * step) for g in range(GROUPS)) if units is None else units
-    shapes = [kind((rows, step), F32)] * (len(groups) if final else 0)
+    parts = 1 if joined else len(groups)
+    shapes = [kind((rows, len(groups) // parts * step), F32)] * (parts if final else 0)
     shapes += [pltpu.HBM((rows, stop - start), F32) for start, stop in split_out]
     shapes.append(pltpu.HBM((rows, len(groups) * step), F32))
-    plan = (tuple(pieces), len(arrays), extra, final, split_out, units, groups, None if begun is None else begun[0])
+    plan = (tuple(pieces), len(arrays), extra, final, split_out, units, groups, None if begun is None else begun[0], joined)
     work = 3 * 2 * rows * columns * (depth + 4 * width)
     moved = 4 * (depth + 3 * rows) * columns + npairs * 2 * 2 * 8 * width * width
     size = 4 * columns * (depth + (1 + nouts) * rows) + 4 * rows * columns + npairs * 2 * 2 * 8 * width * width
@@ -632,7 +636,10 @@
 
     near_columns = [(0, cols_all * 3 // 4), (cols_all * 3 // 4, cols_all // 4)]
     if spread:
-        cross1 = cross_send(cut("cut_cross", side, scaling, cross_row, width, cross_parts(cols_all)))
+        parts = cross_parts(cols_all)
+        halves = cut("cut_cross_halves", side, scaling, cross_row, width, parts[0::2])
+        quarters = cut("cut_cross_quarters", side, scaling, cross_row, width, parts[1::2])
+        cross1 = cross_send([halves[0], quarters[0], halves[1], quarters[1]])
     else:
         cross1 = [cross(cut("cut_cross", side, scaling, cross_row, width, [(0, cols_all)])[0])]
     near1 = [near(part) for part in cut("cut_near", side, scaling, near_row, width, near_columns)]
@@ -720,7 +727,7 @@
             groups = tuple(g for g in range(GROUPS) if column <= g * step < column + half)
             t, m = blur(
                 "logs_" + name, side, arrays, pieces, near_bands, wts, scaling, near_row, weights,
-                pin=False, units=units, groups=groups, begun=(half - more, begun) if part == 1 else None,
+                pin=False, units=units, groups=groups, begun=(half - more, begun) if part == 1 else None, joined=part == 1,
             )
             raw, mass = raw_only("raw_" + name, side, near_row, column, t, [swap(part) for part in t], raw, mass)
             quotient = quotient_part("quotient_" + name, side, near_row, column, raw, m, quotient)

time: 218 us -> 217 us (level)
  Pallas kernels: 112 us -> 115 us
  waiting for transfers between devices: 40.9 us -> 38.4 us
    ppermute x6, waiting for transfers between devices: 20.8 us -> 17.9 us  [send(): return lax.ppermute(part, 'space', pairs)]
    pallas_call x2 -> x3, Pallas kernels: 6.46 us -> 8.95 us  [cut(): pl.pallas_call(functools.partial(cut_kernel, first, [column for column, _...]
  transfers between devices with their start and end apart: 26 -> 25, of which waited for: 10 -> 9; matrix products, arithmetic and copies ran while one was open for 1% -> 1% of each run, Pallas kernels for 44% -> 45%
where the time goes in v3:
time: 217 us; the launch traced here: 216 us
  Pallas kernels  115 us (53%)
  starting transfers between devices  60 us (28%)
  waiting for transfers between devices  38.4 us (18%)
  local copies, waits for them, and re-layouts  2.26 us (1%)
    pallas_call x7, Pallas kernels, blur(): pl.pallas_call(functools.partial(blur_kernel, plan), in_specs=[INSMEM] +...  62.3 us
    ppermute x6, waiting for transfers between devices, send(): return lax.ppermute(part, 'space', pairs)  17.9 us
    ppermute x6, starting transfers between devices, send(): return lax.ppermute(part, 'space', pairs)  16.9 us
    ppermute x2, starting transfers between devices, local(): near2 = [near(part) for part in parts]  16.5 us
    ppermute x2, starting transfers between devices, local(): near(part)  14.5 us
    pallas_call x2, Pallas kernels, raw_rows(): pl.pallas_call(functools.partial(raw_kernel, fresh, row), grid_spec=pltpu...  13.8 us
    ppermute x2, waiting for transfers between devices, local(): near2 = [near(part) for part in parts]  11.9 us
    pallas_call x1, Pallas kernels, row_weights(): pl.pallas_call(functools.partial(weight_kernel, nblocks), grid=(nblocks /...  11.6 us
  transfers between devices with their start and end apart: 25, of which 9 were waited for; matrix products, arithmetic and copies ran while one was open for 1% of the time, Pallas kernels for 45%

profile of v3, /device:TPU:0, one launch (start us, length us, event | category | flops | bytes accessed | tf_op | source)
XLA Modules:
  0.0 216.5 jit_solution(2409312113437284882)
XLA Ops:
  0.7 3.0 %cut_cross_halves.1 = (f32[128,1,2048]{2,1,0:T(1,128)}, f32[128,1,2048]{2,1,0:T(1,128)}) custom-call(s32[4]{0:T(128)S(1)} %pad_add_fusion.side_ref.refs_0_, f32[512,1,4096]{2,1,0:T(1,128)} %refs_8_.5), custom_call_target="tpu_custom_call" | custom-call | tf_op jit(solution)/shard_map/cut_cross_halves/pallas_call | solution.py:72
  5.8 2.9 %cut_cross_quarters.1 = (f32[128,1,1024]{2,1,0:T(1,128)}, f32[128,1,1024]{2,1,0:T(1,128)}) custom-call(s32[4]{0:T(128)S(1)} %pad_add_fusion.side_ref.refs_0_, f32[512,1,4096]{2,1,0:T(1,128)} %refs_8_.5), custom_call_target="tpu_custom_call" | custom-call | tf_op jit(solution)/shard_map/cut_cross_quarters/pallas_call | solution.py:72
  10.7 3.1 %cut_near.1 = (f32[128,1,3072]{2,1,0:T(1,128)}, f32[128,1,1024]{2,1,0:T(1,128)}) custom-call(s32[4]{0:T(128)S(1)} %pad_add_fusion.side_ref.refs_0_, f32[512,1,4096]{2,1,0:T(1,128)} %refs_8_.5), custom_call_target="tpu_custom_call" | custom-call | tf_op jit(solution)/shard_map/cut_near/pallas_call | solution.py:72
  13.7 14.5 %collective-permute-start.6 = (f32[128,1,3072]{2,1,0:T(1,128)}, f32[128,1,3072]{2,1,0:T(1,128)S(1)}, u32[]{:S(2)}, u32[]{:S(2)}) collective-permute-start(f32[128,1,3072]{2,1,0:T(1,128)} %get-tuple-element.80), channel_id=1, source_target_pairs={{0,2},{4,6},{8,10},{12,14},{2,0},{6,4},{10,8},{14,12},{1,3},{5,7},... | collective-permute-start | bytes 4718600 | tf_op jit(solution)/shard_map/ppermute | solution.py:645
  28.2 15.3 %collective-permute-done.1 = f32[128,1,1024]{2,1,0:T(1,128)} collective-permute-done((f32[128,1,1024]{2,1,0:T(1,128)}, f32[128,1,1024]{2,1,0:T(1,128)}, u32[]{:S(2)}, u32[]{:S(2)}) %collective-permute-start.1) | collective-permute-done | bytes 524320 | tf_op jit(solution)/shard_map/ppermute | solution.py:104
  43.5 7.6 %collective-permute-start.4 = (f32[128,1,2048]{2,1,0:T(1,128)}, f32[128,1,2048]{2,1,0:T(1,128)}, u32[]{:S(2)}, u32[]{:S(2)}) collective-permute-start(f32[128,1,2048]{2,1,0:T(1,128)} %collective-permute-done), channel_id=1, source_target_pairs={{0,4},{4,8},{10,6},{14,10},{1,5},{5,9},{11,7},{15,11},{16,20},{20,... | collective-permute-start | bytes 3145736 | tf_op jit(solution)/shard_map/ppermute | solution.py:104
  51.2 5.3 %collective-permute-start.5 = (f32[128,1,1024]{2,1,0:T(1,128)}, f32[128,1,1024]{2,1,0:T(1,128)}, u32[]{:S(2)}, u32[]{:S(2)}) collective-permute-start(f32[128,1,1024]{2,1,0:T(1,128)} %collective-permute-done.1), channel_id=1, source_target_pairs={{0,4},{6,2},{8,12},{14,10},{1,5},{7,3},{9,13},{15,11},{16,20},{22,... | collective-permute-start | bytes 1572872 | tf_op jit(solution)/shard_map/ppermute | solution.py:104
  56.5 11.6 %row_weights.1 = (bf16[16,256,512]{2,1,0:T(8,128)(2,1)}, bf16[16,256,512]{2,1,0:T(8,128)(2,1)}) custom-call(f32[32,3,128,128]{3,2,1,0:T(8,128)} %band_ref.1), custom_call_target="tpu_custom_call" | custom-call | tf_op jit(solution)/shard_map/row_weights/pallas_call | solution.py:149
  69.1 11.4 %ratio_inner.1.beside_ref.refs_1_.refs_2_ = f32[256,4096]{1,0:T(8,128)} custom-call(s32[4]{0:T(128)S(1)} %pad_add_fusion.side_ref.refs_0_, f32[512,1,4096]{2,1,0:T(1,128)} %refs_8_.5, f32[2,3,128,128]{3,2,1,0:T(8,128)S(1)} %constant_dynamic-slice_fusion.2.refs_2_.refs_4_, bf16[16,256,512]{2,1,0:T(8,128)(2,1)} %get-tuple-element.74.refs_3_.refs_7_.refs_5_.refs_6_, ...), custom_call_target="tpu_custom_call" | custom-call | flops 100663296 | bytes 458752 | tf_op jit(solution)/shard_map/ratio_inner/pallas_call | solution.py:334
  84.2 8.7 %ratio_cross.1.refs_2_.refs_1_ = f32[128,4096]{1,0:T(8,128)} custom-call(s32[4]{0:T(128)S(1)} %pad_add_fusion.side_ref.refs_0_, f32[512,1,4096]{2,1,0:T(1,128)} %refs_8_.5, f32[128,1,2048]{2,1,0:T(1,128)} %collective-permute-done.4.refs_2_, f32[128,1,1024]{2,1,0:T(1,128)} %collective-permute-done.5.refs_3_, f32[128,1,2048]{2,1,0:T(1,128)} %copy-done.1, ...), custom_call_target="tpu_custom_call" | custom-call | flops 44040192 | bytes 327680 | tf_op jit(solution)/shard_map/ratio_cross/pallas_call | solution.py:334
  94.1 9.0 %ratio_near.1 = (f32[128,2304]{1,0:T(8,128)}, f32[128,1792]{1,0:T(8,128)}, f32[128,4096]{1,0:T(8,128)}) custom-call(s32[4]{0:T(128)S(1)} %pad_add_fusion.side_ref.refs_0_, f32[512,1,4096]{2,1,0:T(1,128)} %refs_8_.5, f32[128,1,3072]{2,1,0:T(1,128)} %copy-done, f32[128,1,1024]{2,1,0:T(1,128)} %collective-permute-done.7.refs_3_, ...), custom_call_target="tpu_custom_call" | custom-call | flops 44040192 | bytes 327680 | tf_op jit(solution)/shard_map/ratio_near/pallas_call | solution.py:334
  103.2 12.4 %logs_inner.1 = (f32[256,1024]{1,0:T(8,128)}, f32[256,1024]{1,0:T(8,128)}, f32[256,1024]{1,0:T(8,128)}, f32[256,1024]{1,0:T(8,128)}, f32[256,4096]{1,0:T(8,128)}) custom-call(s32[4]{0:T(128)S(1)} %pad_add_fusion.side_ref.refs_0_, f32[256,4096]{1,0:T(8,128)} %ratio_inner.1.beside_ref.refs_1_.refs_2_, f32[128,4096]{1,0:T(8,128)} %ratio_cross.1.refs_2_.refs_1_, ...), custom_call_target="tpu_custom_call" | custom-call | flops 100663296 | bytes 458752 | tf_op jit(solution)/shard_map/logs_inner/pallas_call | solution.py:334
  118.5 4.9 %collective-permute-start.8 = (f32[128,2304]{1,0:T(8,128)S(1)}, f32[128,2304]{1,0:T(8,128)S(1)}, u32[]{:S(2)}, u32[]{:S(2)}) collective-permute-start(f32[128,2304]{1,0:T(8,128)S(1)} %copy-done.3), channel_id=1, source_target_pairs={{0,2},{4,6},{8,10},{12,14},{2,0},{6,4},{10,8},{14,12},{1,3},{5,7},... | collective-permute-start | bytes 3538952 | tf_op jit(solution)/shard_map/ppermute | solution.py:683
  123.4 8.8 %raw_inner.1 = (f32[512,4096]{1,0:T(8,128)S(1)}, f32[512,1,4096]{2,1,0:T(1,128)S(1)}, f32[1,128]{1,0:T(1,128)S(1)}) custom-call(s32[4]{0:T(128)S(1)} %pad_add_fusion.side_ref.refs_0_, f32[256,1024]{1,0:T(8,128)} %get-tuple-element.89.refs_0_, f32[256,1024]{1,0:T(8,128)} %get-tuple-element.90.refs_1_, f32[256,1024]{1,0:T(8,128)} %get-tuple-element.91.refs_2_, ...), custom_call_target="tpu_custom_call" | custom-call | flops 65536 | bytes 262144 | tf_op jit(solution)/shard_map/raw_inner/pallas_call | solution.py:445
  132.3 8.9 %logs_cross.1 = (f32[128,1024]{1,0:T(8,128)}, f32[128,1024]{1,0:T(8,128)}, f32[128,1024]{1,0:T(8,128)}, f32[128,1024]{1,0:T(8,128)}, f32[128,4096]{1,0:T(8,128)}) custom-call(s32[4]{0:T(128)S(1)} %pad_add_fusion.side_ref.refs_0_, f32[128,4096]{1,0:T(8,128)} %ratio_cross.1.refs_2_.refs_1_, f32[256,4096]{1,0:T(8,128)} %ratio_inner.1.beside_ref.refs_1_.refs_2_, ...), custom_call_target="tpu_custom_call" | custom-call | flops 44040192 | bytes 327680 | tf_op jit(solution)/shard_map/logs_cross/pallas_call | solution.py:334
  143.4 11.6 %collective-permute-start.9 = (f32[128,1792]{1,0:T(8,128)S(1)}, f32[128,1792]{1,0:T(8,128)S(1)}, u32[]{:S(2)}, u32[]{:S(2)}) collective-permute-start(f32[128,1792]{1,0:T(8,128)S(1)} %copy-done.4), channel_id=1, source_target_pairs={{0,2},{4,6},{8,10},{12,14},{2,0},{6,4},{10,8},{14,12},{1,3},{5,7},... | collective-permute-start | bytes 2752520 | tf_op jit(solution)/shard_map/ppermute | solution.py:683
  155.0 4.9 %raw_cross.1 = (f32[512,4096]{1,0:T(8,128)S(1)}, f32[512,1,4096]{2,1,0:T(1,128)S(1)}, f32[1,128]{1,0:T(1,128)S(1)}) custom-call(s32[4]{0:T(128)S(1)} %pad_add_fusion.side_ref.refs_0_, f32[128,1024]{1,0:T(8,128)} %get-tuple-element.98.refs_0_, f32[128,1024]{1,0:T(8,128)} %get-tuple-element.99.refs_1_, ...), custom_call_target="tpu_custom_call", output_to_operand_aliasing={{0}: (10, {}), {1}: (11, {})} | custom-call | flops 32768 | bytes 131072 | tf_op jit(solution)/shard_map/raw_cross/pallas_call | solution.py:445
  159.9 6.8 %collective-permute-done.8.refs_3_ = f32[128,2304]{1,0:T(8,128)S(1)} collective-permute-done((f32[128,2304]{1,0:T(8,128)S(1)}, f32[128,2304]{1,0:T(8,128)S(1)}, u32[]{:S(2)}, u32[]{:S(2)}) %collective-permute-start.8) | collective-permute-done | bytes 1179680 | tf_op jit(solution)/shard_map/ppermute | solution.py:683
  166.8 6.2 %logs_near_first.1 = (f32[128,1024]{1,0:T(8,128)S(1)}, f32[128,1024]{1,0:T(8,128)S(1)}, f32[128,2048]{1,0:T(8,128)}) custom-call(s32[4]{0:T(128)S(1)} %pad_add_fusion.side_ref.refs_0_, f32[128,4096]{1,0:T(8,128)} %get-tuple-element.84.own_ref.refs_3_.refs_1_, f32[256,4096]{1,0:T(8,128)} %ratio_inner.1.beside_ref.refs_1_.refs_2_, ...), custom_call_target="tpu_custom_call" | custom-call | flops 44040192 | bytes 327680 | tf_op jit(solution)/shard_map/logs_near_first/pallas_call | solution.py:334
  173.5 3.9 %begin_near.1.refs_9_ = f32[128,2304]{1,0:T(8,128)} custom-call(s32[4]{0:T(128)S(1)} %pad_add_fusion.side_ref.refs_0_, f32[128,4096]{1,0:T(8,128)} %get-tuple-element.84.own_ref.refs_3_.refs_1_, f32[256,4096]{1,0:T(8,128)} %ratio_inner.1.beside_ref.refs_1_.refs_2_, f32[1,3,128,128]{3,2,1,0:T(8,128)S(1)} %get-tuple-element.132.refs_4_.band_ref.refs_5_), custom_call_target="tpu_custom_call" | custom-call | flops 294912 | bytes 294912 | tf_op jit(solution)/shard_map/begin_near/pallas_call | solution.py:389
  181.3 5.1 %collective-permute-done.9.refs_4_ = f32[128,1792]{1,0:T(8,128)S(1)} collective-permute-done((f32[128,1792]{1,0:T(8,128)S(1)}, f32[128,1792]{1,0:T(8,128)S(1)}, u32[]{:S(2)}, u32[]{:S(2)}) %collective-permute-start.9) | collective-permute-done | bytes 917536 | tf_op jit(solution)/shard_map/ppermute | solution.py:683
  186.4 5.6 %logs_near_later.1 = (f32[128,2048]{1,0:T(8,128)S(1)}, f32[128,2048]{1,0:T(8,128)}) custom-call(s32[4]{0:T(128)S(1)} %pad_add_fusion.side_ref.refs_0_, f32[128,4096]{1,0:T(8,128)} %get-tuple-element.84.own_ref.refs_3_.refs_1_, f32[256,4096]{1,0:T(8,128)} %ratio_inner.1.beside_ref.refs_1_.refs_2_, f32[128,2304]{1,0:T(8,128)S(1)} %collective-permute-done.8.refs_3_, ...), custom_call_target="tpu_custom_call" | custom-call | flops 31457280 | bytes 262144 | tf_op jit(solution)/shard_map/logs_near_later/pallas_call | solution.py:334
  205.1 3.4 %collective-permute-start.24 = (f32[1,128]{1,0:T(1,128)S(1)}, f32[1,128]{1,0:T(1,128)S(1)}, u32[]{:S(2)}, u32[]{:S(2)}) collective-permute-start(f32[1,128]{1,0:T(1,128)S(1)} %mass.3.refs_0_), channel_id=1, source_target_pairs={{0,8},{2,10},{4,12},{6,14},{8,0},{10,2},{12,4},{14,6},{1,9},{3,11}... | collective-permute-start | bytes 1544 | tf_op jit(solution)/shard_map/ppermute | solution.py:578
  210.0 6.4 %outputs.1 = (f32[512,4096]{1,0:T(8,128)}, f32[512,32,128]{2,1,0:T(8,128)}) custom-call(f32[512,4096]{1,0:T(8,128)S(1)} %get-tuple-element.122.raw_ref, f32[512,32,128]{2,1,0:T(8,128)S(1)} %bitcast.6, f32[1,128]{1,0:T(1,128)S(1)} %mass.3.refs_0_, f32[1,128]{1,0:T(1,128)S(1)} %collective-permute-done.24.refs_1_), custom_call_target="tpu_custom_call" | custom-call | tf_op jit(solution)/shard_map/outputs/pallas_call | solution.py:600
  (60 shorter events, 34.0 us)
Async XLA Ops:
  3.7 39.8 %collective-permute-start = (f32[128,1,2048]{2,1,0:T(1,128)}, f32[128,1,2048]{2,1,0:T(1,128)}, u32[]{:S(2)}, u32[]{:S(2)}) collective-permute-start(f32[128,1,2048]{2,1,0:T(1,128)} %get-tuple-element.66), channel_id=1, source_target_pairs={{2,0},{6,4},{8,10},{12,14},{3,1},{7,5},{9,11},{13,15},{18,16},{22,... | collective-permute-start | bytes 3145736 | tf_op jit(solution)/shard_map/ppermute | solution.py:104
  5.0 38.5 %collective-permute-start.2 = (f32[128,1,2048]{2,1,0:T(1,128)}, f32[128,1,2048]{2,1,0:T(1,128)S(1)}, u32[]{:S(2)}, u32[]{:S(2)}) collective-permute-start(f32[128,1,2048]{2,1,0:T(1,128)} %get-tuple-element.68), channel_id=1, source_target_pairs={{4,2},{6,8},{8,6},{10,12},{5,3},{7,9},{9,7},{11,13},{20,18},{22,24... | collective-permute-start | bytes 3145736 | tf_op jit(solution)/shard_map/ppermute | solution.py:104
  8.7 34.8 %collective-permute-start.1 = (f32[128,1,1024]{2,1,0:T(1,128)}, f32[128,1,1024]{2,1,0:T(1,128)}, u32[]{:S(2)}, u32[]{:S(2)}) collective-permute-start(f32[128,1,1024]{2,1,0:T(1,128)} %get-tuple-element.67), channel_id=1, source_target_pairs={{2,0},{4,6},{10,8},{12,14},{3,1},{5,7},{11,9},{13,15},{18,16},{20,... | collective-permute-start | bytes 1572872 | tf_op jit(solution)/shard_map/ppermute | solution.py:104
  10.0 33.5 %collective-permute-start.3 = (f32[128,1,1024]{2,1,0:T(1,128)}, f32[128,1,1024]{2,1,0:T(1,128)S(1)}, u32[]{:S(2)}, u32[]{:S(2)}) collective-permute-start(f32[128,1,1024]{2,1,0:T(1,128)} %get-tuple-element.69), channel_id=1, source_target_pairs={{2,4},{4,2},{10,12},{12,10},{3,5},{5,3},{11,13},{13,11},{18,20},{2... | collective-permute-start | bytes 1572872 | tf_op jit(solution)/shard_map/ppermute | solution.py:104
  13.7 79.2 %collective-permute-start.6 = (f32[128,1,3072]{2,1,0:T(1,128)}, f32[128,1,3072]{2,1,0:T(1,128)S(1)}, u32[]{:S(2)}, u32[]{:S(2)}) collective-permute-start(f32[128,1,3072]{2,1,0:T(1,128)} %get-tuple-element.80), channel_id=1, source_target_pairs={{0,2},{4,6},{8,10},{12,14},{2,0},{6,4},{10,8},{14,12},{1,3},{5,7},... | collective-permute-start | bytes 4718600 | tf_op jit(solution)/shard_map/ppermute | solution.py:645
  43.5 40.7 %collective-permute-start.4 = (f32[128,1,2048]{2,1,0:T(1,128)}, f32[128,1,2048]{2,1,0:T(1,128)}, u32[]{:S(2)}, u32[]{:S(2)}) collective-permute-start(f32[128,1,2048]{2,1,0:T(1,128)} %collective-permute-done), channel_id=1, source_target_pairs={{0,4},{4,8},{10,6},{14,10},{1,5},{5,9},{11,7},{15,11},{16,20},{20,... | collective-permute-start | bytes 3145736 | tf_op jit(solution)/shard_map/ppermute | solution.py:104
  51.2 33.0 %collective-permute-start.5 = (f32[128,1,1024]{2,1,0:T(1,128)}, f32[128,1,1024]{2,1,0:T(1,128)}, u32[]{:S(2)}, u32[]{:S(2)}) collective-permute-start(f32[128,1,1024]{2,1,0:T(1,128)} %collective-permute-done.1), channel_id=1, source_target_pairs={{0,4},{6,2},{8,12},{14,10},{1,5},{7,3},{9,13},{15,11},{16,20},{22,... | collective-permute-start | bytes 1572872 | tf_op jit(solution)/shard_map/ppermute | solution.py:104
  56.5 36.5 %collective-permute-start.7 = (f32[128,1,1024]{2,1,0:T(1,128)}, f32[128,1,1024]{2,1,0:T(1,128)}, u32[]{:S(2)}, u32[]{:S(2)}) collective-permute-start(f32[128,1,1024]{2,1,0:T(1,128)} %get-tuple-element.81), channel_id=1, source_target_pairs={{0,2},{4,6},{8,10},{12,14},{2,0},{6,4},{10,8},{14,12},{1,3},{5,7},... | collective-permute-start | bytes 1572872 | tf_op jit(solution)/shard_map/ppermute | solution.py:645
  93.0 39.3 %collective-permute-start.14 = (f32[128,4096]{1,0:T(8,128)}, f32[128,4096]{1,0:T(8,128)S(1)}, u32[]{:S(2)}, u32[]{:S(2)}) collective-permute-start(f32[128,4096]{1,0:T(8,128)} %ratio_cross.1.refs_2_.refs_1_), channel_id=1, source_target_pairs={{2,4},{6,8},{10,12},{4,2},{8,6},{12,10},{3,5},{7,9},{11,13},{5,3},... | collective-permute-start | bytes 6291464 | tf_op jit(solution)/shard_map/ppermute | solution.py:675
  115.6 2.9 %collective-permute-start.10 = (f32[256,1024]{1,0:T(8,128)}, f32[256,1024]{1,0:T(8,128)S(1)}, u32[]{:S(2)}, u32[]{:S(2)}) collective-permute-start(f32[256,1024]{1,0:T(8,128)} %get-tuple-element.89.refs_0_), channel_id=1, source_target_pairs={{0,1},{1,0},{2,3},{3,2},{4,5},{5,4},{6,7},{7,6},{8,9},{9,8},{10,11... | collective-permute-start | bytes 3145736 | tf_op jit(solution)/shard_map/ppermute | solution.py:688
  115.7 7.8 %collective-permute-start.11 = (f32[256,1024]{1,0:T(8,128)}, f32[256,1024]{1,0:T(8,128)S(1)}, u32[]{:S(2)}, u32[]{:S(2)}) collective-permute-start(f32[256,1024]{1,0:T(8,128)} %get-tuple-element.90.refs_1_), channel_id=1, source_target_pairs={{0,1},{1,0},{2,3},{3,2},{4,5},{5,4},{6,7},{7,6},{8,9},{9,8},{10,11... | collective-permute-start | bytes 3145736 | tf_op jit(solution)/shard_map/ppermute | solution.py:688
  116.2 7.3 %collective-permute-start.12 = (f32[256,1024]{1,0:T(8,128)}, f32[256,1024]{1,0:T(8,128)S(1)}, u32[]{:S(2)}, u32[]{:S(2)}) collective-permute-start(f32[256,1024]{1,0:T(8,128)} %get-tuple-element.91.refs_2_), channel_id=1, source_target_pairs={{0,1},{1,0},{2,3},{3,2},{4,5},{5,4},{6,7},{7,6},{8,9},{9,8},{10,11... | collective-permute-start | bytes 3145736 | tf_op jit(solution)/shard_map/ppermute | solution.py:688
  116.2 7.2 %collective-permute-start.13 = (f32[256,1024]{1,0:T(8,128)}, f32[256,1024]{1,0:T(8,128)S(1)}, u32[]{:S(2)}, u32[]{:S(2)}) collective-permute-start(f32[256,1024]{1,0:T(8,128)} %get-tuple-element.92.refs_3_), channel_id=1, source_target_pairs={{0,1},{1,0},{2,3},{3,2},{4,5},{5,4},{6,7},{7,6},{8,9},{9,8},{10,11... | collective-permute-start | bytes 3145736 | tf_op jit(solution)/shard_map/ppermute | solution.py:688
  118.5 48.2 %collective-permute-start.8 = (f32[128,2304]{1,0:T(8,128)S(1)}, f32[128,2304]{1,0:T(8,128)S(1)}, u32[]{:S(2)}, u32[]{:S(2)}) collective-permute-start(f32[128,2304]{1,0:T(8,128)S(1)} %copy-done.3), channel_id=1, source_target_pairs={{0,2},{4,6},{8,10},{12,14},{2,0},{6,4},{10,8},{14,12},{1,3},{5,7},... | collective-permute-start | bytes 3538952 | tf_op jit(solution)/shard_map/ppermute | solution.py:683
  141.3 13.7 %collective-permute-start.16 = (f32[128,1024]{1,0:T(8,128)}, f32[128,1024]{1,0:T(8,128)S(1)}, u32[]{:S(2)}, u32[]{:S(2)}) collective-permute-start(f32[128,1024]{1,0:T(8,128)} %get-tuple-element.99.refs_1_), channel_id=1, source_target_pairs={{0,1},{1,0},{2,3},{3,2},{4,5},{5,4},{6,7},{7,6},{8,9},{9,8},{10,11... | collective-permute-start | bytes 1572872 | tf_op jit(solution)/shard_map/ppermute | solution.py:688
  141.8 13.2 %collective-permute-start.17 = (f32[128,1024]{1,0:T(8,128)}, f32[128,1024]{1,0:T(8,128)S(1)}, u32[]{:S(2)}, u32[]{:S(2)}) collective-permute-start(f32[128,1024]{1,0:T(8,128)} %get-tuple-element.100.refs_2_), channel_id=1, source_target_pairs={{0,1},{1,0},{2,3},{3,2},{4,5},{5,4},{6,7},{7,6},{8,9},{9,8},{10,11... | collective-permute-start | bytes 1572872 | tf_op jit(solution)/shard_map/ppermute | solution.py:688
  141.9 13.1 %collective-permute-start.18 = (f32[128,1024]{1,0:T(8,128)}, f32[128,1024]{1,0:T(8,128)S(1)}, u32[]{:S(2)}, u32[]{:S(2)}) collective-permute-start(f32[128,1024]{1,0:T(8,128)} %get-tuple-element.101.refs_3_), channel_id=1, source_target_pairs={{0,1},{1,0},{2,3},{3,2},{4,5},{5,4},{6,7},{7,6},{8,9},{9,8},{10,11... | collective-permute-start | bytes 1572872 | tf_op jit(solution)/shard_map/ppermute | solution.py:688
  143.4 42.9 %collective-permute-start.9 = (f32[128,1792]{1,0:T(8,128)S(1)}, f32[128,1792]{1,0:T(8,128)S(1)}, u32[]{:S(2)}, u32[]{:S(2)}) collective-permute-start(f32[128,1792]{1,0:T(8,128)S(1)} %copy-done.4), channel_id=1, source_target_pairs={{0,2},{4,6},{8,10},{12,14},{2,0},{6,4},{10,8},{14,12},{1,3},{5,7},... | collective-permute-start | bytes 2752520 | tf_op jit(solution)/shard_map/ppermute | solution.py:683
  172.9 4.5 %collective-permute-start.19 = (f32[128,1024]{1,0:T(8,128)S(1)}, f32[128,1024]{1,0:T(8,128)S(1)}, u32[]{:S(2)}, u32[]{:S(2)}) collective-permute-start(f32[128,1024]{1,0:T(8,128)S(1)} %get-tuple-element.110.refs_0_), channel_id=1, source_target_pairs={{0,1},{1,0},{2,3},{3,2},{4,5},{5,4},{6,7},{7,6},{8,9},{9,8},{10,11... | collective-permute-start | bytes 1572872 | tf_op jit(solution)/shard_map/ppermute | solution.py:732
  173.0 4.4 %collective-permute-start.20 = (f32[128,1024]{1,0:T(8,128)S(1)}, f32[128,1024]{1,0:T(8,128)S(1)}, u32[]{:S(2)}, u32[]{:S(2)}) collective-permute-start(f32[128,1024]{1,0:T(8,128)S(1)} %get-tuple-element.111.refs_1_), channel_id=1, source_target_pairs={{0,1},{1,0},{2,3},{3,2},{4,5},{5,4},{6,7},{7,6},{8,9},{9,8},{10,11... | collective-permute-start | bytes 1572872 | tf_op jit(solution)/shard_map/ppermute | solution.py:732
  192.0 2.7 %collective-permute-start.21 = (f32[128,2048]{1,0:T(8,128)S(1)}, f32[128,2048]{1,0:T(8,128)S(1)}, u32[]{:S(2)}, u32[]{:S(2)}) collective-permute-start(f32[128,2048]{1,0:T(8,128)S(1)} %get-tuple-element.119.refs_0_), channel_id=1, source_target_pairs={{0,1},{1,0},{2,3},{3,2},{4,5},{5,4},{6,7},{7,6},{8,9},{9,8},{10,11... | collective-permute-start | bytes 3145736 | tf_op jit(solution)/shard_map/ppermute | solution.py:732
  196.1 5.2 %collective-permute-start.22 = (f32[1,128]{1,0:T(1,128)S(1)}, f32[1,128]{1,0:T(1,128)S(1)}, u32[]{:S(2)}, u32[]{:S(2)}) collective-permute-start(f32[1,128]{1,0:T(1,128)S(1)} %get-tuple-element.123.a_ref), channel_id=1, source_target_pairs={{0,2},{2,0},{4,6},{6,4},{8,10},{10,8},{12,14},{14,12},{1,3},{3,1},... | collective-permute-start | bytes 1544 | tf_op jit(solution)/shard_map/ppermute | solution.py:578
  201.3 3.8 %collective-permute-start.23 = (f32[1,128]{1,0:T(1,128)S(1)}, f32[1,128]{1,0:T(1,128)S(1)}, u32[]{:S(2)}, u32[]{:S(2)}) collective-permute-start(f32[1,128]{1,0:T(1,128)S(1)} %mass.2.a_ref), channel_id=1, source_target_pairs={{0,4},{2,6},{4,0},{6,2},{8,12},{10,14},{12,8},{14,10},{1,5},{3,7},... | collective-permute-start | bytes 1544 | tf_op jit(solution)/shard_map/ppermute | solution.py:578
  205.1 5.0 %collective-permute-start.24 = (f32[1,128]{1,0:T(1,128)S(1)}, f32[1,128]{1,0:T(1,128)S(1)}, u32[]{:S(2)}, u32[]{:S(2)}) collective-permute-start(f32[1,128]{1,0:T(1,128)S(1)} %mass.3.refs_0_), channel_id=1, source_target_pairs={{0,8},{2,10},{4,12},{6,14},{8,0},{10,2},{12,4},{14,6},{1,9},{3,11}... | collective-permute-start | bytes 1544 | tf_op jit(solution)/shard_map/ppermute | solution.py:578
  (6 other events, 103.9 us)

commit v4 on v3

--- a/solution.py
+++ b/solution.py
@@ -106,9 +106,9 @@
     to_partner = lambda k: ((2 * k + 1, 2 * k), (2 * k + 2, 2 * k + 3))
     onward = lambda k: ((2 * k, 2 * k + 2), (2 * k + 3, 2 * k + 1))
     direct = lambda k: ((2 * k + 1, 2 * k + 2), (2 * k + 2, 2 * k + 1))
+    straight = [send(part, numbers, direct) for part, numbers in zip(parts[2:], ((1, 2), (0, 2)))]
     relayed = [send(part, numbers, to_partner) for part, numbers in zip(parts[:2], ((0, 1), (0, 2)))]
-    straight = [send(part, numbers, direct) for part, numbers in zip(parts[2:], ((1, 2), (0, 2)))]
-    a, b, c, d = lax.optimization_barrier((*relayed, *straight))
+    c, d, a, b = lax.optimization_barrier((*straight, *relayed))
     relayed, straight = [a, b], [c, d]
     passed = [send(part, numbers, onward) for part, numbers in zip(relayed, ((0, 1), (0, 2)))]
     return passed + straight

time: 217 us -> 215 us (level)
  starting transfers between devices: 60 us -> 50.5 us
  waiting for transfers between devices: 38.4 us -> 45.3 us
    ppermute x6, waiting for transfers between devices: 17.9 us -> 24.5 us  [send(): return lax.ppermute(part, 'space', pairs)]
    ppermute x2, starting transfers between devices: 14.5 us -> 9.22 us  [local(): near(part)]
    ppermute x6, starting transfers between devices: 16.9 us -> 14.2 us  [send(): return lax.ppermute(part, 'space', pairs)]
  transfers between devices with their start and end apart: 25 -> 25, of which waited for: 9 -> 9; matrix products, arithmetic and copies ran while one was open for 1% -> 1% of each run, Pallas kernels for 45% -> 46%
where the time goes in v4:
time: 215 us; the launch traced here: 214 us
  Pallas kernels  115 us (53%)
  starting transfers between devices  50.5 us (23%)
  waiting for transfers between devices  45.3 us (21%)
  local copies, waits for them, and re-layouts  2.26 us (1%)
    pallas_call x7, Pallas kernels, blur(): pl.pallas_call(functools.partial(blur_kernel, plan), in_specs=[INSMEM] +...  62.3 us
    ppermute x6, waiting for transfers between devices, send(): return lax.ppermute(part, 'space', pairs)  24.5 us
    ppermute x2, starting transfers between devices, local(): near2 = [near(part) for part in parts]  15.3 us
    ppermute x6, starting transfers between devices, send(): return lax.ppermute(part, 'space', pairs)  14.2 us
    pallas_call x2, Pallas kernels, raw_rows(): pl.pallas_call(functools.partial(raw_kernel, fresh, row), grid_spec=pltpu...  13.8 us
    ppermute x2, waiting for transfers between devices, local(): near2 = [near(part) for part in parts]  11.9 us
    pallas_call x1, Pallas kernels, row_weights(): pl.pallas_call(functools.partial(weight_kernel, nblocks), grid=(nblocks /...  11.6 us
    ppermute x2, starting transfers between devices, local(): near(part)  9.22 us
  transfers between devices with their start and end apart: 25, of which 9 were waited for; matrix products, arithmetic and copies ran while one was open for 1% of the time, Pallas kernels for 46%

profile of v4, /device:TPU:0, one launch (start us, length us, event | category | flops | bytes accessed | tf_op | source)
XLA Modules:
  0.0 213.9 jit_solution(17934688900326503427)
XLA Ops:
  0.7 3.0 %cut_cross_halves.1 = (f32[128,1,2048]{2,1,0:T(1,128)}, f32[128,1,2048]{2,1,0:T(1,128)}) custom-call(s32[4]{0:T(128)S(1)} %pad_add_fusion.side_ref.refs_0_, f32[512,1,4096]{2,1,0:T(1,128)} %refs_8_.5), custom_call_target="tpu_custom_call" | custom-call | tf_op jit(solution)/shard_map/cut_cross_halves/pallas_call | solution.py:72
  5.8 2.9 %cut_cross_quarters.1 = (f32[128,1,1024]{2,1,0:T(1,128)}, f32[128,1,1024]{2,1,0:T(1,128)}) custom-call(s32[4]{0:T(128)S(1)} %pad_add_fusion.side_ref.refs_0_, f32[512,1,4096]{2,1,0:T(1,128)} %refs_8_.5), custom_call_target="tpu_custom_call" | custom-call | tf_op jit(solution)/shard_map/cut_cross_quarters/pallas_call | solution.py:72
  10.7 3.1 %cut_near.1 = (f32[128,1,3072]{2,1,0:T(1,128)}, f32[128,1,1024]{2,1,0:T(1,128)}) custom-call(s32[4]{0:T(128)S(1)} %pad_add_fusion.side_ref.refs_0_, f32[512,1,4096]{2,1,0:T(1,128)} %refs_8_.5), custom_call_target="tpu_custom_call" | custom-call | tf_op jit(solution)/shard_map/cut_near/pallas_call | solution.py:72
  13.7 9.2 %collective-permute-start.6 = (f32[128,1,3072]{2,1,0:T(1,128)}, f32[128,1,3072]{2,1,0:T(1,128)S(1)}, u32[]{:S(2)}, u32[]{:S(2)}) collective-permute-start(f32[128,1,3072]{2,1,0:T(1,128)} %get-tuple-element.80), channel_id=1, source_target_pairs={{0,2},{4,6},{8,10},{12,14},{2,0},{6,4},{10,8},{14,12},{1,3},{5,7},... | collective-permute-start | bytes 4718600 | tf_op jit(solution)/shard_map/ppermute | solution.py:645
  22.9 21.9 %collective-permute-done.3 = f32[128,1,1024]{2,1,0:T(1,128)} collective-permute-done((f32[128,1,1024]{2,1,0:T(1,128)}, f32[128,1,1024]{2,1,0:T(1,128)}, u32[]{:S(2)}, u32[]{:S(2)}) %collective-permute-start.3) | collective-permute-done | bytes 524320 | tf_op jit(solution)/shard_map/ppermute | solution.py:104
  44.8 7.8 %collective-permute-start.4 = (f32[128,1,2048]{2,1,0:T(1,128)}, f32[128,1,2048]{2,1,0:T(1,128)}, u32[]{:S(2)}, u32[]{:S(2)}) collective-permute-start(f32[128,1,2048]{2,1,0:T(1,128)} %collective-permute-done.2), channel_id=1, source_target_pairs={{0,4},{4,8},{10,6},{14,10},{1,5},{5,9},{11,7},{15,11},{16,20},{20,... | collective-permute-start | bytes 3145736 | tf_op jit(solution)/shard_map/ppermute | solution.py:104
  55.0 11.6 %row_weights.1 = (bf16[16,256,512]{2,1,0:T(8,128)(2,1)}, bf16[16,256,512]{2,1,0:T(8,128)(2,1)}) custom-call(f32[32,3,128,128]{3,2,1,0:T(8,128)} %band_ref.1), custom_call_target="tpu_custom_call" | custom-call | tf_op jit(solution)/shard_map/row_weights/pallas_call | solution.py:149
  67.7 11.4 %ratio_inner.1.beside_ref.refs_1_.refs_2_ = f32[256,4096]{1,0:T(8,128)} custom-call(s32[4]{0:T(128)S(1)} %pad_add_fusion.side_ref.refs_0_, f32[512,1,4096]{2,1,0:T(1,128)} %refs_8_.5, f32[2,3,128,128]{3,2,1,0:T(8,128)S(1)} %constant_dynamic-slice_fusion.2.refs_2_.refs_4_, bf16[16,256,512]{2,1,0:T(8,128)(2,1)} %get-tuple-element.74.refs_3_.refs_7_.refs_5_.refs_6_, ...), custom_call_target="tpu_custom_call" | custom-call | flops 100663296 | bytes 458752 | tf_op jit(solution)/shard_map/ratio_inner/pallas_call | solution.py:334
  80.2 2.7 %collective-permute-done.5.refs_3_ = f32[128,1,1024]{2,1,0:T(1,128)} collective-permute-done((f32[128,1,1024]{2,1,0:T(1,128)}, f32[128,1,1024]{2,1,0:T(1,128)}, u32[]{:S(2)}, u32[]{:S(2)}) %collective-permute-start.5) | collective-permute-done | bytes 524320 | tf_op jit(solution)/shard_map/ppermute | solution.py:104
  82.9 8.7 %ratio_cross.1.refs_2_.refs_1_ = f32[128,4096]{1,0:T(8,128)} custom-call(s32[4]{0:T(128)S(1)} %pad_add_fusion.side_ref.refs_0_, f32[512,1,4096]{2,1,0:T(1,128)} %refs_8_.5, f32[128,1,2048]{2,1,0:T(1,128)} %collective-permute-done.4.refs_2_, f32[128,1,1024]{2,1,0:T(1,128)} %collective-permute-done.5.refs_3_, f32[128,1,2048]{2,1,0:T(1,128)} %copy-done.1, ...), custom_call_target="tpu_custom_call" | custom-call | flops 44040192 | bytes 327680 | tf_op jit(solution)/shard_map/ratio_cross/pallas_call | solution.py:334
  92.8 9.0 %ratio_near.1 = (f32[128,2304]{1,0:T(8,128)}, f32[128,1792]{1,0:T(8,128)}, f32[128,4096]{1,0:T(8,128)}) custom-call(s32[4]{0:T(128)S(1)} %pad_add_fusion.side_ref.refs_0_, f32[512,1,4096]{2,1,0:T(1,128)} %refs_8_.5, f32[128,1,3072]{2,1,0:T(1,128)} %copy-done, f32[128,1,1024]{2,1,0:T(1,128)} %collective-permute-done.7.refs_3_, ...), custom_call_target="tpu_custom_call" | custom-call | flops 44040192 | bytes 327680 | tf_op jit(solution)/shard_map/ratio_near/pallas_call | solution.py:334
  101.9 12.4 %logs_inner.1 = (f32[256,1024]{1,0:T(8,128)}, f32[256,1024]{1,0:T(8,128)}, f32[256,1024]{1,0:T(8,128)}, f32[256,1024]{1,0:T(8,128)}, f32[256,4096]{1,0:T(8,128)}) custom-call(s32[4]{0:T(128)S(1)} %pad_add_fusion.side_ref.refs_0_, f32[256,4096]{1,0:T(8,128)} %ratio_inner.1.beside_ref.refs_1_.refs_2_, f32[128,4096]{1,0:T(8,128)} %ratio_cross.1.refs_2_.refs_1_, ...), custom_call_target="tpu_custom_call" | custom-call | flops 100663296 | bytes 458752 | tf_op jit(solution)/shard_map/logs_inner/pallas_call | solution.py:334
  117.2 4.9 %collective-permute-start.8 = (f32[128,2304]{1,0:T(8,128)S(1)}, f32[128,2304]{1,0:T(8,128)S(1)}, u32[]{:S(2)}, u32[]{:S(2)}) collective-permute-start(f32[128,2304]{1,0:T(8,128)S(1)} %copy-done.3), channel_id=1, source_target_pairs={{0,2},{4,6},{8,10},{12,14},{2,0},{6,4},{10,8},{14,12},{1,3},{5,7},... | collective-permute-start | bytes 3538952 | tf_op jit(solution)/shard_map/ppermute | solution.py:683
  122.1 8.8 %raw_inner.1 = (f32[512,4096]{1,0:T(8,128)S(1)}, f32[512,1,4096]{2,1,0:T(1,128)S(1)}, f32[1,128]{1,0:T(1,128)S(1)}) custom-call(s32[4]{0:T(128)S(1)} %pad_add_fusion.side_ref.refs_0_, f32[256,1024]{1,0:T(8,128)} %get-tuple-element.89.refs_0_, f32[256,1024]{1,0:T(8,128)} %get-tuple-element.90.refs_1_, f32[256,1024]{1,0:T(8,128)} %get-tuple-element.91.refs_2_, ...), custom_call_target="tpu_custom_call" | custom-call | flops 65536 | bytes 262144 | tf_op jit(solution)/shard_map/raw_inner/pallas_call | solution.py:445
  131.0 8.9 %logs_cross.1 = (f32[128,1024]{1,0:T(8,128)}, f32[128,1024]{1,0:T(8,128)}, f32[128,1024]{1,0:T(8,128)}, f32[128,1024]{1,0:T(8,128)}, f32[128,4096]{1,0:T(8,128)}) custom-call(s32[4]{0:T(128)S(1)} %pad_add_fusion.side_ref.refs_0_, f32[128,4096]{1,0:T(8,128)} %ratio_cross.1.refs_2_.refs_1_, f32[256,4096]{1,0:T(8,128)} %ratio_inner.1.beside_ref.refs_1_.refs_2_, ...), custom_call_target="tpu_custom_call" | custom-call | flops 44040192 | bytes 327680 | tf_op jit(solution)/shard_map/logs_cross/pallas_call | solution.py:334
  142.1 10.4 %collective-permute-start.9 = (f32[128,1792]{1,0:T(8,128)S(1)}, f32[128,1792]{1,0:T(8,128)S(1)}, u32[]{:S(2)}, u32[]{:S(2)}) collective-permute-start(f32[128,1792]{1,0:T(8,128)S(1)} %copy-done.4), channel_id=1, source_target_pairs={{0,2},{4,6},{8,10},{12,14},{2,0},{6,4},{10,8},{14,12},{1,3},{5,7},... | collective-permute-start | bytes 2752520 | tf_op jit(solution)/shard_map/ppermute | solution.py:683
  152.5 4.9 %raw_cross.1 = (f32[512,4096]{1,0:T(8,128)S(1)}, f32[512,1,4096]{2,1,0:T(1,128)S(1)}, f32[1,128]{1,0:T(1,128)S(1)}) custom-call(s32[4]{0:T(128)S(1)} %pad_add_fusion.side_ref.refs_0_, f32[128,1024]{1,0:T(8,128)} %get-tuple-element.98.refs_0_, f32[128,1024]{1,0:T(8,128)} %get-tuple-element.99.refs_1_, ...), custom_call_target="tpu_custom_call", output_to_operand_aliasing={{0}: (10, {}), {1}: (11, {})} | custom-call | flops 32768 | bytes 131072 | tf_op jit(solution)/shard_map/raw_cross/pallas_call | solution.py:445
  157.5 6.8 %collective-permute-done.8.refs_3_ = f32[128,2304]{1,0:T(8,128)S(1)} collective-permute-done((f32[128,2304]{1,0:T(8,128)S(1)}, f32[128,2304]{1,0:T(8,128)S(1)}, u32[]{:S(2)}, u32[]{:S(2)}) %collective-permute-start.8) | collective-permute-done | bytes 1179680 | tf_op jit(solution)/shard_map/ppermute | solution.py:683
  164.3 6.2 %logs_near_first.1 = (f32[128,1024]{1,0:T(8,128)S(1)}, f32[128,1024]{1,0:T(8,128)S(1)}, f32[128,2048]{1,0:T(8,128)}) custom-call(s32[4]{0:T(128)S(1)} %pad_add_fusion.side_ref.refs_0_, f32[128,4096]{1,0:T(8,128)} %get-tuple-element.84.own_ref.refs_3_.refs_1_, f32[256,4096]{1,0:T(8,128)} %ratio_inner.1.beside_ref.refs_1_.refs_2_, ...), custom_call_target="tpu_custom_call" | custom-call | flops 44040192 | bytes 327680 | tf_op jit(solution)/shard_map/logs_near_first/pallas_call | solution.py:334
  171.0 3.9 %begin_near.1.refs_9_ = f32[128,2304]{1,0:T(8,128)} custom-call(s32[4]{0:T(128)S(1)} %pad_add_fusion.side_ref.refs_0_, f32[128,4096]{1,0:T(8,128)} %get-tuple-element.84.own_ref.refs_3_.refs_1_, f32[256,4096]{1,0:T(8,128)} %ratio_inner.1.beside_ref.refs_1_.refs_2_, f32[1,3,128,128]{3,2,1,0:T(8,128)S(1)} %get-tuple-element.132.refs_4_.band_ref.refs_5_), custom_call_target="tpu_custom_call" | custom-call | flops 294912 | bytes 294912 | tf_op jit(solution)/shard_map/begin_near/pallas_call | solution.py:389
  178.8 5.1 %collective-permute-done.9.refs_4_ = f32[128,1792]{1,0:T(8,128)S(1)} collective-permute-done((f32[128,1792]{1,0:T(8,128)S(1)}, f32[128,1792]{1,0:T(8,128)S(1)}, u32[]{:S(2)}, u32[]{:S(2)}) %collective-permute-start.9) | collective-permute-done | bytes 917536 | tf_op jit(solution)/shard_map/ppermute | solution.py:683
  183.9 5.6 %logs_near_later.1 = (f32[128,2048]{1,0:T(8,128)S(1)}, f32[128,2048]{1,0:T(8,128)}) custom-call(s32[4]{0:T(128)S(1)} %pad_add_fusion.side_ref.refs_0_, f32[128,4096]{1,0:T(8,128)} %get-tuple-element.84.own_ref.refs_3_.refs_1_, f32[256,4096]{1,0:T(8,128)} %ratio_inner.1.beside_ref.refs_1_.refs_2_, f32[128,2304]{1,0:T(8,128)S(1)} %collective-permute-done.8.refs_3_, ...), custom_call_target="tpu_custom_call" | custom-call | flops 31457280 | bytes 262144 | tf_op jit(solution)/shard_map/logs_near_later/pallas_call | solution.py:334
  202.4 3.5 %collective-permute-start.24 = (f32[1,128]{1,0:T(1,128)S(1)}, f32[1,128]{1,0:T(1,128)S(1)}, u32[]{:S(2)}, u32[]{:S(2)}) collective-permute-start(f32[1,128]{1,0:T(1,128)S(1)} %mass.3.refs_0_), channel_id=1, source_target_pairs={{0,8},{2,10},{4,12},{6,14},{8,0},{10,2},{12,4},{14,6},{1,9},{3,11}... | collective-permute-start | bytes 1544 | tf_op jit(solution)/shard_map/ppermute | solution.py:578
  207.5 6.4 %outputs.1 = (f32[512,4096]{1,0:T(8,128)}, f32[512,32,128]{2,1,0:T(8,128)}) custom-call(f32[512,4096]{1,0:T(8,128)S(1)} %get-tuple-element.122.raw_ref, f32[512,32,128]{2,1,0:T(8,128)S(1)} %bitcast.6, f32[1,128]{1,0:T(1,128)S(1)} %mass.3.refs_0_, f32[1,128]{1,0:T(1,128)S(1)} %collective-permute-done.24.refs_1_), custom_call_target="tpu_custom_call" | custom-call | tf_op jit(solution)/shard_map/outputs/pallas_call | solution.py:600
  (60 shorter events, 33.6 us)
Async XLA Ops:
  3.7 41.1 %collective-permute-start = (f32[128,1,2048]{2,1,0:T(1,128)}, f32[128,1,2048]{2,1,0:T(1,128)S(1)}, u32[]{:S(2)}, u32[]{:S(2)}) collective-permute-start(f32[128,1,2048]{2,1,0:T(1,128)} %get-tuple-element.66), channel_id=1, source_target_pairs={{4,2},{6,8},{8,6},{10,12},{5,3},{7,9},{9,7},{11,13},{20,18},{22,24... | collective-permute-start | bytes 3145736 | tf_op jit(solution)/shard_map/ppermute | solution.py:104
  4.5 40.4 %collective-permute-start.2 = (f32[128,1,2048]{2,1,0:T(1,128)}, f32[128,1,2048]{2,1,0:T(1,128)}, u32[]{:S(2)}, u32[]{:S(2)}) collective-permute-start(f32[128,1,2048]{2,1,0:T(1,128)} %get-tuple-element.68), channel_id=1, source_target_pairs={{2,0},{6,4},{8,10},{12,14},{3,1},{7,5},{9,11},{13,15},{18,16},{22,... | collective-permute-start | bytes 3145736 | tf_op jit(solution)/shard_map/ppermute | solution.py:104
  8.7 14.3 %collective-permute-start.1 = (f32[128,1,1024]{2,1,0:T(1,128)}, f32[128,1,1024]{2,1,0:T(1,128)S(1)}, u32[]{:S(2)}, u32[]{:S(2)}) collective-permute-start(f32[128,1,1024]{2,1,0:T(1,128)} %get-tuple-element.67), channel_id=1, source_target_pairs={{2,4},{4,2},{10,12},{12,10},{3,5},{5,3},{11,13},{13,11},{18,20},{2... | collective-permute-start | bytes 1572872 | tf_op jit(solution)/shard_map/ppermute | solution.py:104
  9.4 35.4 %collective-permute-start.3 = (f32[128,1,1024]{2,1,0:T(1,128)}, f32[128,1,1024]{2,1,0:T(1,128)}, u32[]{:S(2)}, u32[]{:S(2)}) collective-permute-start(f32[128,1,1024]{2,1,0:T(1,128)} %get-tuple-element.69), channel_id=1, source_target_pairs={{2,0},{4,6},{10,8},{12,14},{3,1},{5,7},{11,9},{13,15},{18,16},{20,... | collective-permute-start | bytes 1572872 | tf_op jit(solution)/shard_map/ppermute | solution.py:104
  13.7 77.9 %collective-permute-start.6 = (f32[128,1,3072]{2,1,0:T(1,128)}, f32[128,1,3072]{2,1,0:T(1,128)S(1)}, u32[]{:S(2)}, u32[]{:S(2)}) collective-permute-start(f32[128,1,3072]{2,1,0:T(1,128)} %get-tuple-element.80), channel_id=1, source_target_pairs={{0,2},{4,6},{8,10},{12,14},{2,0},{6,4},{10,8},{14,12},{1,3},{5,7},... | collective-permute-start | bytes 4718600 | tf_op jit(solution)/shard_map/ppermute | solution.py:645
  44.8 38.0 %collective-permute-start.4 = (f32[128,1,2048]{2,1,0:T(1,128)}, f32[128,1,2048]{2,1,0:T(1,128)}, u32[]{:S(2)}, u32[]{:S(2)}) collective-permute-start(f32[128,1,2048]{2,1,0:T(1,128)} %collective-permute-done.2), channel_id=1, source_target_pairs={{0,4},{4,8},{10,6},{14,10},{1,5},{5,9},{11,7},{15,11},{16,20},{20,... | collective-permute-start | bytes 3145736 | tf_op jit(solution)/shard_map/ppermute | solution.py:104
  52.6 30.3 %collective-permute-start.5 = (f32[128,1,1024]{2,1,0:T(1,128)}, f32[128,1,1024]{2,1,0:T(1,128)}, u32[]{:S(2)}, u32[]{:S(2)}) collective-permute-start(f32[128,1,1024]{2,1,0:T(1,128)} %collective-permute-done.3), channel_id=1, source_target_pairs={{0,4},{6,2},{8,12},{14,10},{1,5},{7,3},{9,13},{15,11},{16,20},{22,... | collective-permute-start | bytes 1572872 | tf_op jit(solution)/shard_map/ppermute | solution.py:104
  55.0 36.6 %collective-permute-start.7 = (f32[128,1,1024]{2,1,0:T(1,128)}, f32[128,1,1024]{2,1,0:T(1,128)}, u32[]{:S(2)}, u32[]{:S(2)}) collective-permute-start(f32[128,1,1024]{2,1,0:T(1,128)} %get-tuple-element.81), channel_id=1, source_target_pairs={{0,2},{4,6},{8,10},{12,14},{2,0},{6,4},{10,8},{14,12},{1,3},{5,7},... | collective-permute-start | bytes 1572872 | tf_op jit(solution)/shard_map/ppermute | solution.py:645
  91.6 39.3 %collective-permute-start.14 = (f32[128,4096]{1,0:T(8,128)}, f32[128,4096]{1,0:T(8,128)S(1)}, u32[]{:S(2)}, u32[]{:S(2)}) collective-permute-start(f32[128,4096]{1,0:T(8,128)} %ratio_cross.1.refs_2_.refs_1_), channel_id=1, source_target_pairs={{2,4},{6,8},{10,12},{4,2},{8,6},{12,10},{3,5},{7,9},{11,13},{5,3},... | collective-permute-start | bytes 6291464 | tf_op jit(solution)/shard_map/ppermute | solution.py:675
  114.3 2.9 %collective-permute-start.10 = (f32[256,1024]{1,0:T(8,128)}, f32[256,1024]{1,0:T(8,128)S(1)}, u32[]{:S(2)}, u32[]{:S(2)}) collective-permute-start(f32[256,1024]{1,0:T(8,128)} %get-tuple-element.89.refs_0_), channel_id=1, source_target_pairs={{0,1},{1,0},{2,3},{3,2},{4,5},{5,4},{6,7},{7,6},{8,9},{9,8},{10,11... | collective-permute-start | bytes 3145736 | tf_op jit(solution)/shard_map/ppermute | solution.py:688
  114.3 7.8 %collective-permute-start.11 = (f32[256,1024]{1,0:T(8,128)}, f32[256,1024]{1,0:T(8,128)S(1)}, u32[]{:S(2)}, u32[]{:S(2)}) collective-permute-start(f32[256,1024]{1,0:T(8,128)} %get-tuple-element.90.refs_1_), channel_id=1, source_target_pairs={{0,1},{1,0},{2,3},{3,2},{4,5},{5,4},{6,7},{7,6},{8,9},{9,8},{10,11... | collective-permute-start | bytes 3145736 | tf_op jit(solution)/shard_map/ppermute | solution.py:688
  114.8 7.3 %collective-permute-start.12 = (f32[256,1024]{1,0:T(8,128)}, f32[256,1024]{1,0:T(8,128)S(1)}, u32[]{:S(2)}, u32[]{:S(2)}) collective-permute-start(f32[256,1024]{1,0:T(8,128)} %get-tuple-element.91.refs_2_), channel_id=1, source_target_pairs={{0,1},{1,0},{2,3},{3,2},{4,5},{5,4},{6,7},{7,6},{8,9},{9,8},{10,11... | collective-permute-start | bytes 3145736 | tf_op jit(solution)/shard_map/ppermute | solution.py:688
  114.9 7.2 %collective-permute-start.13 = (f32[256,1024]{1,0:T(8,128)}, f32[256,1024]{1,0:T(8,128)S(1)}, u32[]{:S(2)}, u32[]{:S(2)}) collective-permute-start(f32[256,1024]{1,0:T(8,128)} %get-tuple-element.92.refs_3_), channel_id=1, source_target_pairs={{0,1},{1,0},{2,3},{3,2},{4,5},{5,4},{6,7},{7,6},{8,9},{9,8},{10,11... | collective-permute-start | bytes 3145736 | tf_op jit(solution)/shard_map/ppermute | solution.py:688
  117.2 47.1 %collective-permute-start.8 = (f32[128,2304]{1,0:T(8,128)S(1)}, f32[128,2304]{1,0:T(8,128)S(1)}, u32[]{:S(2)}, u32[]{:S(2)}) collective-permute-start(f32[128,2304]{1,0:T(8,128)S(1)} %copy-done.3), channel_id=1, source_target_pairs={{0,2},{4,6},{8,10},{12,14},{2,0},{6,4},{10,8},{14,12},{1,3},{5,7},... | collective-permute-start | bytes 3538952 | tf_op jit(solution)/shard_map/ppermute | solution.py:683
  140.0 12.5 %collective-permute-start.16 = (f32[128,1024]{1,0:T(8,128)}, f32[128,1024]{1,0:T(8,128)S(1)}, u32[]{:S(2)}, u32[]{:S(2)}) collective-permute-start(f32[128,1024]{1,0:T(8,128)} %get-tuple-element.99.refs_1_), channel_id=1, source_target_pairs={{0,1},{1,0},{2,3},{3,2},{4,5},{5,4},{6,7},{7,6},{8,9},{9,8},{10,11... | collective-permute-start | bytes 1572872 | tf_op jit(solution)/shard_map/ppermute | solution.py:688
  140.5 12.0 %collective-permute-start.17 = (f32[128,1024]{1,0:T(8,128)}, f32[128,1024]{1,0:T(8,128)S(1)}, u32[]{:S(2)}, u32[]{:S(2)}) collective-permute-start(f32[128,1024]{1,0:T(8,128)} %get-tuple-element.100.refs_2_), channel_id=1, source_target_pairs={{0,1},{1,0},{2,3},{3,2},{4,5},{5,4},{6,7},{7,6},{8,9},{9,8},{10,11... | collective-permute-start | bytes 1572872 | tf_op jit(solution)/shard_map/ppermute | solution.py:688
  140.5 12.0 %collective-permute-start.18 = (f32[128,1024]{1,0:T(8,128)}, f32[128,1024]{1,0:T(8,128)S(1)}, u32[]{:S(2)}, u32[]{:S(2)}) collective-permute-start(f32[128,1024]{1,0:T(8,128)} %get-tuple-element.101.refs_3_), channel_id=1, source_target_pairs={{0,1},{1,0},{2,3},{3,2},{4,5},{5,4},{6,7},{7,6},{8,9},{9,8},{10,11... | collective-permute-start | bytes 1572872 | tf_op jit(solution)/shard_map/ppermute | solution.py:688
  142.1 41.8 %collective-permute-start.9 = (f32[128,1792]{1,0:T(8,128)S(1)}, f32[128,1792]{1,0:T(8,128)S(1)}, u32[]{:S(2)}, u32[]{:S(2)}) collective-permute-start(f32[128,1792]{1,0:T(8,128)S(1)} %copy-done.4), channel_id=1, source_target_pairs={{0,2},{4,6},{8,10},{12,14},{2,0},{6,4},{10,8},{14,12},{1,3},{5,7},... | collective-permute-start | bytes 2752520 | tf_op jit(solution)/shard_map/ppermute | solution.py:683
  170.5 4.5 %collective-permute-start.19 = (f32[128,1024]{1,0:T(8,128)S(1)}, f32[128,1024]{1,0:T(8,128)S(1)}, u32[]{:S(2)}, u32[]{:S(2)}) collective-permute-start(f32[128,1024]{1,0:T(8,128)S(1)} %get-tuple-element.110.refs_0_), channel_id=1, source_target_pairs={{0,1},{1,0},{2,3},{3,2},{4,5},{5,4},{6,7},{7,6},{8,9},{9,8},{10,11... | collective-permute-start | bytes 1572872 | tf_op jit(solution)/shard_map/ppermute | solution.py:732
  170.6 4.4 %collective-permute-start.20 = (f32[128,1024]{1,0:T(8,128)S(1)}, f32[128,1024]{1,0:T(8,128)S(1)}, u32[]{:S(2)}, u32[]{:S(2)}) collective-permute-start(f32[128,1024]{1,0:T(8,128)S(1)} %get-tuple-element.111.refs_1_), channel_id=1, source_target_pairs={{0,1},{1,0},{2,3},{3,2},{4,5},{5,4},{6,7},{7,6},{8,9},{9,8},{10,11... | collective-permute-start | bytes 1572872 | tf_op jit(solution)/shard_map/ppermute | solution.py:732
  189.5 2.7 %collective-permute-start.21 = (f32[128,2048]{1,0:T(8,128)S(1)}, f32[128,2048]{1,0:T(8,128)S(1)}, u32[]{:S(2)}, u32[]{:S(2)}) collective-permute-start(f32[128,2048]{1,0:T(8,128)S(1)} %get-tuple-element.119.refs_0_), channel_id=1, source_target_pairs={{0,1},{1,0},{2,3},{3,2},{4,5},{5,4},{6,7},{7,6},{8,9},{9,8},{10,11... | collective-permute-start | bytes 3145736 | tf_op jit(solution)/shard_map/ppermute | solution.py:732
  193.6 5.2 %collective-permute-start.22 = (f32[1,128]{1,0:T(1,128)S(1)}, f32[1,128]{1,0:T(1,128)S(1)}, u32[]{:S(2)}, u32[]{:S(2)}) collective-permute-start(f32[1,128]{1,0:T(1,128)S(1)} %get-tuple-element.123.a_ref), channel_id=1, source_target_pairs={{0,2},{2,0},{4,6},{6,4},{8,10},{10,8},{12,14},{14,12},{1,3},{3,1},... | collective-permute-start | bytes 1544 | tf_op jit(solution)/shard_map/ppermute | solution.py:578
  198.8 3.6 %collective-permute-start.23 = (f32[1,128]{1,0:T(1,128)S(1)}, f32[1,128]{1,0:T(1,128)S(1)}, u32[]{:S(2)}, u32[]{:S(2)}) collective-permute-start(f32[1,128]{1,0:T(1,128)S(1)} %mass.2.a_ref), channel_id=1, source_target_pairs={{0,4},{2,6},{4,0},{6,2},{8,12},{10,14},{12,8},{14,10},{1,5},{3,7},... | collective-permute-start | bytes 1544 | tf_op jit(solution)/shard_map/ppermute | solution.py:578
  202.4 5.1 %collective-permute-start.24 = (f32[1,128]{1,0:T(1,128)S(1)}, f32[1,128]{1,0:T(1,128)S(1)}, u32[]{:S(2)}, u32[]{:S(2)}) collective-permute-start(f32[1,128]{1,0:T(1,128)S(1)} %mass.3.refs_0_), channel_id=1, source_target_pairs={{0,8},{2,10},{4,12},{6,14},{8,0},{10,2},{12,4},{14,6},{1,9},{3,11}... | collective-permute-start | bytes 1544 | tf_op jit(solution)/shard_map/ppermute | solution.py:578
  (6 other events, 120.3 us)

commit v5 on v4

--- a/solution.py
+++ b/solution.py
@@ -594,7 +594,7 @@
 
 def outputs(raw, quotient, masses):
     rows, columns = raw.shape
-    tile = 64
+    tile = 32
     flat = pl.BlockSpec((tile, columns), lambda i: (i, 0))
     deep = pl.BlockSpec((tile,) + quotient.shape[1:], lambda i: (i, 0, 0))
     return pl.pallas_call(

time: 215 us -> 217 us (level)
  no operation moved by 1% of the time
where the time goes in v5:
time: 217 us; the launch traced here: 216 us
  Pallas kernels  117 us (54%)
  starting transfers between devices  50.5 us (23%)
  waiting for transfers between devices  45.3 us (21%)
  local copies, waits for them, and re-layouts  2.26 us (1%)
    pallas_call x7, Pallas kernels, blur(): pl.pallas_call(functools.partial(blur_kernel, plan), in_specs=[INSMEM] +...  62.3 us
    ppermute x6, waiting for transfers between devices, send(): return lax.ppermute(part, 'space', pairs)  24.5 us
    ppermute x2, starting transfers between devices, local(): near2 = [near(part) for part in parts]  15.3 us
    ppermute x6, starting transfers between devices, send(): return lax.ppermute(part, 'space', pairs)  14.2 us
    pallas_call x2, Pallas kernels, raw_rows(): pl.pallas_call(functools.partial(raw_kernel, fresh, row), grid_spec=pltpu...  13.8 us
    ppermute x2, waiting for transfers between devices, local(): near2 = [near(part) for part in parts]  11.9 us
    pallas_call x1, Pallas kernels, row_weights(): pl.pallas_call(functools.partial(weight_kernel, nblocks), grid=(nblocks /...  11.6 us
    ppermute x2, starting transfers between devices, local(): near(part)  9.22 us
  transfers between devices with their start and end apart: 25, of which 9 were waited for; matrix products, arithmetic and copies ran while one was open for 1% of the time, Pallas kernels for 46%

profile of v5, /device:TPU:0, one launch (start us, length us, event | category | flops | bytes accessed | tf_op | source)
XLA Modules:
  0.0 216.0 jit_solution(8818721677572814281)
XLA Ops:
  0.7 3.0 %cut_cross_halves.1 = (f32[128,1,2048]{2,1,0:T(1,128)}, f32[128,1,2048]{2,1,0:T(1,128)}) custom-call(s32[4]{0:T(128)S(1)} %pad_add_fusion.side_ref.refs_0_, f32[512,1,4096]{2,1,0:T(1,128)} %refs_8_.5), custom_call_target="tpu_custom_call" | custom-call | tf_op jit(solution)/shard_map/cut_cross_halves/pallas_call | solution.py:72
  5.8 2.9 %cut_cross_quarters.1 = (f32[128,1,1024]{2,1,0:T(1,128)}, f32[128,1,1024]{2,1,0:T(1,128)}) custom-call(s32[4]{0:T(128)S(1)} %pad_add_fusion.side_ref.refs_0_, f32[512,1,4096]{2,1,0:T(1,128)} %refs_8_.5), custom_call_target="tpu_custom_call" | custom-call | tf_op jit(solution)/shard_map/cut_cross_quarters/pallas_call | solution.py:72
  10.7 3.1 %cut_near.1 = (f32[128,1,3072]{2,1,0:T(1,128)}, f32[128,1,1024]{2,1,0:T(1,128)}) custom-call(s32[4]{0:T(128)S(1)} %pad_add_fusion.side_ref.refs_0_, f32[512,1,4096]{2,1,0:T(1,128)} %refs_8_.5), custom_call_target="tpu_custom_call" | custom-call | tf_op jit(solution)/shard_map/cut_near/pallas_call | solution.py:72
  13.7 9.2 %collective-permute-start.6 = (f32[128,1,3072]{2,1,0:T(1,128)}, f32[128,1,3072]{2,1,0:T(1,128)S(1)}, u32[]{:S(2)}, u32[]{:S(2)}) collective-permute-start(f32[128,1,3072]{2,1,0:T(1,128)} %get-tuple-element.80), channel_id=1, source_target_pairs={{0,2},{4,6},{8,10},{12,14},{2,0},{6,4},{10,8},{14,12},{1,3},{5,7},... | collective-permute-start | bytes 4718600 | tf_op jit(solution)/shard_map/ppermute | solution.py:645
  22.9 21.9 %collective-permute-done.3 = f32[128,1,1024]{2,1,0:T(1,128)} collective-permute-done((f32[128,1,1024]{2,1,0:T(1,128)}, f32[128,1,1024]{2,1,0:T(1,128)}, u32[]{:S(2)}, u32[]{:S(2)}) %collective-permute-start.3) | collective-permute-done | bytes 524320 | tf_op jit(solution)/shard_map/ppermute | solution.py:104
  44.8 7.8 %collective-permute-start.4 = (f32[128,1,2048]{2,1,0:T(1,128)}, f32[128,1,2048]{2,1,0:T(1,128)}, u32[]{:S(2)}, u32[]{:S(2)}) collective-permute-start(f32[128,1,2048]{2,1,0:T(1,128)} %collective-permute-done.2), channel_id=1, source_target_pairs={{0,4},{4,8},{10,6},{14,10},{1,5},{5,9},{11,7},{15,11},{16,20},{20,... | collective-permute-start | bytes 3145736 | tf_op jit(solution)/shard_map/ppermute | solution.py:104
  55.0 11.6 %row_weights.1 = (bf16[16,256,512]{2,1,0:T(8,128)(2,1)}, bf16[16,256,512]{2,1,0:T(8,128)(2,1)}) custom-call(f32[32,3,128,128]{3,2,1,0:T(8,128)} %band_ref.1), custom_call_target="tpu_custom_call" | custom-call | tf_op jit(solution)/shard_map/row_weights/pallas_call | solution.py:149
  67.7 11.4 %ratio_inner.1.beside_ref.refs_1_.refs_2_ = f32[256,4096]{1,0:T(8,128)} custom-call(s32[4]{0:T(128)S(1)} %pad_add_fusion.side_ref.refs_0_, f32[512,1,4096]{2,1,0:T(1,128)} %refs_8_.5, f32[2,3,128,128]{3,2,1,0:T(8,128)S(1)} %constant_dynamic-slice_fusion.2.refs_2_.refs_4_, bf16[16,256,512]{2,1,0:T(8,128)(2,1)} %get-tuple-element.74.refs_3_.refs_7_.refs_5_.refs_6_, ...), custom_call_target="tpu_custom_call" | custom-call | flops 100663296 | bytes 458752 | tf_op jit(solution)/shard_map/ratio_inner/pallas_call | solution.py:334
  80.2 2.7 %collective-permute-done.5.refs_3_ = f32[128,1,1024]{2,1,0:T(1,128)} collective-permute-done((f32[128,1,1024]{2,1,0:T(1,128)}, f32[128,1,1024]{2,1,0:T(1,128)}, u32[]{:S(2)}, u32[]{:S(2)}) %collective-permute-start.5) | collective-permute-done | bytes 524320 | tf_op jit(solution)/shard_map/ppermute | solution.py:104
  82.9 8.7 %ratio_cross.1.refs_2_.refs_1_ = f32[128,4096]{1,0:T(8,128)} custom-call(s32[4]{0:T(128)S(1)} %pad_add_fusion.side_ref.refs_0_, f32[512,1,4096]{2,1,0:T(1,128)} %refs_8_.5, f32[128,1,2048]{2,1,0:T(1,128)} %collective-permute-done.4.refs_2_, f32[128,1,1024]{2,1,0:T(1,128)} %collective-permute-done.5.refs_3_, f32[128,1,2048]{2,1,0:T(1,128)} %copy-done.1, ...), custom_call_target="tpu_custom_call" | custom-call | flops 44040192 | bytes 327680 | tf_op jit(solution)/shard_map/ratio_cross/pallas_call | solution.py:334
  92.8 9.0 %ratio_near.1 = (f32[128,2304]{1,0:T(8,128)}, f32[128,1792]{1,0:T(8,128)}, f32[128,4096]{1,0:T(8,128)}) custom-call(s32[4]{0:T(128)S(1)} %pad_add_fusion.side_ref.refs_0_, f32[512,1,4096]{2,1,0:T(1,128)} %refs_8_.5, f32[128,1,3072]{2,1,0:T(1,128)} %copy-done, f32[128,1,1024]{2,1,0:T(1,128)} %collective-permute-done.7.refs_3_, ...), custom_call_target="tpu_custom_call" | custom-call | flops 44040192 | bytes 327680 | tf_op jit(solution)/shard_map/ratio_near/pallas_call | solution.py:334
  101.9 12.4 %logs_inner.1 = (f32[256,1024]{1,0:T(8,128)}, f32[256,1024]{1,0:T(8,128)}, f32[256,1024]{1,0:T(8,128)}, f32[256,1024]{1,0:T(8,128)}, f32[256,4096]{1,0:T(8,128)}) custom-call(s32[4]{0:T(128)S(1)} %pad_add_fusion.side_ref.refs_0_, f32[256,4096]{1,0:T(8,128)} %ratio_inner.1.beside_ref.refs_1_.refs_2_, f32[128,4096]{1,0:T(8,128)} %ratio_cross.1.refs_2_.refs_1_, ...), custom_call_target="tpu_custom_call" | custom-call | flops 100663296 | bytes 458752 | tf_op jit(solution)/shard_map/logs_inner/pallas_call | solution.py:334
  117.2 4.9 %collective-permute-start.8 = (f32[128,2304]{1,0:T(8,128)S(1)}, f32[128,2304]{1,0:T(8,128)S(1)}, u32[]{:S(2)}, u32[]{:S(2)}) collective-permute-start(f32[128,2304]{1,0:T(8,128)S(1)} %copy-done.3), channel_id=1, source_target_pairs={{0,2},{4,6},{8,10},{12,14},{2,0},{6,4},{10,8},{14,12},{1,3},{5,7},... | collective-permute-start | bytes 3538952 | tf_op jit(solution)/shard_map/ppermute | solution.py:683
  122.1 8.8 %raw_inner.1 = (f32[512,4096]{1,0:T(8,128)S(1)}, f32[512,1,4096]{2,1,0:T(1,128)S(1)}, f32[1,128]{1,0:T(1,128)S(1)}) custom-call(s32[4]{0:T(128)S(1)} %pad_add_fusion.side_ref.refs_0_, f32[256,1024]{1,0:T(8,128)} %get-tuple-element.89.refs_0_, f32[256,1024]{1,0:T(8,128)} %get-tuple-element.90.refs_1_, f32[256,1024]{1,0:T(8,128)} %get-tuple-element.91.refs_2_, ...), custom_call_target="tpu_custom_call" | custom-call | flops 65536 | bytes 262144 | tf_op jit(solution)/shard_map/raw_inner/pallas_call | solution.py:445
  131.0 8.9 %logs_cross.1 = (f32[128,1024]{1,0:T(8,128)}, f32[128,1024]{1,0:T(8,128)}, f32[128,1024]{1,0:T(8,128)}, f32[128,1024]{1,0:T(8,128)}, f32[128,4096]{1,0:T(8,128)}) custom-call(s32[4]{0:T(128)S(1)} %pad_add_fusion.side_ref.refs_0_, f32[128,4096]{1,0:T(8,128)} %ratio_cross.1.refs_2_.refs_1_, f32[256,4096]{1,0:T(8,128)} %ratio_inner.1.beside_ref.refs_1_.refs_2_, ...), custom_call_target="tpu_custom_call" | custom-call | flops 44040192 | bytes 327680 | tf_op jit(solution)/shard_map/logs_cross/pallas_call | solution.py:334
  142.1 10.4 %collective-permute-start.9 = (f32[128,1792]{1,0:T(8,128)S(1)}, f32[128,1792]{1,0:T(8,128)S(1)}, u32[]{:S(2)}, u32[]{:S(2)}) collective-permute-start(f32[128,1792]{1,0:T(8,128)S(1)} %copy-done.4), channel_id=1, source_target_pairs={{0,2},{4,6},{8,10},{12,14},{2,0},{6,4},{10,8},{14,12},{1,3},{5,7},... | collective-permute-start | bytes 2752520 | tf_op jit(solution)/shard_map/ppermute | solution.py:683
  152.5 4.9 %raw_cross.1 = (f32[512,4096]{1,0:T(8,128)S(1)}, f32[512,1,4096]{2,1,0:T(1,128)S(1)}, f32[1,128]{1,0:T(1,128)S(1)}) custom-call(s32[4]{0:T(128)S(1)} %pad_add_fusion.side_ref.refs_0_, f32[128,1024]{1,0:T(8,128)} %get-tuple-element.98.refs_0_, f32[128,1024]{1,0:T(8,128)} %get-tuple-element.99.refs_1_, ...), custom_call_target="tpu_custom_call", output_to_operand_aliasing={{0}: (10, {}), {1}: (11, {})} | custom-call | flops 32768 | bytes 131072 | tf_op jit(solution)/shard_map/raw_cross/pallas_call | solution.py:445
  157.5 6.8 %collective-permute-done.8.refs_3_ = f32[128,2304]{1,0:T(8,128)S(1)} collective-permute-done((f32[128,2304]{1,0:T(8,128)S(1)}, f32[128,2304]{1,0:T(8,128)S(1)}, u32[]{:S(2)}, u32[]{:S(2)}) %collective-permute-start.8) | collective-permute-done | bytes 1179680 | tf_op jit(solution)/shard_map/ppermute | solution.py:683
  164.3 6.2 %logs_near_first.1 = (f32[128,1024]{1,0:T(8,128)S(1)}, f32[128,1024]{1,0:T(8,128)S(1)}, f32[128,2048]{1,0:T(8,128)}) custom-call(s32[4]{0:T(128)S(1)} %pad_add_fusion.side_ref.refs_0_, f32[128,4096]{1,0:T(8,128)} %get-tuple-element.84.own_ref.refs_3_.refs_1_, f32[256,4096]{1,0:T(8,128)} %ratio_inner.1.beside_ref.refs_1_.refs_2_, ...), custom_call_target="tpu_custom_call" | custom-call | flops 44040192 | bytes 327680 | tf_op jit(solution)/shard_map/logs_near_first/pallas_call | solution.py:334
  171.0 3.9 %begin_near.1.refs_9_ = f32[128,2304]{1,0:T(8,128)} custom-call(s32[4]{0:T(128)S(1)} %pad_add_fusion.side_ref.refs_0_, f32[128,4096]{1,0:T(8,128)} %get-tuple-element.84.own_ref.refs_3_.refs_1_, f32[256,4096]{1,0:T(8,128)} %ratio_inner.1.beside_ref.refs_1_.refs_2_, f32[1,3,128,128]{3,2,1,0:T(8,128)S(1)} %get-tuple-element.132.refs_4_.band_ref.refs_5_), custom_call_target="tpu_custom_call" | custom-call | flops 294912 | bytes 294912 | tf_op jit(solution)/shard_map/begin_near/pallas_call | solution.py:389
  178.8 5.1 %collective-permute-done.9.refs_4_ = f32[128,1792]{1,0:T(8,128)S(1)} collective-permute-done((f32[128,1792]{1,0:T(8,128)S(1)}, f32[128,1792]{1,0:T(8,128)S(1)}, u32[]{:S(2)}, u32[]{:S(2)}) %collective-permute-start.9) | collective-permute-done | bytes 917536 | tf_op jit(solution)/shard_map/ppermute | solution.py:683
  183.9 5.6 %logs_near_later.1 = (f32[128,2048]{1,0:T(8,128)S(1)}, f32[128,2048]{1,0:T(8,128)}) custom-call(s32[4]{0:T(128)S(1)} %pad_add_fusion.side_ref.refs_0_, f32[128,4096]{1,0:T(8,128)} %get-tuple-element.84.own_ref.refs_3_.refs_1_, f32[256,4096]{1,0:T(8,128)} %ratio_inner.1.beside_ref.refs_1_.refs_2_, f32[128,2304]{1,0:T(8,128)S(1)} %collective-permute-done.8.refs_3_, ...), custom_call_target="tpu_custom_call" | custom-call | flops 31457280 | bytes 262144 | tf_op jit(solution)/shard_map/logs_near_later/pallas_call | solution.py:334
  202.4 3.5 %collective-permute-start.24 = (f32[1,128]{1,0:T(1,128)S(1)}, f32[1,128]{1,0:T(1,128)S(1)}, u32[]{:S(2)}, u32[]{:S(2)}) collective-permute-start(f32[1,128]{1,0:T(1,128)S(1)} %mass.3.refs_0_), channel_id=1, source_target_pairs={{0,8},{2,10},{4,12},{6,14},{8,0},{10,2},{12,4},{14,6},{1,9},{3,11}... | collective-permute-start | bytes 1544 | tf_op jit(solution)/shard_map/ppermute | solution.py:578
  207.5 8.6 %outputs.1 = (f32[512,4096]{1,0:T(8,128)}, f32[512,32,128]{2,1,0:T(8,128)}) custom-call(f32[512,4096]{1,0:T(8,128)S(1)} %get-tuple-element.122.raw_ref, f32[512,32,128]{2,1,0:T(8,128)S(1)} %bitcast.6, f32[1,128]{1,0:T(1,128)S(1)} %mass.3.refs_0_, f32[1,128]{1,0:T(1,128)S(1)} %collective-permute-done.24.refs_1_), custom_call_target="tpu_custom_call" | custom-call | tf_op jit(solution)/shard_map/outputs/pallas_call | solution.py:600
  (60 shorter events, 33.6 us)
Async XLA Ops:
  3.7 41.1 %collective-permute-start = (f32[128,1,2048]{2,1,0:T(1,128)}, f32[128,1,2048]{2,1,0:T(1,128)S(1)}, u32[]{:S(2)}, u32[]{:S(2)}) collective-permute-start(f32[128,1,2048]{2,1,0:T(1,128)} %get-tuple-element.66), channel_id=1, source_target_pairs={{4,2},{6,8},{8,6},{10,12},{5,3},{7,9},{9,7},{11,13},{20,18},{22,24... | collective-permute-start | bytes 3145736 | tf_op jit(solution)/shard_map/ppermute | solution.py:104
  4.5 40.4 %collective-permute-start.2 = (f32[128,1,2048]{2,1,0:T(1,128)}, f32[128,1,2048]{2,1,0:T(1,128)}, u32[]{:S(2)}, u32[]{:S(2)}) collective-permute-start(f32[128,1,2048]{2,1,0:T(1,128)} %get-tuple-element.68), channel_id=1, source_target_pairs={{2,0},{6,4},{8,10},{12,14},{3,1},{7,5},{9,11},{13,15},{18,16},{22,... | collective-permute-start | bytes 3145736 | tf_op jit(solution)/shard_map/ppermute | solution.py:104
  8.7 14.3 %collective-permute-start.1 = (f32[128,1,1024]{2,1,0:T(1,128)}, f32[128,1,1024]{2,1,0:T(1,128)S(1)}, u32[]{:S(2)}, u32[]{:S(2)}) collective-permute-start(f32[128,1,1024]{2,1,0:T(1,128)} %get-tuple-element.67), channel_id=1, source_target_pairs={{2,4},{4,2},{10,12},{12,10},{3,5},{5,3},{11,13},{13,11},{18,20},{2... | collective-permute-start | bytes 1572872 | tf_op jit(solution)/shard_map/ppermute | solution.py:104
  9.4 35.4 %collective-permute-start.3 = (f32[128,1,1024]{2,1,0:T(1,128)}, f32[128,1,1024]{2,1,0:T(1,128)}, u32[]{:S(2)}, u32[]{:S(2)}) collective-permute-start(f32[128,1,1024]{2,1,0:T(1,128)} %get-tuple-element.69), channel_id=1, source_target_pairs={{2,0},{4,6},{10,8},{12,14},{3,1},{5,7},{11,9},{13,15},{18,16},{20,... | collective-permute-start | bytes 1572872 | tf_op jit(solution)/shard_map/ppermute | solution.py:104
  13.7 77.9 %collective-permute-start.6 = (f32[128,1,3072]{2,1,0:T(1,128)}, f32[128,1,3072]{2,1,0:T(1,128)S(1)}, u32[]{:S(2)}, u32[]{:S(2)}) collective-permute-start(f32[128,1,3072]{2,1,0:T(1,128)} %get-tuple-element.80), channel_id=1, source_target_pairs={{0,2},{4,6},{8,10},{12,14},{2,0},{6,4},{10,8},{14,12},{1,3},{5,7},... | collective-permute-start | bytes 4718600 | tf_op jit(solution)/shard_map/ppermute | solution.py:645
  44.8 38.0 %collective-permute-start.4 = (f32[128,1,2048]{2,1,0:T(1,128)}, f32[128,1,2048]{2,1,0:T(1,128)}, u32[]{:S(2)}, u32[]{:S(2)}) collective-permute-start(f32[128,1,2048]{2,1,0:T(1,128)} %collective-permute-done.2), channel_id=1, source_target_pairs={{0,4},{4,8},{10,6},{14,10},{1,5},{5,9},{11,7},{15,11},{16,20},{20,... | collective-permute-start | bytes 3145736 | tf_op jit(solution)/shard_map/ppermute | solution.py:104
  52.6 30.3 %collective-permute-start.5 = (f32[128,1,1024]{2,1,0:T(1,128)}, f32[128,1,1024]{2,1,0:T(1,128)}, u32[]{:S(2)}, u32[]{:S(2)}) collective-permute-start(f32[128,1,1024]{2,1,0:T(1,128)} %collective-permute-done.3), channel_id=1, source_target_pairs={{0,4},{6,2},{8,12},{14,10},{1,5},{7,3},{9,13},{15,11},{16,20},{22,... | collective-permute-start | bytes 1572872 | tf_op jit(solution)/shard_map/ppermute | solution.py:104
  55.0 36.6 %collective-permute-start.7 = (f32[128,1,1024]{2,1,0:T(1,128)}, f32[128,1,1024]{2,1,0:T(1,128)}, u32[]{:S(2)}, u32[]{:S(2)}) collective-permute-start(f32[128,1,1024]{2,1,0:T(1,128)} %get-tuple-element.81), channel_id=1, source_target_pairs={{0,2},{4,6},{8,10},{12,14},{2,0},{6,4},{10,8},{14,12},{1,3},{5,7},... | collective-permute-start | bytes 1572872 | tf_op jit(solution)/shard_map/ppermute | solution.py:645
  91.6 39.3 %collective-permute-start.14 = (f32[128,4096]{1,0:T(8,128)}, f32[128,4096]{1,0:T(8,128)S(1)}, u32[]{:S(2)}, u32[]{:S(2)}) collective-permute-start(f32[128,4096]{1,0:T(8,128)} %ratio_cross.1.refs_2_.refs_1_), channel_id=1, source_target_pairs={{2,4},{6,8},{10,12},{4,2},{8,6},{12,10},{3,5},{7,9},{11,13},{5,3},... | collective-permute-start | bytes 6291464 | tf_op jit(solution)/shard_map/ppermute | solution.py:675
  114.3 2.9 %collective-permute-start.10 = (f32[256,1024]{1,0:T(8,128)}, f32[256,1024]{1,0:T(8,128)S(1)}, u32[]{:S(2)}, u32[]{:S(2)}) collective-permute-start(f32[256,1024]{1,0:T(8,128)} %get-tuple-element.89.refs_0_), channel_id=1, source_target_pairs={{0,1},{1,0},{2,3},{3,2},{4,5},{5,4},{6,7},{7,6},{8,9},{9,8},{10,11... | collective-permute-start | bytes 3145736 | tf_op jit(solution)/shard_map/ppermute | solution.py:688
  114.3 7.8 %collective-permute-start.11 = (f32[256,1024]{1,0:T(8,128)}, f32[256,1024]{1,0:T(8,128)S(1)}, u32[]{:S(2)}, u32[]{:S(2)}) collective-permute-start(f32[256,1024]{1,0:T(8,128)} %get-tuple-element.90.refs_1_), channel_id=1, source_target_pairs={{0,1},{1,0},{2,3},{3,2},{4,5},{5,4},{6,7},{7,6},{8,9},{9,8},{10,11... | collective-permute-start | bytes 3145736 | tf_op jit(solution)/shard_map/ppermute | solution.py:688
  114.8 7.3 %collective-permute-start.12 = (f32[256,1024]{1,0:T(8,128)}, f32[256,1024]{1,0:T(8,128)S(1)}, u32[]{:S(2)}, u32[]{:S(2)}) collective-permute-start(f32[256,1024]{1,0:T(8,128)} %get-tuple-element.91.refs_2_), channel_id=1, source_target_pairs={{0,1},{1,0},{2,3},{3,2},{4,5},{5,4},{6,7},{7,6},{8,9},{9,8},{10,11... | collective-permute-start | bytes 3145736 | tf_op jit(solution)/shard_map/ppermute | solution.py:688
  114.9 7.2 %collective-permute-start.13 = (f32[256,1024]{1,0:T(8,128)}, f32[256,1024]{1,0:T(8,128)S(1)}, u32[]{:S(2)}, u32[]{:S(2)}) collective-permute-start(f32[256,1024]{1,0:T(8,128)} %get-tuple-element.92.refs_3_), channel_id=1, source_target_pairs={{0,1},{1,0},{2,3},{3,2},{4,5},{5,4},{6,7},{7,6},{8,9},{9,8},{10,11... | collective-permute-start | bytes 3145736 | tf_op jit(solution)/shard_map/ppermute | solution.py:688
  117.2 47.1 %collective-permute-start.8 = (f32[128,2304]{1,0:T(8,128)S(1)}, f32[128,2304]{1,0:T(8,128)S(1)}, u32[]{:S(2)}, u32[]{:S(2)}) collective-permute-start(f32[128,2304]{1,0:T(8,128)S(1)} %copy-done.3), channel_id=1, source_target_pairs={{0,2},{4,6},{8,10},{12,14},{2,0},{6,4},{10,8},{14,12},{1,3},{5,7},... | collective-permute-start | bytes 3538952 | tf_op jit(solution)/shard_map/ppermute | solution.py:683
  140.0 12.5 %collective-permute-start.16 = (f32[128,1024]{1,0:T(8,128)}, f32[128,1024]{1,0:T(8,128)S(1)}, u32[]{:S(2)}, u32[]{:S(2)}) collective-permute-start(f32[128,1024]{1,0:T(8,128)} %get-tuple-element.99.refs_1_), channel_id=1, source_target_pairs={{0,1},{1,0},{2,3},{3,2},{4,5},{5,4},{6,7},{7,6},{8,9},{9,8},{10,11... | collective-permute-start | bytes 1572872 | tf_op jit(solution)/shard_map/ppermute | solution.py:688
  140.5 12.0 %collective-permute-start.17 = (f32[128,1024]{1,0:T(8,128)}, f32[128,1024]{1,0:T(8,128)S(1)}, u32[]{:S(2)}, u32[]{:S(2)}) collective-permute-start(f32[128,1024]{1,0:T(8,128)} %get-tuple-element.100.refs_2_), channel_id=1, source_target_pairs={{0,1},{1,0},{2,3},{3,2},{4,5},{5,4},{6,7},{7,6},{8,9},{9,8},{10,11... | collective-permute-start | bytes 1572872 | tf_op jit(solution)/shard_map/ppermute | solution.py:688
  140.5 12.0 %collective-permute-start.18 = (f32[128,1024]{1,0:T(8,128)}, f32[128,1024]{1,0:T(8,128)S(1)}, u32[]{:S(2)}, u32[]{:S(2)}) collective-permute-start(f32[128,1024]{1,0:T(8,128)} %get-tuple-element.101.refs_3_), channel_id=1, source_target_pairs={{0,1},{1,0},{2,3},{3,2},{4,5},{5,4},{6,7},{7,6},{8,9},{9,8},{10,11... | collective-permute-start | bytes 1572872 | tf_op jit(solution)/shard_map/ppermute | solution.py:688
  142.1 41.8 %collective-permute-start.9 = (f32[128,1792]{1,0:T(8,128)S(1)}, f32[128,1792]{1,0:T(8,128)S(1)}, u32[]{:S(2)}, u32[]{:S(2)}) collective-permute-start(f32[128,1792]{1,0:T(8,128)S(1)} %copy-done.4), channel_id=1, source_target_pairs={{0,2},{4,6},{8,10},{12,14},{2,0},{6,4},{10,8},{14,12},{1,3},{5,7},... | collective-permute-start | bytes 2752520 | tf_op jit(solution)/shard_map/ppermute | solution.py:683
  170.5 4.5 %collective-permute-start.19 = (f32[128,1024]{1,0:T(8,128)S(1)}, f32[128,1024]{1,0:T(8,128)S(1)}, u32[]{:S(2)}, u32[]{:S(2)}) collective-permute-start(f32[128,1024]{1,0:T(8,128)S(1)} %get-tuple-element.110.refs_0_), channel_id=1, source_target_pairs={{0,1},{1,0},{2,3},{3,2},{4,5},{5,4},{6,7},{7,6},{8,9},{9,8},{10,11... | collective-permute-start | bytes 1572872 | tf_op jit(solution)/shard_map/ppermute | solution.py:732
  170.6 4.4 %collective-permute-start.20 = (f32[128,1024]{1,0:T(8,128)S(1)}, f32[128,1024]{1,0:T(8,128)S(1)}, u32[]{:S(2)}, u32[]{:S(2)}) collective-permute-start(f32[128,1024]{1,0:T(8,128)S(1)} %get-tuple-element.111.refs_1_), channel_id=1, source_target_pairs={{0,1},{1,0},{2,3},{3,2},{4,5},{5,4},{6,7},{7,6},{8,9},{9,8},{10,11... | collective-permute-start | bytes 1572872 | tf_op jit(solution)/shard_map/ppermute | solution.py:732
  189.5 2.7 %collective-permute-start.21 = (f32[128,2048]{1,0:T(8,128)S(1)}, f32[128,2048]{1,0:T(8,128)S(1)}, u32[]{:S(2)}, u32[]{:S(2)}) collective-permute-start(f32[128,2048]{1,0:T(8,128)S(1)} %get-tuple-element.119.refs_0_), channel_id=1, source_target_pairs={{0,1},{1,0},{2,3},{3,2},{4,5},{5,4},{6,7},{7,6},{8,9},{9,8},{10,11... | collective-permute-start | bytes 3145736 | tf_op jit(solution)/shard_map/ppermute | solution.py:732
  193.6 5.2 %collective-permute-start.22 = (f32[1,128]{1,0:T(1,128)S(1)}, f32[1,128]{1,0:T(1,128)S(1)}, u32[]{:S(2)}, u32[]{:S(2)}) collective-permute-start(f32[1,128]{1,0:T(1,128)S(1)} %get-tuple-element.123.a_ref), channel_id=1, source_target_pairs={{0,2},{2,0},{4,6},{6,4},{8,10},{10,8},{12,14},{14,12},{1,3},{3,1},... | collective-permute-start | bytes 1544 | tf_op jit(solution)/shard_map/ppermute | solution.py:578
  198.8 3.6 %collective-permute-start.23 = (f32[1,128]{1,0:T(1,128)S(1)}, f32[1,128]{1,0:T(1,128)S(1)}, u32[]{:S(2)}, u32[]{:S(2)}) collective-permute-start(f32[1,128]{1,0:T(1,128)S(1)} %mass.2.a_ref), channel_id=1, source_target_pairs={{0,4},{2,6},{4,0},{6,2},{8,12},{10,14},{12,8},{14,10},{1,5},{3,7},... | collective-permute-start | bytes 1544 | tf_op jit(solution)/shard_map/ppermute | solution.py:578
  202.4 5.1 %collective-permute-start.24 = (f32[1,128]{1,0:T(1,128)S(1)}, f32[1,128]{1,0:T(1,128)S(1)}, u32[]{:S(2)}, u32[]{:S(2)}) collective-permute-start(f32[1,128]{1,0:T(1,128)S(1)} %mass.3.refs_0_), channel_id=1, source_target_pairs={{0,8},{2,10},{4,12},{6,14},{8,0},{10,2},{12,4},{14,6},{1,9},{3,11}... | collective-permute-start | bytes 1544 | tf_op jit(solution)/shard_map/ppermute | solution.py:578
  (6 other events, 120.3 us)
